TPU v7x, 32 devices: a whole 2x2x4 slice. The times are simulated.
32 devices in a mesh: obj: 2 (over x), dp: 4 (over y, core), tensor: 4 (over z).
Axes of the slice: x: 2, y: 2, z: 4, core: 2. Of those that a mesh axis runs over, the one named last changes fastest.
Arguments:
- tokens: bfloat16 [2, 8, 1024, 2048], P('obj', 'dp', 'tensor'), may hold values from -6 to 6
- cotangent: bfloat16 [2, 8, 1024, 2048], P('obj', 'dp', 'tensor'), may hold values from -6 to 6
- loss_mask: int32 [2, 8, 1024], P('obj', 'dp', 'tensor'), may hold values 0 or 1
- prefix: int32 [8], P('dp'), may hold values from 1 to 1023
- counts: int32 [2], replicated, may hold values from 256 to 8191
- w_qkv: bfloat16 [2048, 16, 384], P('dp', 'tensor'), may hold values from -0.125 to 0.125
- b_qkv: bfloat16 [16, 384], P('tensor'), may hold values from -1.75 to 1.75
- w_dense: bfloat16 [16, 128, 2048], P('tensor', None, 'dp'), may hold values from -2.5 to 2.5
- b_dense: bfloat16 [2048], replicated, may hold values from -3 to 3
- ln1_gain: bfloat16 [2048], replicated, may hold values from 0.099609375 to 1.8984375
- ln1_bias: bfloat16 [2048], replicated, may hold values from -3 to 3
- w_up: bfloat16 [2, 2048, 5632], P(None, 'dp', 'tensor'), may hold values from -0.125 to 0.125
- b_up: bfloat16 [2, 5632], P(None, 'tensor'), may hold values from -3 to 3
- w_down: bfloat16 [5632, 2048], P('tensor', 'dp'), may hold values from -0.625 to 0.625
- b_down: bfloat16 [2048], replicated, may hold values from -3 to 3
- ln2_gain: bfloat16 [2048], replicated, may hold values from 0.099609375 to 1.8984375
- ln2_bias: bfloat16 [2048], replicated, may hold values from -3 to 3
Outputs:
- layer_out: bfloat16 [2, 8, 1024, 2048], P('obj', 'dp', 'tensor')
- grad_tokens: float32 [2, 8, 1024, 2048], P('obj', 'dp', 'tensor')
- grad_w_qkv: float32 [2048, 16, 384], P('dp', 'tensor')
- grad_b_qkv: float32 [16, 384], P('tensor')
- grad_w_dense: float32 [16, 128, 2048], P('tensor', None, 'dp')
- grad_b_dense: float32 [2048], replicated
- grad_ln1_gain: float32 [2048], replicated
- grad_ln1_bias: float32 [2048], replicated
- grad_w_up: float32 [2, 2048, 5632], P(None, 'dp', 'tensor')
- grad_b_up: float32 [2, 5632], P(None, 'tensor')
- grad_w_down: float32 [5632, 2048], P('tensor', 'dp')
- grad_b_down: float32 [2048], replicated
- grad_ln2_gain: float32 [2048], replicated
- grad_ln2_bias: float32 [2048], replicated
Inputs may be any that keep to these rules, and one draw needn't show every extreme that they name: prefix holds the prefix length of GLM item i: a query at position p of that item sees key q when q < prefix or q <= p; MLM items see every key. counts weigh the two groups in the loss.
All inputs are finite; a program needn't handle non-finite values. No bound on the sum of `loss_mask` on one device may be relied on, other than what follows from the above.
Results may differ from a plain program's by a relative error of at most 0.02.
Values may be sent and summed in bfloat16 or wider, within the bound.
No kernel may reach another device: no remote copies, remote signals or barrier semaphores. Data moves between devices by JAX's collectives and lax.ppermute only.
A program may use at most 320 MiB of HBM per device.

v0:
```python
import jax
import jax.numpy as jnp
from jax import lax
from jax.sharding import PartitionSpec as P

ALPHA = 48.0**0.5
epsilon = 1e-05


def rotary(source):
    length = source.shape[0]
    half_dim = source.shape[-1] // 2
    frequency = 10000.0 ** (-2.0 * jnp.arange(half_dim, dtype=jnp.float32) / source.shape[-1])
    angles = jnp.arange(length, dtype=jnp.float32)[:, None] * frequency[None, :]
    cosine = jnp.cos(angles)[:, None, :]
    sine_table = jnp.sin(angles)[:, None, :]
    first_half = source[..., :half_dim]
    second = source[..., half_dim:]
    return jnp.concatenate(
        [first_half * cosine - second * sine_table, second * cosine + first_half * sine_table],
        axis=-1,
    )


def rope_pair(query_pre, key_pre):
    return (rotary(query_pre), rotary(key_pre))


def layer_norm(source, gain_vec, shift_vec):
    centred = source - jnp.mean(source, axis=-1, keepdims=True)
    variance = jnp.mean(centred * centred, axis=-1, keepdims=True)
    return centred * lax.rsqrt(variance + epsilon) * gain_vec + shift_vec


def geglu(gate_part, up_part):
    return jax.nn.gelu(gate_part) * up_part


def block_scores(query_block, key_bf, start, prefix_length, score_scale):
    length = key_bf.shape[0]
    scores = (
        jnp.einsum("qhd,khd->hqk", query_block, key_bf, preferred_element_type=jnp.float32)
        * score_scale
    )
    query_pos = start + jnp.arange(query_block.shape[0], dtype=jnp.int32)
    key_pos = jnp.arange(length, dtype=jnp.int32)
    visible = (key_pos[None, :] < prefix_length) | (key_pos[None, :] <= query_pos[:, None])
    return jnp.where(visible[None], scores, -1e30)


def shards(
    tokens,
    cotangent,
    loss_mask,
    prefix,
    counts,
    w_qkv,
    b_qkv,
    w_dense,
    b_dense,
    ln1_gain,
    ln1_bias,
    w_up,
    b_up,
    w_down,
    b_down,
    ln2_gain,
    ln2_bias,
):
    item_count = tokens.shape[1]
    row_count = tokens.shape[2]
    model_width = tokens.shape[3]
    length = row_count * lax.axis_size("tensor")
    local_heads = w_qkv.shape[1]
    head_dim = w_qkv.shape[2] // 3
    local_hidden = w_up.shape[2]
    block_rows = min(512, length)
    score_scale = head_dim ** (-0.5)
    group_id = lax.axis_index("obj")
    count_float = counts.astype(jnp.float32)
    share = jnp.where(group_id == 0, count_float[0], count_float[1]) / (
        count_float[0] + count_float[1]
    )
    bias_qkv = b_qkv.astype(jnp.float32)
    bias_dense = b_dense.astype(jnp.float32)
    gain_one = ln1_gain.astype(jnp.float32)
    shift_one = ln1_bias.astype(jnp.float32)
    bias_up = b_up.astype(jnp.float32)
    bias_down = b_down.astype(jnp.float32)
    gain_two = ln2_gain.astype(jnp.float32)
    shift_two = ln2_bias.astype(jnp.float32)

    def fetch():
        return (
            lax.all_gather(w_qkv, "dp", axis=0, tiled=True),
            lax.all_gather(w_dense, "dp", axis=2, tiled=True),
            lax.all_gather(w_up, "dp", axis=1, tiled=True),
            lax.all_gather(w_down, "dp", axis=1, tiled=True),
        )

    def one_item(item_slot, carry):
        outputs, grad_inputs, large_grads, bias_grads, norm_grads = carry
        qkv_full, dense_full, up_full, down_full = fetch()
        token_rows = lax.dynamic_index_in_dim(tokens[0], item_slot, 0, keepdims=False)
        prefix_length = jnp.where(group_id == 0, length, prefix[item_slot])
        gathered = lax.all_gather(token_rows, "tensor", axis=0, tiled=True)
        projected = (
            jnp.einsum("ld,dhe->lhe", gathered, qkv_full, preferred_element_type=jnp.float32)
            + bias_qkv
        )
        (query_rot, key_rot), rope_pull = jax.vjp(
            rope_pair, projected[..., :head_dim], projected[..., head_dim : 2 * head_dim]
        )
        query_bf = query_rot.astype(jnp.bfloat16)
        key_bf = key_rot.astype(jnp.bfloat16)
        value_bf = projected[..., 2 * head_dim :].astype(jnp.bfloat16)
        context_parts = []
        lse_parts = []
        for start in range(0, length, block_rows):
            scores = block_scores(
                query_bf[start : start + block_rows], key_bf, start, prefix_length, score_scale
            )
            highest_score = jnp.max(scores, axis=-1, keepdims=True)
            expo = jnp.exp(scores - highest_score)
            totals = jnp.sum(expo, axis=-1, keepdims=True)
            soft_weights = (expo / totals).astype(jnp.bfloat16)
            context_parts.append(
                jnp.einsum(
                    "hqk,khd->qhd", soft_weights, value_bf, preferred_element_type=jnp.float32
                )
            )
            lse_parts.append((highest_score + jnp.log(totals))[..., 0])
        context_bf = jnp.concatenate(context_parts, axis=0).astype(jnp.bfloat16)
        log_totals = jnp.concatenate(lse_parts, axis=1)
        source = token_rows.astype(jnp.float32)
        piece = lax.slice_in_dim(context_bf, 0, lax.axis_size("tensor") * row_count, axis=0)
        attn_rows = (
            lax.psum_scatter(
                jnp.einsum("lhd,hde->le", piece, dense_full, preferred_element_type=jnp.float32),
                "tensor",
                scatter_dimension=0,
                tiled=True,
            )
            + bias_dense
        )
        first_norm, norm_one_pull = jax.vjp(
            layer_norm, ALPHA * source + attn_rows, gain_one, shift_one
        )
        norm_full = lax.all_gather(first_norm.astype(jnp.bfloat16), "tensor", axis=0, tiled=True)
        gate_up = (
            jnp.einsum("ld,kdf->klf", norm_full, up_full, preferred_element_type=jnp.float32)
            + bias_up[:, None, :]
        )
        activated, act_pull = jax.vjp(geglu, gate_up[0], gate_up[1])
        hidden_bf = activated.astype(jnp.bfloat16)
        piece = lax.slice_in_dim(hidden_bf, 0, lax.axis_size("tensor") * row_count, axis=0)
        mlp_rows = (
            lax.psum_scatter(
                jnp.dot(piece, down_full, preferred_element_type=jnp.float32),
                "tensor",
                scatter_dimension=0,
                tiled=True,
            )
            + bias_down
        )
        result, norm_two_pull = jax.vjp(
            layer_norm, ALPHA * first_norm + mlp_rows, gain_two, shift_two
        )
        qkv_back, dense_back, up_back, down_back = fetch()
        mask_rows = lax.dynamic_index_in_dim(loss_mask[0], item_slot, 0, keepdims=False).astype(
            jnp.float32
        )
        cot_rows = lax.dynamic_index_in_dim(cotangent[0], item_slot, 0, keepdims=False).astype(
            jnp.float32
        )
        grad_out = cot_rows * mask_rows[:, None] * share
        grad_second, grad_gain_two, grad_shift_two = norm_two_pull(grad_out)
        grad_mlp = grad_second.astype(jnp.bfloat16)
        grad_bias_down = jnp.sum(grad_mlp.astype(jnp.float32), axis=0)
        grad_mlp_full = lax.all_gather(grad_mlp, "tensor", axis=0, tiled=True)
        grad_down = jnp.einsum(
            "lf,ld->fd", hidden_bf, grad_mlp_full, preferred_element_type=jnp.float32
        )
        grad_hidden = jnp.einsum(
            "ld,fd->lf", grad_mlp_full, down_back, preferred_element_type=jnp.float32
        )
        grad_gate, grad_upper = act_pull(grad_hidden)
        grad_gate_up = jnp.stack([grad_gate, grad_upper]).astype(jnp.bfloat16)
        grad_bias_up = jnp.sum(grad_gate_up.astype(jnp.float32), axis=1)
        grad_up = jnp.einsum(
            "ld,klf->kdf", norm_full, grad_gate_up, preferred_element_type=jnp.float32
        )
        piece = lax.slice_in_dim(grad_gate_up, 0, lax.axis_size("tensor") * row_count, axis=1)
        grad_norm_one = ALPHA * grad_second + lax.psum_scatter(
            jnp.einsum("klf,kdf->ld", piece, up_back, preferred_element_type=jnp.float32),
            "tensor",
            scatter_dimension=0,
            tiled=True,
        )
        grad_first, grad_gain_one, grad_shift_one = norm_one_pull(grad_norm_one)
        grad_attn = grad_first.astype(jnp.bfloat16)
        grad_bias_dense = jnp.sum(grad_attn.astype(jnp.float32), axis=0)
        grad_attn_full = lax.all_gather(grad_attn, "tensor", axis=0, tiled=True)
        grad_dense = jnp.einsum(
            "lhd,le->hde", context_bf, grad_attn_full, preferred_element_type=jnp.float32
        )
        grad_context = jnp.einsum(
            "le,hde->lhd", grad_attn_full, dense_back, preferred_element_type=jnp.float32
        ).astype(jnp.bfloat16)
        query_grads = []
        key_grad = jnp.zeros((length, local_heads, head_dim), jnp.float32)
        value_grad = jnp.zeros((length, local_heads, head_dim), jnp.float32)
        for start in range(0, length, block_rows):
            query_block = query_bf[start : start + block_rows]
            scores = block_scores(query_block, key_bf, start, prefix_length, score_scale)
            soft_full = jnp.exp(scores - log_totals[:, start : start + block_rows, None])
            context_block = grad_context[start : start + block_rows]
            grad_soft = jnp.einsum(
                "qhd,khd->hqk", context_block, value_bf, preferred_element_type=jnp.float32
            )
            grad_scores = (
                soft_full * (grad_soft - jnp.sum(soft_full * grad_soft, axis=-1, keepdims=True))
            ).astype(jnp.bfloat16)
            query_grads.append(
                jnp.einsum("hqk,khd->qhd", grad_scores, key_bf, preferred_element_type=jnp.float32)
                * score_scale
            )
            key_grad = (
                key_grad
                + jnp.einsum(
                    "hqk,qhd->khd", grad_scores, query_block, preferred_element_type=jnp.float32
                )
                * score_scale
            )
            value_grad = value_grad + jnp.einsum(
                "hqk,qhd->khd",
                soft_full.astype(jnp.bfloat16),
                context_block,
                preferred_element_type=jnp.float32,
            )
        grad_query_pre, grad_key_pre = rope_pull((jnp.concatenate(query_grads, axis=0), key_grad))
        grad_projected = jnp.concatenate(
            [grad_query_pre, grad_key_pre, value_grad], axis=-1
        ).astype(jnp.bfloat16)
        grad_bias_qkv = jnp.sum(grad_projected.astype(jnp.float32), axis=0)
        grad_qkv = jnp.einsum(
            "ld,lhe->dhe", gathered, grad_projected, preferred_element_type=jnp.float32
        )
        piece = lax.slice_in_dim(grad_projected, 0, row_count * lax.axis_size("tensor"), axis=0)
        grad_source = ALPHA * grad_first + lax.psum_scatter(
            jnp.einsum("lhe,dhe->ld", piece, qkv_back, preferred_element_type=jnp.float32).astype(
                jnp.bfloat16
            ),
            "tensor",
            scatter_dimension=0,
            tiled=True,
        ).astype(jnp.float32)
        outputs = lax.dynamic_update_index_in_dim(
            outputs, result.astype(jnp.bfloat16), item_slot, 0
        )
        grad_inputs = lax.dynamic_update_index_in_dim(grad_inputs, grad_source, item_slot, 0)
        large_grads = (
            large_grads[0] + grad_qkv,
            large_grads[1] + grad_dense,
            large_grads[2] + grad_up,
            large_grads[3] + grad_down,
        )
        bias_grads = (bias_grads[0] + grad_bias_qkv, bias_grads[1] + grad_bias_up)
        norm_grads = (
            norm_grads[0] + grad_bias_dense,
            norm_grads[1] + grad_gain_one,
            norm_grads[2] + grad_shift_one,
            norm_grads[3] + grad_bias_down,
            norm_grads[4] + grad_gain_two,
            norm_grads[5] + grad_shift_two,
        )
        return (outputs, grad_inputs, large_grads, bias_grads, norm_grads)

    zero_vector = jnp.zeros((model_width,), jnp.float32)
    initial = (
        jnp.zeros((item_count, row_count, model_width), jnp.bfloat16),
        jnp.zeros((item_count, row_count, model_width), jnp.float32),
        (
            jnp.zeros((model_width, local_heads, 3 * head_dim), jnp.float32),
            jnp.zeros((local_heads, head_dim, model_width), jnp.float32),
            jnp.zeros((2, model_width, local_hidden), jnp.float32),
            jnp.zeros((local_hidden, model_width), jnp.float32),
        ),
        (
            jnp.zeros((local_heads, 3 * head_dim), jnp.float32),
            jnp.zeros((2, local_hidden), jnp.float32),
        ),
        (zero_vector, zero_vector, zero_vector, zero_vector, zero_vector, zero_vector),
    )
    outputs, grad_inputs, large_grads, bias_grads, norm_grads = lax.fori_loop(
        0, item_count, one_item, initial
    )
    sharded = (
        lax.psum_scatter(
            large_grads[0].astype(jnp.bfloat16), "dp", scatter_dimension=0, tiled=True
        ).astype(jnp.float32),
        lax.psum_scatter(
            large_grads[1].astype(jnp.bfloat16), "dp", scatter_dimension=2, tiled=True
        ).astype(jnp.float32),
        lax.psum_scatter(
            large_grads[2].astype(jnp.bfloat16), "dp", scatter_dimension=1, tiled=True
        ).astype(jnp.float32),
        lax.psum_scatter(
            large_grads[3].astype(jnp.bfloat16), "dp", scatter_dimension=1, tiled=True
        ).astype(jnp.float32),
    )
    merged = (
        lax.psum(sharded[0].astype(jnp.bfloat16), "obj").astype(jnp.float32),
        lax.psum(sharded[1].astype(jnp.bfloat16), "obj").astype(jnp.float32),
        lax.psum(sharded[2].astype(jnp.bfloat16), "obj").astype(jnp.float32),
        lax.psum(sharded[3].astype(jnp.bfloat16), "obj").astype(jnp.float32),
    )
    bias_total = lax.psum((bias_grads[0], bias_grads[1]), ("obj", "dp"))
    norm_total = lax.psum(
        (norm_grads[0], norm_grads[1], norm_grads[2], norm_grads[3], norm_grads[4], norm_grads[5]),
        ("obj", "dp", "tensor"),
    )
    return (
        outputs[None],
        grad_inputs[None],
        merged[0],
        bias_total[0],
        merged[1],
        norm_total[0],
        norm_total[1],
        norm_total[2],
        merged[2],
        bias_total[1],
        merged[3],
        norm_total[3],
        norm_total[4],
        norm_total[5],
    )


def solution(mesh):
    return jax.shard_map(
        shards,
        mesh=mesh,
        in_specs=(
            P("obj", "dp", "tensor", None),
            P("obj", "dp", "tensor", None),
            P("obj", "dp", "tensor"),
            P("dp"),
            P(),
            P("dp", "tensor", None),
            P("tensor", None),
            P("tensor", None, "dp"),
            P(),
            P(),
            P(),
            P(None, "dp", "tensor"),
            P(None, "tensor"),
            P("tensor", "dp"),
            P(),
            P(),
            P(),
        ),
        out_specs=(
            P("obj", "dp", "tensor", None),
            P("obj", "dp", "tensor", None),
            P("dp", "tensor", None),
            P("tensor", None),
            P("tensor", None, "dp"),
            P(),
            P(),
            P(),
            P(None, "dp", "tensor"),
            P(None, "tensor"),
            P("tensor", "dp"),
            P(),
            P(),
            P(),
        ),
        check_vma=False,
    )
```

profile of v0, /device:TPU:0, one launch (start us, length us, event | category | flops | bytes accessed | tf_op | source)
XLA Modules:
  0.0 2827.7 jit_solution(6902877429281962899)
XLA Ops:
  21.9 2303.0 %while.42 = (s32[]{:T(128)}, bf16[2,256,2048]{2,1,0:T(8,128)(2,1)}, f32[2,256,2048]{2,1,0:T(8,128)}, f32[2048,4,384]{2,0,1:T(8,128)}, f32[4,128,2048]{2,1,0:T(8,...) while((s32[]{:T(128)}, bf16[2,256,2048]{2,1,0:T(8,128)(2,1)}, ...), condition=%wide.region_27.28_spmd.clone, body=%wide.region_0.27_spmd.clone.sunk | while | flops 85634670592 | bytes 1224860288 | solution.py:295
  29.0 79.8 %all-gather.19.cloned.1.call-done = bf16[1,1,1024,2048]{3,2,1,0:T(8,128)(2,1)} async-done(((bf16[1,1,256,2048]{3,2,1,0:T(8,128)(2,1)}), bf16[1,1,1024,2048]{3,2,1,0:T(8,128)(2,1)}) %all-gather.19.cloned.1.call-update) | async-done | bytes 4194320 | tf_op jit(solution)/shard_map/while/body/eval_jaxpr/all_gather | solution.py:106
  108.8 46.6 %all-gather.17.cloned.1.call-done = bf16[2048,4,384]{0,2,1:T(8,128)(2,1)} async-done(((bf16[512,4,384]{0,2,1:T(8,128)(2,1)}), bf16[2048,4,384]{0,2,1:T(8,128)(2,1)}) %all-gather.17.cloned.1.call-update) | async-done | bytes 6291472 | tf_op jit(solution)/shard_map/while/body/eval_jaxpr/all_gather | solution.py:95
  155.4 10.1 broadcast_add_fusion.2
  179.6 7.2 convolution_bitcast_fusion.4
  187.5 144.0 %reduce-scatter.14.cloned.1.call-done = f32[256,2048]{1,0:T(8,128)} async-done(((f32[1024,2048]{1,0:T(8,128)}), f32[256,2048]{1,0:T(8,128)}) %reduce-scatter.14.cloned.1.call-update) | async-done | bytes 2097168 | tf_op jit(solution)/shard_map/while/body/eval_jaxpr/reduce_scatter | solution.py:138
  336.4 73.5 %all-gather.13.cloned.1.call-done = bf16[2,2048,1408]{2,1,0:T(8,128)(2,1)} async-done(((bf16[2,512,1408]{2,1,0:T(8,128)(2,1)}), bf16[2,2048,1408]{2,1,0:T(8,128)(2,1)}) %all-gather.13.cloned.1.call-update) | async-done | bytes 11534352 | tf_op jit(solution)/shard_map/while/body/eval_jaxpr/all_gather | solution.py:97
  409.9 82.9 %all-gather.21.cloned.1.call-done = bf16[1024,2048]{1,0:T(8,128)(2,1)} async-done(((bf16[256,2048]{1,0:T(8,128)(2,1)}), bf16[1024,2048]{1,0:T(8,128)(2,1)}) %all-gather.21.cloned.1.call-update) | async-done | bytes 4194320 | tf_op jit(solution)/shard_map/while/body/eval_jaxpr/all_gather | solution.py:149
  492.8 17.2 add_bitcast_fusion.2
  510.0 4.2 copy-done.7
  517.3 19.1 all-gather.23.cloned.1.call-done
  536.4 11.5 fusion.210
  548.6 144.0 %reduce-scatter.16.cloned.1.call-done = f32[256,2048]{1,0:T(8,128)} async-done(((f32[1024,2048]{1,0:T(8,128)}), f32[256,2048]{1,0:T(8,128)}) %reduce-scatter.16.cloned.1.call-update) | async-done | bytes 2097168 | tf_op jit(solution)/shard_map/while/body/eval_jaxpr/reduce_scatter | solution.py:158
  700.0 81.6 %all-gather.25.cloned.1.call-done = bf16[1024,2048]{1,0:T(8,128)(2,1)} async-done(((bf16[256,2048]{1,0:T(8,128)(2,1)}), bf16[1024,2048]{1,0:T(8,128)(2,1)}) %all-gather.25.cloned.1.call-update) | async-done | bytes 4194320 | tf_op jit(solution)/shard_map/while/body/eval_jaxpr/all_gather | solution.py:180
  781.6 16.2 fusion.217
  800.3 16.9 convolution_bitcast_fusion.5
  817.3 143.1 %reduce-scatter.18.cloned.1.call-done = f32[256,2048]{1,0:T(8,128)} async-done(((f32[1024,2048]{1,0:T(8,128)}), f32[256,2048]{1,0:T(8,128)}) %reduce-scatter.18.cloned.1.call-update) | async-done | bytes 2097168 | tf_op jit(solution)/shard_map/while/body/eval_jaxpr/reduce_scatter | solution.py:194
  968.7 79.8 %all-gather.27.cloned.1.call-done = bf16[1024,2048]{1,0:T(8,128)(2,1)} async-done(((bf16[256,2048]{1,0:T(8,128)(2,1)}), bf16[1024,2048]{1,0:T(8,128)(2,1)}) %all-gather.27.cloned.1.call-update) | async-done | bytes 4194320 | tf_op jit(solution)/shard_map/while/body/eval_jaxpr/all_gather | solution.py:203
  1048.6 5.2 fusion.219
  1053.8 5.5 multiply_reduce_fusion.15
  1059.4 4.4 multiply_convert_fusion.9
  1070.3 3.8 multiply_reduce_fusion.14
  1084.4 9.0 bitcast_convert_fusion.2
  1093.5 11.4 select_add_fusion.22
  1106.0 20.5 bitcast_add_fusion.4
  1127.2 7.0 select_add_fusion.21
  1134.3 10.0 select_add_fusion.20
  1144.4 24.6 reduce-scatter.20.cloned.1.call-done
  1178.8 77.9 %all-gather.19.cloned.1.call-done = bf16[1,1,1024,2048]{3,2,1,0:T(8,128)(2,1)} async-done(((bf16[1,1,256,2048]{3,2,1,0:T(8,128)(2,1)}), bf16[1,1,1024,2048]{3,2,1,0:T(8,128)(2,1)}) %all-gather.19.cloned.1.call-update) | async-done | bytes 4194320 | tf_op jit(solution)/shard_map/while/body/eval_jaxpr/all_gather | solution.py:106
  1256.7 46.4 %all-gather.17.cloned.1.call-done = bf16[2048,4,384]{0,2,1:T(8,128)(2,1)} async-done(((bf16[512,4,384]{0,2,1:T(8,128)(2,1)}), bf16[2048,4,384]{0,2,1:T(8,128)(2,1)}) %all-gather.17.cloned.1.call-update) | async-done | bytes 6291472 | tf_op jit(solution)/shard_map/while/body/eval_jaxpr/all_gather | solution.py:95
  1303.1 10.1 broadcast_add_fusion.2
  1327.3 7.2 convolution_bitcast_fusion.4
  1335.1 144.0 %reduce-scatter.14.cloned.1.call-done = f32[256,2048]{1,0:T(8,128)} async-done(((f32[1024,2048]{1,0:T(8,128)}), f32[256,2048]{1,0:T(8,128)}) %reduce-scatter.14.cloned.1.call-update) | async-done | bytes 2097168 | tf_op jit(solution)/shard_map/while/body/eval_jaxpr/reduce_scatter | solution.py:138
  1484.0 73.5 %all-gather.13.cloned.1.call-done = bf16[2,2048,1408]{2,1,0:T(8,128)(2,1)} async-done(((bf16[2,512,1408]{2,1,0:T(8,128)(2,1)}), bf16[2,2048,1408]{2,1,0:T(8,128)(2,1)}) %all-gather.13.cloned.1.call-update) | async-done | bytes 11534352 | tf_op jit(solution)/shard_map/while/body/eval_jaxpr/all_gather | solution.py:97
  1557.5 82.9 %all-gather.21.cloned.1.call-done = bf16[1024,2048]{1,0:T(8,128)(2,1)} async-done(((bf16[256,2048]{1,0:T(8,128)(2,1)}), bf16[1024,2048]{1,0:T(8,128)(2,1)}) %all-gather.21.cloned.1.call-update) | async-done | bytes 4194320 | tf_op jit(solution)/shard_map/while/body/eval_jaxpr/all_gather | solution.py:149
  1640.4 17.2 add_bitcast_fusion.2
  1657.6 4.2 copy-done.7
  1664.9 19.1 all-gather.23.cloned.1.call-done
  1684.0 11.5 fusion.210
  1696.2 144.0 %reduce-scatter.16.cloned.1.call-done = f32[256,2048]{1,0:T(8,128)} async-done(((f32[1024,2048]{1,0:T(8,128)}), f32[256,2048]{1,0:T(8,128)}) %reduce-scatter.16.cloned.1.call-update) | async-done | bytes 2097168 | tf_op jit(solution)/shard_map/while/body/eval_jaxpr/reduce_scatter | solution.py:158
  1847.6 81.6 %all-gather.25.cloned.1.call-done = bf16[1024,2048]{1,0:T(8,128)(2,1)} async-done(((bf16[256,2048]{1,0:T(8,128)(2,1)}), bf16[1024,2048]{1,0:T(8,128)(2,1)}) %all-gather.25.cloned.1.call-update) | async-done | bytes 4194320 | tf_op jit(solution)/shard_map/while/body/eval_jaxpr/all_gather | solution.py:180
  1929.2 16.2 fusion.217
  1947.9 16.9 convolution_bitcast_fusion.5
  1964.9 143.1 %reduce-scatter.18.cloned.1.call-done = f32[256,2048]{1,0:T(8,128)} async-done(((f32[1024,2048]{1,0:T(8,128)}), f32[256,2048]{1,0:T(8,128)}) %reduce-scatter.18.cloned.1.call-update) | async-done | bytes 2097168 | tf_op jit(solution)/shard_map/while/body/eval_jaxpr/reduce_scatter | solution.py:194
  2116.3 79.8 %all-gather.27.cloned.1.call-done = bf16[1024,2048]{1,0:T(8,128)(2,1)} async-done(((bf16[256,2048]{1,0:T(8,128)(2,1)}), bf16[1024,2048]{1,0:T(8,128)(2,1)}) %all-gather.27.cloned.1.call-update) | async-done | bytes 4194320 | tf_op jit(solution)/shard_map/while/body/eval_jaxpr/all_gather | solution.py:203
  2196.2 5.2 fusion.219
  2201.4 5.5 multiply_reduce_fusion.15
  2207.0 4.4 multiply_convert_fusion.9
  2232.1 8.8 bitcast_convert_fusion.2
  2240.9 13.1 select_add_fusion.22
  2255.0 24.0 bitcast_add_fusion.4
  2279.8 8.3 select_add_fusion.21
  2288.2 12.9 select_add_fusion.20
  2301.1 15.2 reduce-scatter.20.cloned.1.call-done
  2324.9 15.7 copy.81
  2344.6 8.9 convert_element_type.342
  2353.6 18.6 copy.64
  2374.2 86.4 %all-reduce.11.cloned.1.call-done = bf16[2048,4,384]{2,1,0:T(4,128)(2,1)} async-done(((bf16[2048,4,384]{2,1,0:T(4,128)(2,1)}), bf16[2048,4,384]{2,1,0:T(4,128)(2,1)}) %all-reduce.11.cloned.1.call-update) | async-done | bytes 6291472
  2463.7 31.4 %reduce-scatter.8.cloned.1.call-done = bf16[4,128,512]{2,1,0:T(8,128)(2,1)} async-done(((bf16[4,128,2048]{2,1,0:T(8,128)(2,1)}), bf16[4,128,512]{2,1,0:T(8,128)(2,1)}) %reduce-scatter.8.cloned.1.call-update) | async-done | bytes 524304 | tf_op jit(solution)/shard_map/reduce_scatter | solution.py:302
  2495.2 57.9 %reduce-scatter.12.cloned.1.call-done = bf16[1408,512]{1,0:T(8,128)(2,1)} async-done(((bf16[1408,2048]{1,0:T(8,128)(2,1)}), bf16[1408,512]{1,0:T(8,128)(2,1)}) %reduce-scatter.12.cloned.1.call-update) | async-done | bytes 1441808 | tf_op jit(solution)/shard_map/reduce_scatter | solution.py:308
  2553.1 94.7 %reduce-scatter.10.cloned.1.call-done = bf16[2,512,1408]{2,1,0:T(8,128)(2,1)} async-done(((bf16[2,2048,1408]{2,1,0:T(8,128)(2,1)}), bf16[2,512,1408]{2,1,0:T(8,128)(2,1)}) %reduce-scatter.10.cloned.1.call-update) | async-done | bytes 2883600 | tf_op jit(solution)/shard_map/reduce_scatter | solution.py:305
  2647.9 41.0 %all-reduce.5 = (f32[2048]{0:T(1024)}, f32[2048]{0:T(1024)}, f32[2048]{0:T(1024)}, f32[2048]{0:T(1024)}, f32[2048]{0:T(1024)}, /*index=5*/f32[2048]{0:T(1024)}) all-reduce(f32[2048]{0:T(1024)S(1)} %copy-done.61, f32[2048]{0:T(1024)S(1)} %copy-done.58, ...), channel_id=1, replica_groups=mesh['obj'=2,'dp'=4,'tensor'=4] {'obj','dp','tensor'}, use_global_device_ids=true, to_apply=%region_33.34 | all-reduce | flops 12288 | bytes 98304 | tf_op jit(solution)/shard_map/psum | solution.py:319
  2688.9 24.1 all-reduce.6
  2713.0 96.1 %all-reduce.13.cloned.1.call-done = (bf16[512,4,384]{2,1,0:T(4,128)(2,1)}, bf16[4,128,512]{2,1,0:T(8,128)(2,1)}, bf16[2,512,1408]{2,1,0:T(8,128)(2,1)}, bf16[1408,512]{1,0:T(8,128)(2,1)}) async-done(((bf16[512,4,384]{2,1,0:T(4,128)(2,1)}, bf16[4,128,512]{2,1,0:T(8,128)(2,1)}, bf16[2,512,1408]{2,1,0:T(8,128)(2,1)}, bf16[1408,512]{1,0:T(8,128)(2,1)}), (bf16[512,4,384]{2,1,0:T(4,128)(2,1)}, ...) | async-done | bytes 6422544 | tf_op jit(solution)/shard_map/psum | solution.py:313
  (511 shorter events, 171.1 us)
Async XLA Ops:
  22.2 143.3 %copy-start.68 = (f32[4,384]{1,0:T(4,128)}, f32[4,384]{1,0:T(4,128)S(1)}, u32[]{:S(2)}) copy-start(f32[4,384]{1,0:T(4,128)S(1)} %get-tuple-element.1471) | copy-start | bytes 18436 | tf_op jit(solution)/shard_map/while
  22.2 309.3 %copy-start.39 = (f32[2048]{0:T(1024)}, f32[2048]{0:T(1024)S(1)}, u32[]{:S(2)}) copy-start(f32[2048]{0:T(1024)S(1)} %get-tuple-element.1475) | copy-start | bytes 24580 | tf_op jit(solution)/shard_map/while
  22.2 470.6 %copy-start.66 = (f32[2,1408]{1,0:T(2,128)}, f32[2,1408]{1,0:T(2,128)S(1)}, u32[]{:S(2)}) copy-start(f32[2,1408]{1,0:T(2,128)S(1)} %get-tuple-element.1479) | copy-start | bytes 33796 | tf_op jit(solution)/shard_map/while
  22.2 670.3 %copy-start.34 = (f32[2048]{0:T(1024)}, f32[2048]{0:T(1024)S(1)}, u32[]{:S(2)}) copy-start(f32[2048]{0:T(1024)S(1)} %get-tuple-element.1477) | copy-start | bytes 24580 | tf_op jit(solution)/shard_map/while
  22.2 670.3 %copy-start.41 = (f32[2048]{0:T(1024)}, f32[2048]{0:T(1024)S(1)}, u32[]{:S(2)}) copy-start(f32[2048]{0:T(1024)S(1)} %get-tuple-element.1481) | copy-start | bytes 24580 | tf_op jit(solution)/shard_map/while
  22.2 86.6 %all-gather.19.cloned.1.call-start = ((), (), s32[]{:S(2)}) async-start(), calls=%async_computation.15 | async-start | bytes 5242880 | tf_op jit(solution)/shard_map/while/body/eval_jaxpr/all_gather | solution.py:106
  24.6 130.8 %all-gather.17.cloned.1.call-start = ((), (), s32[]{:S(2)}) async-start(), calls=%async_computation.14 | async-start | bytes 7864320 | tf_op jit(solution)/shard_map/while/body/eval_jaxpr/all_gather | solution.py:95
  25.4 154.3 %all-gather.15.cloned.1.call-start = ((), (), s32[]{:S(2)}) async-start(), calls=%async_computation.13 | async-start | bytes 2621440 | tf_op jit(solution)/shard_map/while/body/eval_jaxpr/all_gather | solution.py:96
  26.1 305.4 %reduce-scatter.14.cloned.1.call-start = ((), (), s32[]{:S(2)}) async-start(), calls=%async_computation.16 | async-start | bytes 10485760 | tf_op jit(solution)/shard_map/while/body/eval_jaxpr/reduce_scatter | solution.py:138
  28.4 137.1 %copy-start.27 = (f32[1024,64]{0,1:T(8,128)}, f32[1024,64]{0,1:T(8,128)S(1)}, u32[]{:S(2)}) copy-start(f32[1024,64]{0,1:T(8,128)S(1)} %get-tuple-element.1336) | copy-start | bytes 786436 | tf_op jit(solution)/shard_map/while
  28.4 137.1 %copy-start.29 = (f32[1024,64]{0,1:T(8,128)}, f32[1024,64]{0,1:T(8,128)S(1)}, u32[]{:S(2)}) copy-start(f32[1024,64]{0,1:T(8,128)S(1)} %get-tuple-element.1335) | copy-start | bytes 786436 | tf_op jit(solution)/shard_map/while
  186.9 223.0 %all-gather.13.cloned.1.call-start = ((), (), s32[]{:S(2)}) async-start(), calls=%async_computation.12 | async-start | bytes 14417920 | tf_op jit(solution)/shard_map/while/body/eval_jaxpr/all_gather | solution.py:97
  187.5 305.3 %all-gather.21.cloned.1.call-start = ((), (), s32[]{:S(2)}) async-start(), calls=%async_computation.17 | async-start | bytes 5242880 | tf_op jit(solution)/shard_map/while/body/eval_jaxpr/all_gather | solution.py:149
  335.6 200.8 %all-gather.23.cloned.1.call-start = ((), (), s32[]{:S(2)}) async-start(), calls=%async_computation.18 | async-start | bytes 7208960 | tf_op jit(solution)/shard_map/while/body/eval_jaxpr/all_gather | solution.py:98
  336.4 356.2 %reduce-scatter.16.cloned.1.call-start = ((), (), s32[]{:S(2)}) async-start(), calls=%async_computation.19 | async-start | bytes 10485760 | tf_op jit(solution)/shard_map/while/body/eval_jaxpr/reduce_scatter | solution.py:158
  547.9 233.7 %all-gather.25.cloned.1.call-start = ((), (), s32[]{:S(2)}) async-start(), calls=%async_computation.20 | async-start | bytes 5242880 | tf_op jit(solution)/shard_map/while/body/eval_jaxpr/all_gather | solution.py:180
  699.9 260.4 %reduce-scatter.18.cloned.1.call-start = ((), (), s32[]{:S(2)}) async-start(), calls=%async_computation.21 | async-start | bytes 10485760 | tf_op jit(solution)/shard_map/while/body/eval_jaxpr/reduce_scatter | solution.py:194
  817.3 231.3 %all-gather.27.cloned.1.call-start = ((), (), s32[]{:S(2)}) async-start(), calls=%async_computation.22 | async-start | bytes 5242880 | tf_op jit(solution)/shard_map/while/body/eval_jaxpr/all_gather | solution.py:203
  966.9 202.0 %reduce-scatter.20.cloned.1.call-start = ((), (), s32[]{:S(2)}) async-start(), calls=%async_computation.23 | async-start | bytes 5242880 | tf_op jit(solution)/shard_map/while/body/eval_jaxpr/reduce_scatter | solution.py:250
  967.2 86.6 %copy-start.51 = (f32[2048]{0:T(1024)}, f32[2048]{0:T(1024)S(1)}, u32[]{:S(2)}) copy-start(f32[2048]{0:T(1024)S(1)} %select_add_fusion.27) | copy-start | bytes 24580 | tf_op jit(solution)/shard_map/while
  967.3 86.5 %copy-start.45 = (f32[2048]{0:T(1024)}, f32[2048]{0:T(1024)S(1)}, u32[]{:S(2)}) copy-start(f32[2048]{0:T(1024)S(1)} %get-tuple-element.1468) | copy-start | bytes 24580 | tf_op jit(solution)/shard_map/while
  967.3 86.5 %copy-start.48 = (f32[2048]{0:T(1024)}, f32[2048]{0:T(1024)S(1)}, u32[]{:S(2)}) copy-start(f32[2048]{0:T(1024)S(1)} %get-tuple-element.1467) | copy-start | bytes 24580 | tf_op jit(solution)/shard_map/while
  1134.3 34.6 %copy-start.6 = (f32[256,2048]{1,0:T(8,128)S(1)}, f32[256,2048]{1,0:T(8,128)}, u32[]{:S(2)}) copy-start(f32[256,2048]{1,0:T(8,128)} %copy-done.5) | copy-start | bytes 6291460 | tf_op jit(solution)/shard_map/while
  1144.3 27.5 copy-start.35
  1144.4 27.5 copy-start.40
  1144.4 27.5 copy-start.42
  1144.4 27.5 copy-start.67
  1144.4 27.5 copy-start.69
  1172.3 141.0 %copy-start.68 = (f32[4,384]{1,0:T(4,128)}, f32[4,384]{1,0:T(4,128)S(1)}, u32[]{:S(2)}) copy-start(f32[4,384]{1,0:T(4,128)S(1)} %get-tuple-element.1471) | copy-start | bytes 18436 | tf_op jit(solution)/shard_map/while
  1172.3 306.8 %copy-start.39 = (f32[2048]{0:T(1024)}, f32[2048]{0:T(1024)S(1)}, u32[]{:S(2)}) copy-start(f32[2048]{0:T(1024)S(1)} %get-tuple-element.1475) | copy-start | bytes 24580 | tf_op jit(solution)/shard_map/while
  1172.3 468.1 %copy-start.66 = (f32[2,1408]{1,0:T(2,128)}, f32[2,1408]{1,0:T(2,128)S(1)}, u32[]{:S(2)}) copy-start(f32[2,1408]{1,0:T(2,128)S(1)} %get-tuple-element.1479) | copy-start | bytes 33796 | tf_op jit(solution)/shard_map/while
  1172.3 667.8 %copy-start.34 = (f32[2048]{0:T(1024)}, f32[2048]{0:T(1024)S(1)}, u32[]{:S(2)}) copy-start(f32[2048]{0:T(1024)S(1)} %get-tuple-element.1477) | copy-start | bytes 24580 | tf_op jit(solution)/shard_map/while
  1172.3 667.8 %copy-start.41 = (f32[2048]{0:T(1024)}, f32[2048]{0:T(1024)S(1)}, u32[]{:S(2)}) copy-start(f32[2048]{0:T(1024)S(1)} %get-tuple-element.1481) | copy-start | bytes 24580 | tf_op jit(solution)/shard_map/while
  1172.3 84.4 %all-gather.19.cloned.1.call-start = ((), (), s32[]{:S(2)}) async-start(), calls=%async_computation.15 | async-start | bytes 5242880 | tf_op jit(solution)/shard_map/while/body/eval_jaxpr/all_gather | solution.py:106
  1174.7 128.4 %all-gather.17.cloned.1.call-start = ((), (), s32[]{:S(2)}) async-start(), calls=%async_computation.14 | async-start | bytes 7864320 | tf_op jit(solution)/shard_map/while/body/eval_jaxpr/all_gather | solution.py:95
  1175.3 152.0 %all-gather.15.cloned.1.call-start = ((), (), s32[]{:S(2)}) async-start(), calls=%async_computation.13 | async-start | bytes 2621440 | tf_op jit(solution)/shard_map/while/body/eval_jaxpr/all_gather | solution.py:96
  1175.9 303.2 %reduce-scatter.14.cloned.1.call-start = ((), (), s32[]{:S(2)}) async-start(), calls=%async_computation.16 | async-start | bytes 10485760 | tf_op jit(solution)/shard_map/while/body/eval_jaxpr/reduce_scatter | solution.py:138
  1178.2 135.1 %copy-start.27 = (f32[1024,64]{0,1:T(8,128)}, f32[1024,64]{0,1:T(8,128)S(1)}, u32[]{:S(2)}) copy-start(f32[1024,64]{0,1:T(8,128)S(1)} %get-tuple-element.1336) | copy-start | bytes 786436 | tf_op jit(solution)/shard_map/while
  1178.2 135.1 %copy-start.29 = (f32[1024,64]{0,1:T(8,128)}, f32[1024,64]{0,1:T(8,128)S(1)}, u32[]{:S(2)}) copy-start(f32[1024,64]{0,1:T(8,128)S(1)} %get-tuple-element.1335) | copy-start | bytes 786436 | tf_op jit(solution)/shard_map/while
  1334.5 223.0 %all-gather.13.cloned.1.call-start = ((), (), s32[]{:S(2)}) async-start(), calls=%async_computation.12 | async-start | bytes 14417920 | tf_op jit(solution)/shard_map/while/body/eval_jaxpr/all_gather | solution.py:97
  1335.1 305.3 %all-gather.21.cloned.1.call-start = ((), (), s32[]{:S(2)}) async-start(), calls=%async_computation.17 | async-start | bytes 5242880 | tf_op jit(solution)/shard_map/while/body/eval_jaxpr/all_gather | solution.py:149
  1483.2 200.8 %all-gather.23.cloned.1.call-start = ((), (), s32[]{:S(2)}) async-start(), calls=%async_computation.18 | async-start | bytes 7208960 | tf_op jit(solution)/shard_map/while/body/eval_jaxpr/all_gather | solution.py:98
  1484.0 356.2 %reduce-scatter.16.cloned.1.call-start = ((), (), s32[]{:S(2)}) async-start(), calls=%async_computation.19 | async-start | bytes 10485760 | tf_op jit(solution)/shard_map/while/body/eval_jaxpr/reduce_scatter | solution.py:158
  1695.5 233.7 %all-gather.25.cloned.1.call-start = ((), (), s32[]{:S(2)}) async-start(), calls=%async_computation.20 | async-start | bytes 5242880 | tf_op jit(solution)/shard_map/while/body/eval_jaxpr/all_gather | solution.py:180
  1847.6 260.5 %reduce-scatter.18.cloned.1.call-start = ((), (), s32[]{:S(2)}) async-start(), calls=%async_computation.21 | async-start | bytes 10485760 | tf_op jit(solution)/shard_map/while/body/eval_jaxpr/reduce_scatter | solution.py:194
  1964.9 231.3 %all-gather.27.cloned.1.call-start = ((), (), s32[]{:S(2)}) async-start(), calls=%async_computation.22 | async-start | bytes 5242880 | tf_op jit(solution)/shard_map/while/body/eval_jaxpr/all_gather | solution.py:203
  2114.5 201.8 %reduce-scatter.20.cloned.1.call-start = ((), (), s32[]{:S(2)}) async-start(), calls=%async_computation.23 | async-start | bytes 5242880 | tf_op jit(solution)/shard_map/while/body/eval_jaxpr/reduce_scatter | solution.py:250
  2114.8 86.6 %copy-start.51 = (f32[2048]{0:T(1024)}, f32[2048]{0:T(1024)S(1)}, u32[]{:S(2)}) copy-start(f32[2048]{0:T(1024)S(1)} %select_add_fusion.27) | copy-start | bytes 24580 | tf_op jit(solution)/shard_map/while
  2114.9 86.6 %copy-start.45 = (f32[2048]{0:T(1024)}, f32[2048]{0:T(1024)S(1)}, u32[]{:S(2)}) copy-start(f32[2048]{0:T(1024)S(1)} %get-tuple-element.1468) | copy-start | bytes 24580 | tf_op jit(solution)/shard_map/while
  2114.9 86.5 %copy-start.48 = (f32[2048]{0:T(1024)}, f32[2048]{0:T(1024)S(1)}, u32[]{:S(2)}) copy-start(f32[2048]{0:T(1024)S(1)} %get-tuple-element.1467) | copy-start | bytes 24580 | tf_op jit(solution)/shard_map/while
  2288.2 28.2 copy-start.6
  2324.9 135.8 %all-reduce.11.cloned.1.call-start = ((), (), s32[]{:S(2)}) async-start(), calls=%async_computation.10 | async-start | bytes 12582912
  2340.7 154.5 %reduce-scatter.8.cloned.1.call-start = ((), (), s32[]{:S(2)}) async-start(), calls=%async_computation.7 | async-start | bytes 2621440 | tf_op jit(solution)/shard_map/reduce_scatter | solution.py:302
  2344.6 208.5 %reduce-scatter.12.cloned.1.call-start = ((), (), s32[]{:S(2)}) async-start(), calls=%async_computation.9 | async-start | bytes 7208960 | tf_op jit(solution)/shard_map/reduce_scatter | solution.py:308
  2353.5 294.2 %reduce-scatter.10.cloned.1.call-start = ((), (), s32[]{:S(2)}) async-start(), calls=%async_computation.8 | async-start | bytes 14417920 | tf_op jit(solution)/shard_map/reduce_scatter | solution.py:305
  2372.2 436.9 %all-reduce.13.cloned.1.call-start = ((), (), s32[]{:S(2)}) async-start(), calls=%async_computation.11 | async-start | bytes 12845056 | tf_op jit(solution)/shard_map/psum | solution.py:313
  2374.1 273.7 %copy-start.46 = (f32[2048]{0:T(1024)S(1)}, f32[2048]{0:T(1024)}, u32[]{:S(2)}) copy-start(f32[2048]{0:T(1024)} %get-tuple-element.791) | copy-start | bytes 24580
  2374.1 273.7 %copy-start.49 = (f32[2048]{0:T(1024)S(1)}, f32[2048]{0:T(1024)}, u32[]{:S(2)}) copy-start(f32[2048]{0:T(1024)} %get-tuple-element.790) | copy-start | bytes 24580
  2374.1 273.7 %copy-start.52 = (f32[2048]{0:T(1024)S(1)}, f32[2048]{0:T(1024)}, u32[]{:S(2)}) copy-start(f32[2048]{0:T(1024)} %get-tuple-element.789) | copy-start | bytes 24580
  2374.1 273.7 %copy-start.55 = (f32[2048]{0:T(1024)S(1)}, f32[2048]{0:T(1024)}, u32[]{:S(2)}) copy-start(f32[2048]{0:T(1024)} %get-tuple-element.785) | copy-start | bytes 24580
  2374.2 273.7 %copy-start.58 = (f32[2048]{0:T(1024)S(1)}, f32[2048]{0:T(1024)}, u32[]{:S(2)}) copy-start(f32[2048]{0:T(1024)} %get-tuple-element.784) | copy-start | bytes 24580
  2374.2 273.7 %copy-start.61 = (f32[2048]{0:T(1024)S(1)}, f32[2048]{0:T(1024)}, u32[]{:S(2)}) copy-start(f32[2048]{0:T(1024)} %get-tuple-element.783) | copy-start | bytes 24580
  2374.2 314.7 %copy-start.38 = (f32[2,1408]{1,0:T(2,128)S(1)}, f32[2,1408]{1,0:T(2,128)}, u32[]{:S(2)}) copy-start(f32[2,1408]{1,0:T(2,128)} %get-tuple-element.787) | copy-start | bytes 33796
  2374.2 314.7 %copy-start.64 = (f32[4,384]{1,0:T(4,128)S(1)}, f32[4,384]{1,0:T(4,128)}, u32[]{:S(2)}) copy-start(f32[4,384]{1,0:T(4,128)} %get-tuple-element.781) | copy-start | bytes 18436
  (116 other events, 837.9 us)
Sparse Core Ops, SparseCore 0:
  25.3 83.4 all-gather.18
  110.4 44.9 all-gather.16
  157.0 22.5 all-gather.14
  187.0 144.4 reduce-scatter.13
  333.0 76.8 all-gather.12
  412.0 80.7 all-gather.20
  494.4 41.9 all-gather.22
  548.0 144.4 reduce-scatter.15
  700.1 81.4 all-gather.24
  817.4 142.9 reduce-scatter.17
  967.0 81.4 all-gather.26
  1093.6 75.2 reduce-scatter.19
  1175.4 81.2 all-gather.18
  1258.2 44.9 all-gather.16
  1304.6 22.5 all-gather.14
  1334.6 144.4 reduce-scatter.13
  1480.6 76.8 all-gather.12
  1559.6 80.7 all-gather.20
  1642.0 41.9 all-gather.22
  1695.6 144.4 reduce-scatter.15
  1847.7 81.4 all-gather.24
  1965.0 142.9 reduce-scatter.17
  2114.6 81.4 all-gather.26
  2241.0 75.2 reduce-scatter.19
Sparse Core Ops, SparseCore 1:
  2340.8 119.8 all-reduce.10
  2463.6 31.5 reduce-scatter.7
  2498.3 54.7 reduce-scatter.11
  2555.7 92.0 reduce-scatter.9
  2651.0 158.1 all-reduce.12
where the time goes:
time: 2830 us
  waiting for transfers between devices  2200 us (78%)
  matrix products  350 us (12%)
  other arithmetic  105 us (4%)
  local copies, waits for them, and re-layouts  76.4 us (3%)
  blocking collectives  65.2 us (2%)
    reduce_scatter x2, waiting for transfers between devices, one_item(): lax.psum_scatter(jnp.einsum('lhd,hde->le', piece, dense_full, preferred_e...  288 us
    reduce_scatter x2, waiting for transfers between devices, one_item(): lax.psum_scatter(jnp.dot(piece, down_full, preferred_element_type=jnp.flo...  288 us
    reduce_scatter x2, waiting for transfers between devices, one_item(): lax.psum_scatter(jnp.einsum('klf,kdf->ld', piece, up_back, preferred_elem...  286 us
    all_gather x2, waiting for transfers between devices, one_item(): lax.all_gather(first_norm.astype(jnp.bfloat16), 'tensor', axis=0, tiled=T...  166 us
    all_gather x2, waiting for transfers between devices, one_item(): grad_mlp_full = lax.all_gather(grad_mlp, 'tensor', axis=0, tiled=True)  163 us
    all_gather x2, waiting for transfers between devices, one_item(): grad_attn_full = lax.all_gather(grad_attn, 'tensor', axis=0, tiled=True)  160 us
    all_gather x2, waiting for transfers between devices, one_item(): gathered = lax.all_gather(token_rows, 'tensor', axis=0, tiled=True)  158 us
    all_gather x2, waiting for transfers between devices, fetch(): lax.all_gather(w_up, 'dp', axis=1, tiled=True)  147 us
  transfers between devices with their start and end apart: 29, of which 29 were waited for; matrix products, arithmetic and copies ran while one was open for 9% of the time, Pallas kernels for 0%

commit v1 on v0

--- a/solution.py
+++ b/solution.py
@@ -1,6 +1,10 @@
+import math
+
 import jax
 import jax.numpy as jnp
 from jax import lax
+from jax.experimental import pallas as pl
+from jax.experimental.pallas import tpu as pltpu
 from jax.sharding import PartitionSpec as P
 
 ALPHA = 48.0**0.5
@@ -338,9 +342,1190 @@
     )
 
 
+def paced(flops):
+    return pl.CostEstimate(flops=int(flops / 2), bytes_accessed=1, transcendentals=0)
+
+
+def attend(projected, cos_table, sin_table, key_pos, query_pos, limit, first, heads, head_dim):
+    length = projected.shape[0]
+    block = min(256, length)
+    score_scale = head_dim ** (-0.5)
+    half_dim = head_dim // 2
+
+    def kernel(limit_ref, proj_ref, cos_ref, sin_ref, kpos_ref, qpos_ref, ctx_ref, qkv_ref, lse_ref):
+        cosine = cos_ref[...]
+        sine = sin_ref[...]
+        query = proj_ref[:, :head_dim].astype(jnp.float32)
+        key = proj_ref[:, head_dim : 2 * head_dim].astype(jnp.float32)
+        query = query * cosine + pltpu.roll(query, half_dim, 1) * sine
+        key = key * cosine + pltpu.roll(key, half_dim, 1) * sine
+        qkv_ref[:, :head_dim] = query.astype(jnp.bfloat16)
+        key_bf = key.astype(jnp.bfloat16)
+        qkv_ref[:, head_dim : 2 * head_dim] = key_bf
+        value_bf = proj_ref[:, 2 * head_dim :].astype(jnp.bfloat16)
+        qkv_ref[:, 2 * head_dim :] = value_bf
+        prefix_length = limit_ref[0]
+        near = kpos_ref[...] < prefix_length
+        for start in range(0, length, block):
+            rows = slice(start, start + block)
+            scores = (
+                lax.dot_general(
+                    key_bf,
+                    qkv_ref[rows, :head_dim],
+                    (((1,), (1,)), ((), ())),
+                    preferred_element_type=jnp.float32,
+                )
+                * score_scale
+            )
+            visible = near | (kpos_ref[...] <= qpos_ref[:, rows])
+            scores = jnp.where(visible, scores, -1e30)
+            highest_score = jnp.max(scores, axis=0, keepdims=True)
+            expo = jnp.exp(scores - highest_score)
+            totals = jnp.sum(expo, axis=0, keepdims=True)
+            weights = (expo / totals).astype(jnp.bfloat16)
+            ctx_ref[rows, :] = lax.dot_general(
+                weights,
+                value_bf,
+                (((0,), (0,)), ((), ())),
+                preferred_element_type=jnp.float32,
+            ).astype(jnp.bfloat16)
+            lse_ref[0, :, rows] = highest_score + jnp.log(totals)
+
+    fixed = lambda h, lim: (0, 0)
+    return pl.pallas_call(
+        kernel,
+        grid_spec=pltpu.PrefetchScalarGridSpec(
+            num_scalar_prefetch=1,
+            grid=(heads,),
+            in_specs=[
+                pl.BlockSpec((length, 3 * head_dim), lambda h, lim: (0, h + first)),
+                pl.BlockSpec((length, head_dim), fixed),
+                pl.BlockSpec((length, head_dim), fixed),
+                pl.BlockSpec((length, 1), fixed),
+                pl.BlockSpec((1, length), fixed),
+            ],
+            out_specs=[
+                pl.BlockSpec((length, head_dim), lambda h, lim: (0, h)),
+                pl.BlockSpec((length, 3 * head_dim), lambda h, lim: (0, h)),
+                pl.BlockSpec((1, 1, length), lambda h, lim: (h, 0, 0)),
+            ],
+        ),
+        out_shape=[
+            jax.ShapeDtypeStruct((length, heads * head_dim), jnp.bfloat16),
+            jax.ShapeDtypeStruct((length, heads * 3 * head_dim), jnp.bfloat16),
+            jax.ShapeDtypeStruct((heads, 1, length), jnp.float32),
+        ],
+        compiler_params=pltpu.CompilerParams(vmem_limit_bytes=48 * 1024 * 1024),
+        cost_estimate=paced(8 * heads * length * length * head_dim),
+        name="attend",
+    )(limit, projected, cos_table, sin_table, key_pos, query_pos)
+
+
+def attend_back(
+    grad_context,
+    qkv,
+    log_totals,
+    cos_table,
+    sin_table,
+    key_pos,
+    query_pos,
+    limit,
+    first,
+    heads,
+    head_dim,
+):
+    length = qkv.shape[0]
+    block = min(256, length)
+    score_scale = head_dim ** (-0.5)
+    half_dim = head_dim // 2
+
+    def kernel(
+        limit_ref,
+        qkv_ref,
+        grad_ref,
+        lse_ref,
+        cos_ref,
+        sin_ref,
+        kpos_ref,
+        qpos_ref,
+        out_ref,
+        bias_ref,
+        query_grad,
+        key_grad,
+        value_grad,
+    ):
+        key_bf = qkv_ref[:, head_dim : 2 * head_dim]
+        value_bf = qkv_ref[:, 2 * head_dim :]
+        prefix_length = limit_ref[0]
+        near = kpos_ref[...] < prefix_length
+        for start in range(0, length, block):
+            rows = slice(start, start + block)
+            query_block = qkv_ref[rows, :head_dim]
+            grad_block = grad_ref[rows, :]
+            scores = (
+                lax.dot_general(
+                    key_bf,
+                    query_block,
+                    (((1,), (1,)), ((), ())),
+                    preferred_element_type=jnp.float32,
+                )
+                * score_scale
+            )
+            visible = near | (kpos_ref[...] <= qpos_ref[:, rows])
+            soft = jnp.exp(jnp.where(visible, scores, -1e30) - lse_ref[0, :, rows])
+            grad_soft = lax.dot_general(
+                value_bf,
+                grad_block,
+                (((1,), (1,)), ((), ())),
+                preferred_element_type=jnp.float32,
+            )
+            inner = jnp.sum(soft * grad_soft, axis=0, keepdims=True)
+            grad_scores = (soft * (grad_soft - inner)).astype(jnp.bfloat16)
+            query_grad[rows, :] = (
+                lax.dot_general(
+                    grad_scores,
+                    key_bf,
+                    (((0,), (0,)), ((), ())),
+                    preferred_element_type=jnp.float32,
+                )
+                * score_scale
+            )
+            key_term = (
+                jnp.dot(grad_scores, query_block, preferred_element_type=jnp.float32) * score_scale
+            )
+            value_term = jnp.dot(
+                soft.astype(jnp.bfloat16), grad_block, preferred_element_type=jnp.float32
+            )
+            if start == 0:
+                key_grad[...] = key_term
+                value_grad[...] = value_term
+            else:
+                key_grad[...] += key_term
+                value_grad[...] += value_term
+        cosine = cos_ref[...]
+        sine = sin_ref[...]
+        turned = query_grad[...]
+        turned = (turned * cosine + pltpu.roll(turned * sine, half_dim, 1)).astype(jnp.bfloat16)
+        out_ref[:, :head_dim] = turned
+        bias_ref[0, :, :head_dim] = jnp.sum(turned.astype(jnp.float32), axis=0, keepdims=True)
+        turned = key_grad[...]
+        turned = (turned * cosine + pltpu.roll(turned * sine, half_dim, 1)).astype(jnp.bfloat16)
+        out_ref[:, head_dim : 2 * head_dim] = turned
+        bias_ref[0, :, head_dim : 2 * head_dim] = jnp.sum(
+            turned.astype(jnp.float32), axis=0, keepdims=True
+        )
+        turned = value_grad[...].astype(jnp.bfloat16)
+        out_ref[:, 2 * head_dim :] = turned
+        bias_ref[0, :, 2 * head_dim :] = jnp.sum(turned.astype(jnp.float32), axis=0, keepdims=True)
+
+    fixed = lambda h, lim: (0, 0)
+    return pl.pallas_call(
+        kernel,
+        grid_spec=pltpu.PrefetchScalarGridSpec(
+            num_scalar_prefetch=1,
+            grid=(heads,),
+            in_specs=[
+                pl.BlockSpec((length, 3 * head_dim), lambda h, lim: (0, h)),
+                pl.BlockSpec((length, head_dim), lambda h, lim: (0, h + first)),
+                pl.BlockSpec((1, 1, length), lambda h, lim: (h, 0, 0)),
+                pl.BlockSpec((length, head_dim), fixed),
+                pl.BlockSpec((length, head_dim), fixed),
+                pl.BlockSpec((length, 1), fixed),
+                pl.BlockSpec((1, length), fixed),
+            ],
+            out_specs=[
+                pl.BlockSpec((length, 3 * head_dim), lambda h, lim: (0, h)),
+                pl.BlockSpec((1, 1, 3 * head_dim), lambda h, lim: (h, 0, 0)),
+            ],
+            scratch_shapes=[pltpu.VMEM((length, head_dim), jnp.float32)] * 3,
+        ),
+        out_shape=[
+            jax.ShapeDtypeStruct((length, heads * 3 * head_dim), jnp.bfloat16),
+            jax.ShapeDtypeStruct((heads, 1, 3 * head_dim), jnp.float32),
+        ],
+        compiler_params=pltpu.CompilerParams(vmem_limit_bytes=48 * 1024 * 1024),
+        cost_estimate=paced(10 * heads * length * length * head_dim),
+        name="attend_back",
+    )(limit, qkv, grad_context, log_totals, cos_table, sin_table, key_pos, query_pos)
+
+
+def transposed_dot(left, right):
+    return lax.dot_general(
+        left, right, (((1,), (1,)), ((), ())), preferred_element_type=jnp.float32
+    )
+
+
+def rows_outer(features, right):
+    return lax.dot_general(
+        features, right, (((0,), (0,)), ((), ())), preferred_element_type=jnp.float32
+    )
+
+
+VMEM_BYTES = 60 * 1024 * 1024
+
+
+def join(parts, count, target, total, offset):
+    width = parts[0][0].shape[1]
+    rows = count
+    while offset % rows or any(first % rows for _, first in parts):
+        rows //= 2
+    steps = count // rows
+
+    def kernel(*refs):
+        for index in range(4):
+
+            @pl.when(pl.program_id(1) == index)
+            def _():
+                refs[-1][...] = refs[index][...]
+
+    def source(first):
+        return pl.BlockSpec((rows, width), lambda i, p: (first // rows + i, 0))
+
+    given = [] if target is None else [target]
+    return pl.pallas_call(
+        kernel,
+        grid=(steps, 4),
+        in_specs=[source(first) for _, first in parts]
+        + [pl.BlockSpec(memory_space=pl.ANY)] * len(given),
+        out_specs=pl.BlockSpec((rows, width), lambda i, p: (offset // rows + p * steps + i, 0)),
+        out_shape=jax.ShapeDtypeStruct((total, width), parts[0][0].dtype),
+        input_output_aliases={4: 0} if given else {},
+        compiler_params=pltpu.CompilerParams(vmem_limit_bytes=VMEM_BYTES),
+        cost_estimate=paced(1000 * count * width),
+        name="join",
+    )(*[array for array, _ in parts], *given)
+
+
+def pack(arrays):
+    total = sum(array.shape[0] for array in arrays)
+
+    def kernel(*refs):
+        row = 0
+        for ref in refs[:-1]:
+            refs[-1][row : row + ref.shape[0]] = ref[...]
+            row += ref.shape[0]
+
+    return pl.pallas_call(
+        kernel,
+        out_shape=jax.ShapeDtypeStruct((total, 128), arrays[0].dtype),
+        cost_estimate=paced(1),
+        name="pack",
+    )(*arrays)
+
+
+def block_of(count, sizes=(512, 256, 128)):
+    for size in sizes:
+        if count % size == 0:
+            return size
+    return count
+
+
+class Weight:
+    def __init__(self, arrays, start, count):
+        self.arrays = arrays
+        self.start = start
+        self.count = count
+        self.part = arrays[0].shape[1]
+        self.width = 4 * self.part
+
+    def row_specs(self, block):
+        return [pl.BlockSpec((block, self.part), lambda j: (self.start // block + j, 0))] * 4
+
+
+def project_block(rows_ref, weight_refs):
+    total = None
+    for index, ref in enumerate(weight_refs):
+        part = ref.shape[1]
+        product = transposed_dot(rows_ref[:, index * part : (index + 1) * part], ref[...])
+        total = product if total is None else total + product
+    return total
+
+
+def project(rows, weight, bias, kind):
+    count, width = rows.shape
+    features = weight.count
+    block = block_of(features)
+
+    def kernel(rows_ref, w0, w1, w2, w3, bias_ref, out_ref):
+        result = project_block(rows_ref, (w0, w1, w2, w3))
+        out_ref[...] = (result + bias_ref[...]).astype(kind)
+
+    return pl.pallas_call(
+        kernel,
+        grid=(features // block,),
+        in_specs=[pl.BlockSpec((count, width), lambda j: (0, 0))]
+        + weight.row_specs(block)
+        + [pl.BlockSpec((1, block), lambda j: (0, j))],
+        out_specs=pl.BlockSpec((count, block), lambda j: (0, j)),
+        out_shape=jax.ShapeDtypeStruct((count, features), kind),
+        compiler_params=pltpu.CompilerParams(vmem_limit_bytes=VMEM_BYTES),
+        cost_estimate=paced(2 * count * width * features),
+        name="project",
+    )(rows, *weight.arrays, bias)
+
+
+def ff_forward(rows, gate_weight, upper_weight, bias_gate, bias_upper):
+    count, width = rows.shape
+    features = gate_weight.count
+    block = block_of(features)
+
+    def kernel(rows_ref, *refs):
+        bg_ref, bu_ref, gate_ref, upper_ref, hid_ref = refs[8:]
+        gate = project_block(rows_ref, refs[:4]) + bg_ref[...]
+        upper = project_block(rows_ref, refs[4:8]) + bu_ref[...]
+        gate_ref[...] = gate.astype(jnp.bfloat16)
+        upper_ref[...] = upper.astype(jnp.bfloat16)
+        hid_ref[...] = (jax.nn.gelu(gate) * upper).astype(jnp.bfloat16)
+
+    out = jax.ShapeDtypeStruct((count, features), jnp.bfloat16)
+    return pl.pallas_call(
+        kernel,
+        grid=(features // block,),
+        in_specs=[pl.BlockSpec((count, width), lambda j: (0, 0))]
+        + gate_weight.row_specs(block)
+        + upper_weight.row_specs(block)
+        + [pl.BlockSpec((1, block), lambda j: (0, j))] * 2,
+        out_specs=[pl.BlockSpec((count, block), lambda j: (0, j))] * 3,
+        out_shape=[out, out, out],
+        compiler_params=pltpu.CompilerParams(vmem_limit_bytes=VMEM_BYTES),
+        cost_estimate=paced(4 * count * width * features),
+        name="ff_forward",
+    )(rows, *gate_weight.arrays, *upper_weight.arrays, bias_gate, bias_upper)
+
+
+def ff_back(rows, down_weight, gate, upper):
+    count, width = rows.shape
+    features = down_weight.count
+    block = block_of(features)
+    factor = (2.0 / math.pi) ** 0.5
+
+    def kernel(rows_ref, w0, w1, w2, w3, gate_ref, upper_ref, gg_ref, gu_ref, sg_ref, su_ref):
+        grad = project_block(rows_ref, (w0, w1, w2, w3))
+        value = gate_ref[...].astype(jnp.float32)
+        square = value * value
+        bend = jnp.tanh(factor * value * (1.0 + 0.044715 * square))
+        lift = 0.5 * (1.0 + bend)
+        slope = lift + 0.5 * value * (1.0 - bend * bend) * (
+            factor * (1.0 + 3.0 * 0.044715 * square)
+        )
+        grad_gate = (grad * upper_ref[...].astype(jnp.float32) * slope).astype(jnp.bfloat16)
+        grad_upper = (grad * (value * lift)).astype(jnp.bfloat16)
+        gg_ref[...] = grad_gate
+        gu_ref[...] = grad_upper
+        sg_ref[...] = jnp.sum(grad_gate.astype(jnp.float32), axis=0, keepdims=True)
+        su_ref[...] = jnp.sum(grad_upper.astype(jnp.float32), axis=0, keepdims=True)
+
+    out = jax.ShapeDtypeStruct((count, features), jnp.bfloat16)
+    row = jax.ShapeDtypeStruct((1, features), jnp.float32)
+    return pl.pallas_call(
+        kernel,
+        grid=(features // block,),
+        in_specs=[pl.BlockSpec((count, width), lambda j: (0, 0))]
+        + down_weight.row_specs(block)
+        + [pl.BlockSpec((count, block), lambda j: (0, j))] * 2,
+        out_specs=[pl.BlockSpec((count, block), lambda j: (0, j))] * 2
+        + [pl.BlockSpec((1, block), lambda j: (0, j))] * 2,
+        out_shape=[out, out, row, row],
+        compiler_params=pltpu.CompilerParams(vmem_limit_bytes=VMEM_BYTES),
+        cost_estimate=paced(3 * count * width * features),
+        name="ff_back",
+    )(rows, *down_weight.arrays, gate, upper)
+
+
+def expand(*pairs):
+    count = pairs[0][0].shape[0]
+    width = pairs[0][1].width
+    part = width // 4
+    own = count // 2
+    terms = len(pairs)
+    cuts = 2 if sum(weight.count for _, weight in pairs) > 4000 else 1
+    block = part // cuts
+
+    def kernel(*refs):
+        own_ref, other_ref = refs[5 * terms :]
+        for which in range(4):
+
+            @pl.when(pl.program_id(0) // cuts == which)
+            def _():
+                total = None
+                for term in range(terms):
+                    product = jnp.dot(
+                        refs[5 * term][...],
+                        refs[5 * term + 1 + which][...],
+                        preferred_element_type=jnp.float32,
+                    )
+                    total = product if total is None else total + product
+                own_ref[...] = total[:own]
+                other_ref[...] = total[own:].astype(jnp.bfloat16)
+
+    def column(weight, which):
+        return pl.BlockSpec(
+            (weight.count, block),
+            lambda j: (weight.start // weight.count, jnp.clip(j - cuts * which, 0, cuts - 1)),
+        )
+
+    specs = []
+    operands = []
+    for features, weight in pairs:
+        specs.append(pl.BlockSpec((count, weight.count), lambda j: (0, 0)))
+        specs += [column(weight, which) for which in range(4)]
+        operands += [features, *weight.arrays]
+    return pl.pallas_call(
+        kernel,
+        grid=(4 * cuts,),
+        in_specs=specs,
+        out_specs=[pl.BlockSpec((own, block), lambda j: (0, j))] * 2,
+        out_shape=[
+            jax.ShapeDtypeStruct((own, width), jnp.float32),
+            jax.ShapeDtypeStruct((own, width), jnp.bfloat16),
+        ],
+        compiler_params=pltpu.CompilerParams(vmem_limit_bytes=VMEM_BYTES),
+        cost_estimate=paced(2 * count * width * sum(weight.count for _, weight in pairs)),
+        name="expand",
+    )(*operands)
+
+
+def outer(features, rights, start, columns, parts, added=(), pieces=(), steps=2):
+    chunks = len(features)
+    count = rights[0][2]
+    total = features[0][0].shape[1]
+    block = total // steps
+    rows = total // parts
+
+    def kernel(*refs):
+        result = None
+        for chunk in range(chunks):
+            product = rows_outer(refs[chunk][...], refs[chunks + chunk][...])
+            result = product if result is None else result + product
+        first = 2 * chunks
+        for ref in refs[first : first + len(added)]:
+            result = result + ref[...].astype(jnp.float32)
+        first += len(added)
+        outs = refs[first + len(pieces) :]
+        if parts == 1:
+            outs[0][...] = result.astype(jnp.bfloat16)
+            return
+        each = parts // steps
+        for half in range(steps):
+
+            @pl.when(pl.program_id(0) == half)
+            def _():
+                whole = result
+                if pieces:
+                    whole = whole + refs[first + half][...].astype(jnp.float32)
+                whole = whole.astype(jnp.bfloat16)
+                for index in range(each):
+                    outs[half * each + index][...] = whole[index * rows : (index + 1) * rows]
+
+    def at(row, column):
+        return lambda j: (row, column)
+
+    def across(row):
+        return lambda j: (row, j)
+
+    def along(column):
+        return lambda j: (j, column)
+
+    if parts == 1:
+        out_specs = [pl.BlockSpec((block, columns), along(0))]
+    else:
+        out_specs = [pl.BlockSpec((rows, columns), at(0, 0))] * parts
+    return pl.pallas_call(
+        kernel,
+        grid=(steps,),
+        in_specs=[pl.BlockSpec((count, block), across(row)) for _, row, _ in features]
+        + [pl.BlockSpec((count, columns), at(row, start // columns)) for _, row, _ in rights]
+        + [pl.BlockSpec((block, columns), along(column // columns)) for _, column in added]
+        + [pl.BlockSpec((block, columns), at(0, 0))] * len(pieces),
+        out_specs=out_specs,
+        out_shape=[jax.ShapeDtypeStruct((rows, columns), jnp.bfloat16)] * parts,
+        compiler_params=pltpu.CompilerParams(vmem_limit_bytes=VMEM_BYTES),
+        cost_estimate=paced(3 * chunks * count * total * columns),
+        name="outer",
+    )(
+        *[array for array, _, _ in features],
+        *[array for array, _, _ in rights],
+        *[array for array, _ in added],
+        *pieces,
+    )
+
+
+def after(values, *earlier):
+    return lax.optimization_barrier((values,) + earlier)[0]
+
+
+CHUNKS = 2
+
+
+def pair_shards(
+    tokens,
+    cotangent,
+    loss_mask,
+    prefix,
+    counts,
+    w_qkv,
+    b_qkv,
+    w_dense,
+    b_dense,
+    ln1_gain,
+    ln1_bias,
+    w_up,
+    b_up,
+    w_down,
+    b_down,
+    ln2_gain,
+    ln2_bias,
+):
+    slots, home_rows, width = tokens.shape[1:]
+    n_tensor = lax.axis_size("tensor")
+    length = home_rows * n_tensor
+    own_count = length // 2
+    head_dim = w_qkv.shape[2] // 3
+    shard_heads = w_qkv.shape[1]
+    heads = 2 * shard_heads
+    shard_hidden = w_up.shape[2]
+    block_width = w_qkv.shape[0]
+    side = lax.axis_index("obj")
+    place = lax.axis_index("dp")
+    layer = lax.axis_index("tensor")
+    item_slot = layer >> 1
+
+    def along(axis, step, depth=2):
+        moves = [(i, i ^ step) for i in range(lax.axis_size(axis))]
+        sent = []
+
+        def move(values):
+            if len(sent) >= depth:
+                values = after(values, sent[-depth])
+            sent.append(lax.ppermute(values, axis, moves))
+            return sent[-1]
+
+        return move
+
+    over_x = along("obj", 1)
+    over_y = along("dp", 2)
+    over_core = along("dp", 1)
+    swap = along("tensor", 1, 1)
+    over_far = along("tensor", 2, 1)
+    back_x = along("obj", 1, 2)
+    back_y = along("dp", 2, 2)
+    back_far = along("tensor", 2, 1)
+
+    def to_local(values):
+        parts = [
+            lax.dynamic_slice_in_dim(values, (place ^ k) * block_width, block_width, -1)
+            for k in (0, 2, 1, 3)
+        ]
+        return jnp.concatenate(parts, axis=-1)
+
+    def from_local(values):
+        parts = []
+        for g in range(4):
+            k = place ^ g
+            at = ((k & 1) << 1) | (k >> 1)
+            parts.append(lax.dynamic_slice_in_dim(values, at * block_width, block_width, -1))
+        return jnp.concatenate(parts, axis=-1)
+
+    def away(values):
+        stays = lax.dynamic_index_in_dim(values, item_slot, 0, keepdims=False)
+        leaves = lax.dynamic_index_in_dim(values, 1 - item_slot, 0, keepdims=False)
+        return [stays, over_far(leaves)]
+
+    def home(values):
+        stays, leaves = values
+        came = back_far(leaves)
+        first = jnp.where(item_slot == 0, stays, came)
+        second = jnp.where(item_slot == 0, came, stays)
+        return from_local(jnp.stack([first, second])), came
+
+    def side_first(values, axis=0):
+        count = values.shape[axis] // 2
+        return (
+            lax.dynamic_slice_in_dim(values, side * count, count, axis),
+            lax.dynamic_slice_in_dim(values, (1 - side) * count, count, axis),
+        )
+
+    def sides(mine, other):
+        return jnp.concatenate(
+            [jnp.where(side == 0, mine, other), jnp.where(side == 0, other, mine)], axis=0
+        )
+
+    latest = []
+
+    def turn(work, first, *rest, wait=()):
+        result = work(after(first, *latest, *wait), *rest)
+        latest[:] = [result[0] if isinstance(result, (tuple, list)) else result]
+        return result
+
+    narrow = jnp.bfloat16
+    wide = jnp.float32
+
+    class Gathering:
+        def __init__(self, *shards):
+            halves = [side_first(shard) for shard in shards]
+            self.mine = jnp.concatenate([half[0] for half in halves], axis=0)
+            self.rest = jnp.concatenate([half[1] for half in halves], axis=0)
+            self.counts = [half[0].shape[0] for half in halves]
+
+        def to_far(self):
+            self.far = over_far(self.mine)
+
+        def far_to_y(self):
+            self.far_y = over_y(self.far)
+
+        def far_to_x(self):
+            self.other_far = over_x(self.far)
+
+        def both_to_x(self):
+            self.other_far_y = over_x(self.far_y)
+
+        def joined(self, parts, wait):
+            total = 4 * sum(self.counts)
+            target = None
+            first = 0
+            for count in self.counts:
+                rest = [(array, start + first) for array, start in parts[1:]]
+                target = turn(
+                    lambda array: join(
+                        [(array, parts[0][1] + first)] + rest, count, target, total, 4 * first
+                    ),
+                    parts[0][0],
+                    wait=wait,
+                )
+                first += count
+            return target
+
+        def blocks(self, wait=()):
+            near = self.joined(
+                [(self.mine, 0), (self.rest, 0), (self.far, 0), (self.other_far, 0)], wait
+            )
+            next_y = self.joined(
+                [self.near_y, self.other_y, (self.far_y, 0), (self.other_far_y, 0)], ()
+            )
+            self.near = near, over_core(near)
+            self.next = next_y, over_core(next_y)
+
+        def weights(self):
+            arrays = (self.near[0], self.next[0], self.near[1], self.next[1])
+            first = 0
+            result = []
+            for count in self.counts:
+                result.append(Weight(arrays, 4 * first, 4 * count))
+                first += count
+            return result
+
+    class Reduction:
+        def __init__(self, features, rights):
+            self.features = features
+            self.rights = rights
+
+        def part(self, *given, wait=(), **more):
+            array, row, count = self.features[0]
+            return turn(
+                lambda first: outer(
+                    [(first, row, count)] + self.features[1:], self.rights, *given, **more
+                ),
+                array,
+                wait=wait,
+            )
+
+        def to_core(self, wait=()):
+            (sent,) = self.part(2 * block_width, 2 * block_width, 1, wait=wait)
+            self.came = over_core(sent)
+
+        def to_y(self, wait=()):
+            sent = self.part(
+                block_width, block_width, 2, added=[(self.came, block_width)], wait=wait
+            )
+            far = back_y(sent[1])
+            self.came_y = [back_y(sent[0]), far]
+
+        def to_x(self, wait=()):
+            near, near_sent, far, far_sent = self.part(
+                0, block_width, 4, added=[(self.came, 0)], pieces=self.came_y, wait=wait
+            )
+            self.far = (far, back_x(far_sent))
+            self.near = (near, back_x(near_sent))
+
+        def to_x_first(self, wait=()):
+            near, near_sent, far, far_sent = self.part(
+                0, 2 * block_width, 4, added=[(self.came, 0)], wait=wait
+            )
+            self.wide_far = (far, back_x(far_sent))
+            self.wide_near = (near, back_x(near_sent))
+
+        def to_y_next(self):
+            def onward(pair):
+                summed = add(*pair)
+                return summed[:, :block_width], back_y(summed[:, block_width:])
+
+            self.far = onward(self.wide_far)
+            self.near = onward(self.wide_near)
+
+        def to_far(self):
+            self.came_far = back_far(add(*self.far))
+
+        def finish(self):
+            self.mine = add(*self.near, self.came_far)
+            return sides(self.mine, back_x(self.mine)).astype(wide)
+
+    class HalfReduction:
+        def __init__(self, features, rights):
+            self.features = features
+            self.rights = rights
+
+        def part(self, *given, wait=(), **more):
+            array, row, count = self.features[0]
+            return turn(
+                lambda first: outer(
+                    [(first, row, count)] + self.features[1:],
+                    self.rights,
+                    *given,
+                    steps=1,
+                    **more,
+                ),
+                array,
+                wait=wait,
+            )
+
+        def to_core(self, wait=()):
+            (sent,) = self.part(2 * block_width, 2 * block_width, 1, wait=wait)
+            self.came = over_core(sent)
+
+        def to_y(self, wait=()):
+            (sent,) = self.part(
+                block_width, block_width, 1, added=[(self.came, block_width)], wait=wait
+            )
+            self.came_y = back_y(sent)
+
+        def to_x(self, wait=()):
+            kept, sent = self.part(
+                0, block_width, 2, added=[(self.came, 0), (self.came_y, 0)], wait=wait
+            )
+            self.pair = (kept, back_x(sent))
+
+    def add(*values):
+        total = values[0].astype(wide)
+        for value in values[1:]:
+            total = total + value.astype(wide)
+        return total.astype(narrow)
+
+    count_float = counts.astype(jnp.float32)
+    share = jnp.where(side == 0, count_float[0], count_float[1]) / (
+        count_float[0] + count_float[1]
+    )
+    limit = jnp.where(side == 0, length, prefix[item_slot]).astype(jnp.int32).reshape(1)
+
+    shard_qkv = w_qkv.reshape(block_width, shard_heads * 3 * head_dim).T
+    shard_dense = w_dense.reshape(shard_heads * head_dim, block_width)
+    up_rows = jnp.swapaxes(w_up, 1, 2)
+
+    near_bias = jnp.concatenate(
+        side_first(b_qkv.reshape(-1))
+        + side_first(b_up[0])
+        + side_first(b_up[1])
+    )
+    far_bias = lax.ppermute(near_bias, "tensor", [(i, i ^ 2) for i in range(n_tensor)])
+    n_qkv = b_qkv.size
+
+    def bias_row(start, count):
+        parts = [near_bias[start : start + count], far_bias[start : start + count]]
+        return jnp.concatenate(parts).astype(jnp.float32)[None]
+
+    bias_qkv = bias_row(0, n_qkv)
+    bias_gate = bias_row(n_qkv, shard_hidden)
+    bias_upper = bias_row(n_qkv + shard_hidden, shard_hidden)
+
+    def row_vector(values):
+        return to_local(values.astype(jnp.float32)[None])
+
+    bias_dense = row_vector(b_dense)
+    gain_one = row_vector(ln1_gain)
+    shift_one = row_vector(ln1_bias)
+    bias_down = row_vector(b_down)
+    gain_two = row_vector(ln2_gain)
+    shift_two = row_vector(ln2_bias)
+
+    share_rows = own_count // CHUNKS
+
+    def positions(owner):
+        return owner * home_rows + jnp.arange(home_rows, dtype=jnp.int32)
+
+    where_rows = jnp.concatenate([positions(layer ^ k) for k in (0, 1, 2, 3)])
+    key_pos = where_rows[:, None]
+    query_pos = where_rows[None, :]
+    half_dim = head_dim // 2
+    frequency = 10000.0 ** (-2.0 * jnp.arange(half_dim, dtype=jnp.float32) / head_dim)
+    angles = where_rows.astype(jnp.float32)[:, None] * frequency[None, :]
+    cos_table = jnp.cos(angles)
+    cos_table = jnp.concatenate([cos_table, cos_table], axis=1)
+    sin_table = jnp.sin(angles)
+    sin_table = jnp.concatenate([-sin_table, sin_table], axis=1)
+
+    masked = cotangent[0] * loss_mask[0].astype(jnp.bfloat16)[..., None]
+    early = Gathering(shard_qkv, shard_dense)
+    middle = Gathering(up_rows[0])
+    third = Gathering(up_rows[1])
+    late = Gathering(w_down)
+
+    early.to_far()
+    early_y = over_y(early.mine)
+    leaving = to_local(tokens[0])
+    stays = lax.dynamic_index_in_dim(leaving, item_slot, 0, keepdims=False)
+    came_tokens = [swap(stays)]
+    others = (middle, third, late)
+    others_y = over_y(jnp.concatenate([part.mine for part in others], axis=0))
+    early_other_y = over_x(early_y)
+    early.near_y = early_y, 0
+    early.other_y = early_other_y, 0
+    early.far = after(early.far, came_tokens[0], early_other_y)
+    own_tokens = away(leaving)
+    early.far_to_y()
+    early.far_to_x()
+    middle.to_far()
+    early.both_to_x()
+    early.blocks(wait=(own_tokens[1],))
+    came_tokens.append(swap(own_tokens[1]))
+    others_other_y = over_x(others_y)
+    first_row = 0
+    for part in others:
+        part.near_y = others_y, first_row
+        part.other_y = others_other_y, first_row
+        first_row += part.counts[0]
+    third.to_far()
+    full_qkv, full_dense = early.weights()
+    token_rows = jnp.concatenate(
+        [part for i in range(CHUNKS) for part in (own_tokens[i], came_tokens[i])], axis=0
+    )
+    projected = turn(project, token_rows, full_qkv, bias_qkv, jnp.float32)
+
+    def attend_heads(first, wait):
+        return turn(
+            attend,
+            projected,
+            cos_table,
+            sin_table,
+            key_pos,
+            query_pos,
+            limit,
+            first,
+            shard_heads,
+            head_dim,
+            wait=wait,
+        )
+
+    middle.far_to_y()
+    middle.far_to_x()
+    near_heads = attend_heads(0, (others_other_y,))
+    late.to_far()
+    far_heads = attend_heads(shard_heads, (middle.far_y, middle.other_far))
+    middle.both_to_x()
+    third.far_to_y()
+    third.far_to_x()
+
+    step = 2 * share_rows
+    half_heads = shard_heads * head_dim
+    dense_near = Weight(full_dense.arrays, full_dense.start, half_heads)
+    dense_far = Weight(full_dense.arrays, full_dense.start + half_heads, half_heads)
+    states = [dict() for _ in range(CHUNKS)]
+
+    def normalize(values):
+        centred = values - jnp.mean(values, axis=-1, keepdims=True)
+        scale = lax.rsqrt(jnp.mean(centred * centred, axis=-1, keepdims=True) + epsilon)
+        return centred * scale, scale
+
+    def normalize_back(grad, gain, normal, scale):
+        turned = grad * gain
+        return scale * (
+            turned
+            - jnp.mean(turned, axis=-1, keepdims=True)
+            - normal * jnp.mean(turned * normal, axis=-1, keepdims=True)
+        )
+
+    for i, state in enumerate(states):
+        rows = slice(i * step, (i + 1) * step)
+        own, other = turn(
+            lambda n, f: expand((n, dense_near), (f, dense_far)),
+            near_heads[0][rows],
+            far_heads[0][rows],
+            wait=(middle.other_far_y, third.far) if i == 0 else (),
+        )
+        state["dense"] = own, swap(other)
+    third.both_to_x()
+    middle.blocks(wait=(third.far_y, third.other_far, late.far))
+    late.far_to_y()
+    late.far_to_x()
+    late.both_to_x()
+    own_cotangent = away(to_local(masked))
+    for i, state in enumerate(states):
+        own, came = state["dense"]
+        attn = own + came.astype(wide) + bias_dense
+        first = ALPHA * own_tokens[i].astype(wide) + attn
+        normal, scale = normalize(first)
+        norm_one = normal * gain_one + shift_one
+        norm_bf = norm_one.astype(narrow)
+        state["one"] = normal, scale, norm_one
+        state["norm_bf"] = norm_bf
+        state["norm_rows"] = jnp.concatenate([norm_bf, swap(norm_bf)], axis=0)
+    third.blocks(wait=[s["norm_bf"] for s in states] + [late.far_y, late.other_far])
+    (full_gate,) = middle.weights()
+    (full_upper,) = third.weights()
+    for i, state in enumerate(states):
+        state["ff"] = turn(
+            ff_forward,
+            state["norm_rows"],
+            full_gate,
+            full_upper,
+            bias_gate,
+            bias_upper,
+            wait=(own_cotangent[1],) if i == 1 else (),
+        )
+    late.blocks()
+    (full_down,) = late.weights()
+    for state in states:
+        own, other = turn(lambda r: expand((r, full_down)), state["ff"][2])
+        state["down"] = own, swap(other)
+    for i, state in enumerate(states):
+        own, came = state["down"]
+        mlp = own + came.astype(wide) + bias_down
+        normal, scale = normalize(ALPHA * state["one"][2] + mlp)
+        state["out"] = (normal * gain_two + shift_two).astype(narrow)
+        grad_out = own_cotangent[i].astype(wide) * share
+        grad_second = normalize_back(grad_out, gain_two, normal, scale)
+        grad_mlp = grad_second.astype(narrow)
+        state["second"] = grad_second
+        state["came_mlp"] = swap(grad_mlp)
+        state["mlp_rows"] = jnp.concatenate([grad_mlp, state["came_mlp"]], axis=0)
+        state["vectors_two"] = (
+            jnp.sum(grad_mlp.astype(wide), axis=0),
+            jnp.sum(grad_out * normal, axis=0),
+            jnp.sum(grad_out, axis=0),
+        )
+
+    layer_out, sent_out = home([s["out"] for s in states])
+
+    def back_ff(state, wait=()):
+        state["back"] = turn(
+            ff_back, state["mlp_rows"], full_down, state["ff"][0], state["ff"][1], wait=wait
+        )
+
+    def back_up(state, wait=()):
+        own, other = turn(
+            lambda g, u: expand((g, full_gate), (u, full_upper)),
+            state["back"][0],
+            state["back"][1],
+            wait=wait,
+        )
+        state["norm_grad"] = own, swap(other)
+
+    def back_one(state):
+        own, came = state["norm_grad"]
+        normal, scale, _ = state["one"]
+        grad_norm = ALPHA * state["second"] + own + came.astype(wide)
+        grad_first = normalize_back(grad_norm, gain_one, normal, scale)
+        grad_attn = grad_first.astype(narrow)
+        state["first"] = grad_first
+        state["grad_attn"] = grad_attn
+        state["came_attn"] = swap(grad_attn)
+        state["attn_rows"] = jnp.concatenate([grad_attn, state["came_attn"]], axis=0)
+        state["vectors_one"] = (
+            jnp.sum(grad_attn.astype(wide), axis=0),
+            jnp.sum(grad_norm * normal, axis=0),
+            jnp.sum(grad_norm, axis=0),
+        )
+
+    def chunks_of(pick):
+        return [(pick(state), 0, step) for state in states]
+
+    back_ff(states[0])
+    back_up(states[0], wait=(states[1]["came_mlp"],))
+    down = Reduction(chunks_of(lambda s: s["ff"][2]), chunks_of(lambda s: s["mlp_rows"]))
+    down.to_core()
+    back_ff(states[1])
+    down.to_y(wait=(states[0]["norm_grad"][1],))
+    back_one(states[0])
+    back_up(states[1], wait=(states[0]["grad_attn"],))
+    norm_all = chunks_of(lambda s: s["norm_rows"])
+    gate = Reduction(chunks_of(lambda s: s["back"][0]), norm_all)
+    upper = Reduction(chunks_of(lambda s: s["back"][1]), norm_all)
+    gate.to_core(wait=(states[0]["came_attn"],))
+    upper.to_core(wait=(down.came_y[1],))
+    back_one(states[1])
+    zero_row = jnp.zeros((1, heads * head_dim), wide)
+
+    def back_dense(state, wait=()):
+        return turn(project, state["attn_rows"], full_dense, zero_row, narrow, wait=wait)
+
+    context_grads = [back_dense(states[0], wait=(states[1]["norm_grad"][1],))]
+    upper.to_x_first(wait=(states[1]["grad_attn"],))
+    gate.to_y(wait=(down.came_y[0],))
+    context_grads.append(back_dense(states[1]))
+    dense_grads = [
+        HalfReduction(
+            [(part[0], i, step) for i in range(CHUNKS)], chunks_of(lambda s: s["attn_rows"])
+        )
+        for part in (near_heads, far_heads)
+    ]
+    dense_grads[1].to_core(wait=(sent_out,))
+    dense_grads[0].to_core()
+    context_grad = jnp.concatenate(context_grads, axis=0)
+
+    def back_heads(saved, first, wait=()):
+        return turn(
+            attend_back,
+            context_grad,
+            saved[1],
+            saved[2],
+            cos_table,
+            sin_table,
+            key_pos,
+            query_pos,
+            limit,
+            first,
+            shard_heads,
+            head_dim,
+            wait=wait,
+        )
+
+    def both_chunks(array):
+        return [(array, i, step) for i in range(CHUNKS)]
+
+    grad_far, bias_far = back_heads(far_heads, shard_heads)
+    qkv_far = HalfReduction(both_chunks(grad_far), both_chunks(token_rows))
+    qkv_far.to_core(wait=(upper.wide_far[1], gate.came_y[1]))
+    down.to_x()
+    grad_near, bias_near = back_heads(near_heads, 0, wait=(upper.wide_near[1],))
+    upper.to_y_next()
+    qkv_near = HalfReduction(both_chunks(grad_near), both_chunks(token_rows))
+
+    grad_bias_qkv = jnp.concatenate([bias_near, bias_far], axis=0)
+    grad_bias_gate = sum(s["back"][2] for s in states)
+    grad_bias_upper = sum(s["back"][3] for s in states)
+
+    def spread(values):
+        cut = values.reshape(2, 2, -1)
+        whole = jnp.zeros((n_tensor, values.size // 2), jnp.float32)
+        whole = lax.dynamic_update_index_in_dim(whole, sides(cut[0, 0], cut[0, 1]), layer, 0)
+        whole = lax.dynamic_update_index_in_dim(whole, sides(cut[1, 0], cut[1, 1]), layer ^ 2, 0)
+        return whole.reshape(-1)
+
+    stacked = jnp.stack(
+        [sum(s[name][i] for s in states) for name in ("vectors_one", "vectors_two") for i in range(3)]
+    ).reshape(6, 4, block_width)
+    targets = place ^ jnp.arange(4, dtype=jnp.int32)
+    targets = (((targets & 1) << 1) | (targets >> 1))[None, :, None]
+    ordered = jnp.zeros_like(stacked)
+    for position in range(4):
+        ordered = jnp.where(targets == position, stacked[:, position : position + 1], ordered)
+    def columns(values):
+        rows = values.reshape(-1, 128)
+        return jnp.pad(rows, ((0, -rows.shape[0] % 8), (0, 0)))
+
+    small = [
+        columns(ordered),
+        columns(spread(grad_bias_qkv)),
+        columns(spread(grad_bias_gate)),
+        columns(spread(grad_bias_upper)),
+    ]
+    packed = pack(small)
+    sums = [packed]
+    for axis, hop in (("obj", 1), ("dp", 1), ("dp", 2), ("tensor", 1), ("tensor", 2)):
+        moves = [(i, i ^ hop) for i in range(lax.axis_size(axis))]
+        sums.append(sums[-1] + lax.ppermute(sums[-1], axis, moves))
+
+    gate.to_x(wait=(gate.came_y[0],))
+    down.to_far()
+    qkv_near.to_core(wait=(down.far[1],))
+    qkv_far.to_y(wait=(upper.far[1], sums[1]))
+    half_count = full_qkv.count // 2
+    weight_near = Weight(full_qkv.arrays, 0, half_count)
+    weight_far = Weight(full_qkv.arrays, half_count, half_count)
+
+    def back_qkv(i, wait=()):
+        rows = slice(i * step, (i + 1) * step)
+        own, other = turn(
+            lambda n, f: expand((n, weight_near), (f, weight_far)),
+            grad_near[rows],
+            grad_far[rows],
+            wait=wait,
+        )
+        states[i]["source"] = own, swap(other)
+
+    back_qkv(0, wait=(upper.near[1], sums[2]))
+    qkv_near.to_y(wait=(down.near[1], sums[3]))
+    sum_down = down.finish()
+    back_qkv(1, wait=(states[0]["source"][1], gate.far[1], sums[4]))
+    gate.to_far()
+    qkv_far.to_x(wait=(gate.near[1], sums[5]))
+    dense_grads[1].to_y()
+    dense_grads[0].to_y()
+    came_qkv = back_far(add(*qkv_far.pair))
+    qkv_near.to_x(wait=(states[1]["source"][1],))
+    dense_grads[1].to_x()
+    dense_grads[0].to_x()
+    grad_inputs, _ = home(
+        [
+            (s["source"][0] + s["source"][1].astype(wide) + ALPHA * s["first"]).astype(narrow)
+            for s in states
+        ]
+    )
+    grad_inputs = grad_inputs.astype(wide)
+    sum_gate = gate.finish()
+    upper.to_far()
+    mine_qkv = add(*qkv_near.pair, came_qkv)
+    sum_qkv = sides(mine_qkv, back_x(mine_qkv)).astype(wide)
+    came_dense = back_far(add(*dense_grads[1].pair))
+    sum_upper = upper.finish()
+    mine_dense = add(*dense_grads[0].pair, came_dense)
+    sum_dense = sides(mine_dense, back_x(mine_dense)).astype(wide)
+    norm_total = sums[-1][: small[0].shape[0]].reshape(6, width)
+    flat_totals = []
+    row = small[0].shape[0]
+    for part, count in zip(small[1:], (n_qkv, shard_hidden, shard_hidden)):
+        rows = sums[-1][row : row + count * n_tensor // 128]
+        flat_totals.append(rows.reshape(-1))
+        row += part.shape[0]
+    total_qkv, total_gate, total_upper = flat_totals
+
+    def own_shard(total, count):
+        return lax.dynamic_slice_in_dim(total, layer * count, count)
+
+    bias_total_qkv = own_shard(total_qkv, n_qkv).reshape(b_qkv.shape)
+    bias_total_up = jnp.stack(
+        [own_shard(total_gate, shard_hidden), own_shard(total_upper, shard_hidden)]
+    )
+
+    grad_w_qkv = sum_qkv.T.reshape(w_qkv.shape)
+    grad_w_dense = sum_dense.reshape(w_dense.shape)
+    grad_w_up = jnp.stack([sum_gate.T, sum_upper.T])
+    grad_w_down = sum_down
+
+    return (
+        layer_out[None],
+        grad_inputs[None],
+        grad_w_qkv,
+        bias_total_qkv,
+        grad_w_dense,
+        norm_total[0],
+        norm_total[1],
+        norm_total[2],
+        grad_w_up,
+        bias_total_up,
+        grad_w_down,
+        norm_total[3],
+        norm_total[4],
+        norm_total[5],
+    )
+
+
+def pair_plan_fits(mesh):
+    return mesh.shape["obj"] == 2 and mesh.shape["dp"] == 4 and mesh.shape["tensor"] == 4
+
+
 def solution(mesh):
+    body = pair_shards if pair_plan_fits(mesh) else shards
     return jax.shard_map(
-        shards,
+        body,
         mesh=mesh,
         in_specs=(
             P("obj", "dp", "tensor", None),

time: 2830 us -> 1230 us (0.43)
  waiting for transfers between devices: 2200 us -> 476 us
  Pallas kernels: 0 us -> 467 us
  matrix products: 350 us -> 0 us
  starting transfers between devices: 2.19 us -> 95 us
  blocking collectives: 65.2 us -> 0 us
    reduce_scatter x11 -> x0, waiting for transfers between devices: 1090 us -> none  [the longest x2 288 us: one_item(): lax.psum_scatter(jnp.einsum('lhd,hde->le', piece, dense_full, preferred_e...]
    all_gather x16 -> x0, waiting for transfers between devices: 926 us -> none  [the longest x2 166 us: one_item(): lax.all_gather(first_norm.astype(jnp.bfloat16), 'tensor', axis=0, tiled=T...]
    ppermute x0 -> x91, waiting for transfers between devices: none -> 476 us  [the longest x85 468 us: move(): sent.append(lax.ppermute(values, axis, moves))]
    pallas_call x0 -> x50, Pallas kernels: none -> 467 us  [the longest x20 141 us: outer(): pl.pallas_call(kernel, grid=(steps,), in_specs=[pl.BlockSpec((count, bloc...]
    dot_general x48 -> x0, matrix products: 350 us -> none  [the longest x2 44.5 us: one_item(): jnp.einsum('ld,klf->kdf', norm_full, grad_gate_up, preferred_element_type...]
    psum x1 -> x0, waiting for transfers between devices: 96.1 us -> none  [shards(): lax.psum(sharded[0].astype(jnp.bfloat16), 'obj').astype(jnp.float32)]
    ppermute x0 -> x91, starting transfers between devices: none -> 95 us  [the longest x85 86 us: move(): sent.append(lax.ppermute(values, axis, moves))]
    unnamed x6 -> x0, waiting for transfers between devices: 86.5 us -> none
  transfers between devices with their start and end apart: 29 -> 91, of which waited for: 29 -> 38; matrix products, arithmetic and copies ran while one was open for 9% -> 11% of each run, Pallas kernels for 0% -> 33%
where the time goes in v1:
time: 1230 us; the launch traced here: 1220 us
  waiting for transfers between devices  476 us (39%)
  Pallas kernels  467 us (38%)
  other arithmetic  111 us (9%)
  starting transfers between devices  95 us (8%)
  local copies, waits for them, and re-layouts  67.3 us (5%)
    ppermute x85, waiting for transfers between devices, move(): sent.append(lax.ppermute(values, axis, moves))  468 us
    pallas_call x20, Pallas kernels, outer(): pl.pallas_call(kernel, grid=(steps,), in_specs=[pl.BlockSpec((count, bloc...  141 us
    pallas_call x8, Pallas kernels, expand(): pl.pallas_call(kernel, grid=(4 * cuts,), in_specs=specs, out_specs=[pl.Bl...  109 us
    ppermute x85, starting transfers between devices, move(): sent.append(lax.ppermute(values, axis, moves))  86 us
    pallas_call x2, Pallas kernels, ff_forward(): pl.pallas_call(kernel, grid=(features // block,), in_specs=[pl.BlockSpec(...  42.2 us
    pallas_call x2, Pallas kernels, attend_back(): pl.pallas_call(kernel, grid_spec=pltpu.PrefetchScalarGridSpec(num_scalar_...  39.2 us
    pallas_call x10, Pallas kernels, join(): pl.pallas_call(kernel, grid=(steps, 4), in_specs=[source(first) for _, fi...  37.3 us
    pallas_call x2, Pallas kernels, ff_back(): pl.pallas_call(kernel, grid=(features // block,), in_specs=[pl.BlockSpec(...  34.9 us
  transfers between devices with their start and end apart: 91, of which 38 were waited for; matrix products, arithmetic and copies ran while one was open for 11% of the time, Pallas kernels for 33%

profile of v1, /device:TPU:0, one launch (start us, length us, event | category | flops | bytes accessed | tf_op | source)
XLA Modules:
  0.0 1222.6 jit_solution(5444629238120365969)
XLA Ops:
  15.6 16.0 %collective-permute-done.4.refs_0_ = bf16[1024,512]{1,0:T(8,128)(2,1)} collective-permute-done((bf16[1024,512]{1,0:T(8,128)(2,1)S(1)}, bf16[1024,512]{1,0:T(8,128)(2,1)}, u32[]{:S(2)}, u32[]{:S(2)}) %collective-permute-start.4) | collective-permute-done | bytes 1048608 | tf_op jit(solution)/shard_map/ppermute | solution.py:900
  33.2 26.5 %collective-permute-done = bf16[256,2048]{1,0:T(8,128)(2,1)S(1)} collective-permute-done((bf16[256,2048]{1,0:T(8,128)(2,1)S(1)}, bf16[256,2048]{1,0:T(8,128)(2,1)S(1)}, u32[]{:S(2)}, u32[]{:S(2)}) %collective-permute-start) | collective-permute-done | bytes 1048608 | tf_op jit(solution)/shard_map/ppermute | solution.py:900
  71.8 12.6 %collective-permute-done.7.refs_2_ = bf16[1024,512]{1,0:T(8,128)(2,1)} collective-permute-done((bf16[1024,512]{1,0:T(8,128)(2,1)}, bf16[1024,512]{1,0:T(8,128)(2,1)}, u32[]{:S(2)}, u32[]{:S(2)}) %collective-permute-start.7) | collective-permute-done | bytes 1048608 | tf_op jit(solution)/shard_map/ppermute | solution.py:900
  91.2 25.3 %collective-permute-done.2 = bf16[256,2048]{1,0:T(8,128)(2,1)} collective-permute-done((bf16[256,2048]{1,0:T(8,128)(2,1)}, bf16[256,2048]{1,0:T(8,128)(2,1)}, u32[]{:S(2)}, u32[]{:S(2)}) %collective-permute-start.2) | collective-permute-done | bytes 1048608 | tf_op jit(solution)/shard_map/ppermute | solution.py:900
  130.6 5.5 collective-permute-done.12.refs_0_
  142.3 25.1 %collective-permute-done.14.refs_2_ = bf16[704,512]{1,0:T(8,128)(2,1)} collective-permute-done((bf16[704,512]{1,0:T(8,128)(2,1)S(1)}, bf16[704,512]{1,0:T(8,128)(2,1)}, u32[]{:S(2)}, u32[]{:S(2)}) %collective-permute-start.14) | collective-permute-done | bytes 720928 | tf_op jit(solution)/shard_map/ppermute | solution.py:900
  181.6 7.7 collective-permute-done.15.refs_2_
  191.3 18.9 %project.3.proj_ref = f32[1024,3072]{1,0:T(8,128)} custom-call(bf16[1024,2048]{1,0:T(8,128)(2,1)} %pad_maximum_fusion.rows_ref.refs_2_.refs_3_, bf16[4096,512]{1,0:T(8,128)(2,1)} %join.11.w0.refs_1_.refs_6_, bf16[4096,512]{1,0:T(8,128)(2,1)} %join.13.w1.refs_2_.refs_7_, bf16[4096,512]{1,0:T(8,128)(2,1)} %collective-permute-done.9.w2.refs_3_.refs_8_, ...), custom_call_target="tpu_custom_call" | custom-call | flops 6442450944 | bytes 1 | tf_op jit(solution)/shard_map/project/pallas_call | solution.py:653
  210.2 15.0 %attend.2 = (bf16[1024,512]{1,0:T(8,128)(2,1)S(1)}, bf16[1024,1536]{1,0:T(8,128)(2,1)S(1)}, f32[4,1,1024]{2,1,0:T(1,128)S(1)}) custom-call(s32[1]{0:T(128)} %bitcast.6.limit_ref, f32[1024,3072]{1,0:T(8,128)} %project.3.proj_ref, f32[1024,128]{1,0:T(8,128)S(1)} %pad_maximum_fusion.13.cos_ref, f32[1024,128]{1,0:T(8,128)S(1)} %pad_maximum_fusion.14.sin_ref, ...), custom_call_target="tpu_custom_call" | custom-call | flops 2147483648 | bytes 1 | tf_op jit(solution)/shard_map/attend/pallas_call | solution.py:395
  226.9 15.2 %attend.3 = (bf16[1024,512]{1,0:T(8,128)(2,1)S(1)}, bf16[1024,1536]{1,0:T(8,128)(2,1)S(1)}, f32[4,1,1024]{2,1,0:T(1,128)S(1)}) custom-call(s32[1]{0:T(128)} %bitcast.6.limit_ref, f32[1024,3072]{1,0:T(8,128)} %project.3.proj_ref, f32[1024,128]{1,0:T(8,128)S(1)} %pad_maximum_fusion.13.cos_ref, f32[1024,128]{1,0:T(8,128)S(1)} %pad_maximum_fusion.14.sin_ref, ...), custom_call_target="tpu_custom_call" | custom-call | flops 2147483648 | bytes 1 | tf_op jit(solution)/shard_map/attend/pallas_call | solution.py:395
  244.8 6.5 expand.8
  255.4 6.5 expand.9
  261.9 27.5 %collective-permute-done.19 = bf16[256,2048]{1,0:T(8,128)(2,1)} collective-permute-done((bf16[256,2048]{1,0:T(8,128)(2,1)}, bf16[256,2048]{1,0:T(8,128)(2,1)}, u32[]{:S(2)}, u32[]{:S(2)}) %collective-permute-start.19) | collective-permute-done | bytes 1048608 | tf_op jit(solution)/shard_map/ppermute | solution.py:900
  305.3 8.1 collective-permute-done.20
  327.3 10.4 collective-permute-done.27.refs_3_
  347.7 19.9 %collective-permute-done.21 = bf16[256,2048]{1,0:T(8,128)(2,1)S(1)} collective-permute-done((bf16[256,2048]{1,0:T(8,128)(2,1)S(1)}, bf16[256,2048]{1,0:T(8,128)(2,1)S(1)}, u32[]{:S(2)}, u32[]{:S(2)}) %collective-permute-start.21) | collective-permute-done | bytes 1048608 | tf_op jit(solution)/shard_map/ppermute | solution.py:900
  373.4 38.1 %collective-permute-done.32 = bf16[256,2048]{1,0:T(8,128)(2,1)S(1)} collective-permute-done((bf16[256,2048]{1,0:T(8,128)(2,1)S(1)}, bf16[256,2048]{1,0:T(8,128)(2,1)S(1)}, u32[]{:S(2)}, u32[]{:S(2)}) %collective-permute-start.32) | collective-permute-done | bytes 1048608 | tf_op jit(solution)/shard_map/ppermute | solution.py:900
  413.1 21.0 %ff_forward.2 = (bf16[512,2816]{1,0:T(8,128)(2,1)}, bf16[512,2816]{1,0:T(8,128)(2,1)}, bf16[512,2816]{1,0:T(8,128)(2,1)}) custom-call(bf16[512,2048]{1,0:T(8,128)(2,1)} %pad_maximum_fusion.3.rows_ref.refs_2_, bf16[2816,512]{1,0:T(8,128)(2,1)} %join.14.refs_0_.refs_1_, bf16[2816,512]{1,0:T(8,128)(2,1)} %join.15.refs_1_.refs_2_, ...), custom_call_target="tpu_custom_call" | custom-call | flops 5905580032 | bytes 1 | tf_op jit(solution)/shard_map/ff_forward/pallas_call | solution.py:681
  434.1 21.3 %ff_forward.3 = (bf16[512,2816]{1,0:T(8,128)(2,1)}, bf16[512,2816]{1,0:T(8,128)(2,1)}, bf16[512,2816]{1,0:T(8,128)(2,1)}) custom-call(bf16[512,2048]{1,0:T(8,128)(2,1)} %pad_maximum_fusion.4.rows_ref.refs_3_, bf16[2816,512]{1,0:T(8,128)(2,1)} %join.14.refs_0_.refs_1_, bf16[2816,512]{1,0:T(8,128)(2,1)} %join.15.refs_1_.refs_2_, ...), custom_call_target="tpu_custom_call" | custom-call | flops 5905580032 | bytes 1 | tf_op jit(solution)/shard_map/ff_forward/pallas_call | solution.py:681
  463.7 5.1 collective-permute-done.36.refs_4_.w3
  473.0 12.8 %expand.10 = (f32[256,2048]{1,0:T(8,128)}, bf16[256,2048]{1,0:T(8,128)(2,1)}) custom-call(bf16[512,2816]{1,0:T(8,128)(2,1)} %get-tuple-element.310.refs_0_, bf16[2816,512]{1,0:T(8,128)(2,1)} %join.18.refs_1_.w0, bf16[2816,512]{1,0:T(8,128)(2,1)} %join.19.refs_2_.w1, bf16[2816,512]{1,0:T(8,128)(2,1)} %collective-permute-done.35.refs_3_.w2, ...), custom_call_target="tpu_custom_call" | custom-call | flops 2952790016 | bytes 1 | tf_op jit(solution)/shard_map/expand/pallas_call | solution.py:773
  485.8 13.1 %expand.11 = (f32[256,2048]{1,0:T(8,128)}, bf16[256,2048]{1,0:T(8,128)(2,1)}) custom-call(bf16[512,2816]{1,0:T(8,128)(2,1)} %get-tuple-element.260.refs_0_.refs_1_, bf16[2816,512]{1,0:T(8,128)(2,1)} %join.18.refs_1_.w0, bf16[2816,512]{1,0:T(8,128)(2,1)} %join.19.refs_2_.w1, bf16[2816,512]{1,0:T(8,128)(2,1)} %collective-permute-done.35.refs_3_.w2, ...), custom_call_target="tpu_custom_call" | custom-call | flops 2952790016 | bytes 1 | tf_op jit(solution)/shard_map/expand/pallas_call | solution.py:773
  498.9 12.4 %collective-permute-done.37 = bf16[256,2048]{1,0:T(8,128)(2,1)} collective-permute-done((bf16[256,2048]{1,0:T(8,128)(2,1)}, bf16[256,2048]{1,0:T(8,128)(2,1)}, u32[]{:S(2)}, u32[]{:S(2)}) %collective-permute-start.37) | collective-permute-done | bytes 1048608 | tf_op jit(solution)/shard_map/ppermute | solution.py:900
  515.0 20.9 %collective-permute-done.38 = bf16[256,2048]{1,0:T(8,128)(2,1)S(1)} collective-permute-done((bf16[256,2048]{1,0:T(8,128)(2,1)}, bf16[256,2048]{1,0:T(8,128)(2,1)S(1)}, u32[]{:S(2)}, u32[]{:S(2)}) %collective-permute-start.38) | collective-permute-done | bytes 1048608 | tf_op jit(solution)/shard_map/ppermute | solution.py:900
  552.1 20.4 %collective-permute-done.40 = bf16[256,2048]{1,0:T(8,128)(2,1)S(1)} collective-permute-done((bf16[256,2048]{1,0:T(8,128)(2,1)S(1)}, bf16[256,2048]{1,0:T(8,128)(2,1)S(1)}, u32[]{:S(2)}, u32[]{:S(2)}) %collective-permute-start.40) | collective-permute-done | bytes 1048608 | tf_op jit(solution)/shard_map/ppermute | solution.py:900
  575.0 17.5 %ff_back.2 = (bf16[512,2816]{1,0:T(8,128)(2,1)}, bf16[512,2816]{1,0:T(8,128)(2,1)}, f32[1,2816]{1,0:T(1,128)}, f32[1,2816]{1,0:T(1,128)}) custom-call(bf16[512,2048]{1,0:T(8,128)(2,1)} %pad_maximum_fusion.6.rows_ref.refs_2_, bf16[2816,512]{1,0:T(8,128)(2,1)} %join.18.refs_1_.w0, bf16[2816,512]{1,0:T(8,128)(2,1)} %join.19.refs_2_.w1, ...), custom_call_target="tpu_custom_call" | custom-call | flops 4429185024 | bytes 1 | tf_op jit(solution)/shard_map/ff_back/pallas_call | solution.py:720
  595.3 21.4 %expand.12 = (f32[256,2048]{1,0:T(8,128)}, bf16[256,2048]{1,0:T(8,128)(2,1)}) custom-call(bf16[512,2816]{1,0:T(8,128)(2,1)} %get-tuple-element.317.refs_0_, bf16[2816,512]{1,0:T(8,128)(2,1)} %join.14.refs_0_.refs_1_, bf16[2816,512]{1,0:T(8,128)(2,1)} %join.15.refs_1_.refs_2_, bf16[2816,512]{1,0:T(8,128)(2,1)} %collective-permute-done.28.refs_2_.refs_3_, ...), custom_call_target="tpu_custom_call" | custom-call | flops 5905580032 | bytes 1 | tf_op jit(solution)/shard_map/expand/pallas_call | solution.py:773
  619.8 10.4 outer.20
  631.5 17.4 %ff_back.3 = (bf16[512,2816]{1,0:T(8,128)(2,1)}, bf16[512,2816]{1,0:T(8,128)(2,1)}, f32[1,2816]{1,0:T(1,128)}, f32[1,2816]{1,0:T(1,128)}) custom-call(bf16[512,2048]{1,0:T(8,128)(2,1)} %pad_maximum_fusion.8.refs_3_.rows_ref, bf16[2816,512]{1,0:T(8,128)(2,1)} %join.18.refs_1_.w0, bf16[2816,512]{1,0:T(8,128)(2,1)} %join.19.refs_2_.w1, ...), custom_call_target="tpu_custom_call" | custom-call | flops 4429185024 | bytes 1 | tf_op jit(solution)/shard_map/ff_back/pallas_call | solution.py:720
  648.9 7.2 collective-permute-done.42
  664.8 8.2 outer.21
  674.3 21.5 %expand.13 = (f32[256,2048]{1,0:T(8,128)}, bf16[256,2048]{1,0:T(8,128)(2,1)}) custom-call(bf16[512,2816]{1,0:T(8,128)(2,1)} %get-tuple-element.283.refs_0_.refs_1_, bf16[2816,512]{1,0:T(8,128)(2,1)} %join.14.refs_0_.refs_1_, bf16[2816,512]{1,0:T(8,128)(2,1)} %join.15.refs_1_.refs_2_, bf16[2816,512]{1,0:T(8,128)(2,1)} %collective-permute-done.28.refs_2_.refs_3_, ...), custom_call_target="tpu_custom_call" | custom-call | flops 5905580032 | bytes 1 | tf_op jit(solution)/shard_map/expand/pallas_call | solution.py:773
  695.8 10.4 outer.22
  706.2 10.9 outer.23
  731.2 16.5 %collective-permute-done.46 = bf16[256,2048]{1,0:T(8,128)(2,1)} collective-permute-done((bf16[256,2048]{1,0:T(8,128)(2,1)}, bf16[256,2048]{1,0:T(8,128)(2,1)}, u32[]{:S(2)}, u32[]{:S(2)}) %collective-permute-start.46) | collective-permute-done | bytes 1048608 | tf_op jit(solution)/shard_map/ppermute | solution.py:900
  760.0 6.0 project.4
  766.1 13.2 %outer.24 = (bf16[704,1024]{1,0:T(8,128)(2,1)}, bf16[704,1024]{1,0:T(8,128)(2,1)}, bf16[704,1024]{1,0:T(8,128)(2,1)}, bf16[704,1024]{1,0:T(8,128)(2,1)}) custom-call(bf16[512,2816]{1,0:T(8,128)(2,1)} %get-tuple-element.293.refs_5_.refs_0_, bf16[512,2816]{1,0:T(8,128)(2,1)} %get-tuple-element.284.refs_5_.refs_1_, ...), custom_call_target="tpu_custom_call" | custom-call | flops 4429185024 | bytes 1 | tf_op jit(solution)/shard_map/outer/pallas_call | solution.py:833
  779.3 8.3 outer.25
  790.3 10.2 collective-permute-done.39
  809.1 6.4 project.5
  828.2 19.6 %attend_back.2 = (bf16[1024,1536]{1,0:T(8,128)(2,1)}, f32[4,1,384]{2,1,0:T(1,128)S(1)}) custom-call(s32[1]{0:T(128)} %bitcast.6.limit_ref, bf16[1024,1536]{1,0:T(8,128)(2,1)} %copy-done.5, bf16[1024,1024]{1,0:T(8,128)(2,1)S(1)} %copy-done.2, f32[4,1,1024]{2,1,0:T(1,128)S(1)} %get-tuple-element.304.lse_ref, f32[1024,128]{1,0:T(8,128)S(1)} %pad_maximum_fusion.13.cos_ref, ...), custom_call_target="tpu_custom_call" | custom-call | flops 2684354560 | bytes 1 | tf_op jit(solution)/shard_map/attend_back/pallas_call | solution.py:522
  848.1 7.6 outer.28
  855.7 9.3 outer.29
  867.2 19.6 %attend_back.3 = (bf16[1024,1536]{1,0:T(8,128)(2,1)}, f32[4,1,384]{2,1,0:T(1,128)S(1)}) custom-call(s32[1]{0:T(128)} %bitcast.6.limit_ref, bf16[1024,1536]{1,0:T(8,128)(2,1)} %copy-done.4, bf16[1024,1024]{1,0:T(8,128)(2,1)S(1)} %copy-done.3, f32[4,1,1024]{2,1,0:T(1,128)S(1)} %get-tuple-element.314.lse_ref, f32[1024,128]{1,0:T(8,128)S(1)} %pad_maximum_fusion.13.cos_ref, ...), custom_call_target="tpu_custom_call" | custom-call | flops 2684354560 | bytes 1 | tf_op jit(solution)/shard_map/attend_back/pallas_call | solution.py:522
  895.4 9.5 outer.30
  905.8 7.9 outer.31
  938.3 6.4 collective-permute-done.56
  947.4 5.6 outer.32
  954.3 5.9 collective-permute-done.60
  960.2 14.0 %expand.14 = (f32[256,2048]{1,0:T(8,128)}, bf16[256,2048]{1,0:T(8,128)(2,1)}) custom-call(bf16[512,1536]{1,0:T(8,128)(2,1)} %get-tuple-element.334.refs_0_, bf16[4096,512]{1,0:T(8,128)(2,1)} %join.11.w0.refs_1_.refs_6_, bf16[4096,512]{1,0:T(8,128)(2,1)} %join.13.w1.refs_2_.refs_7_, bf16[4096,512]{1,0:T(8,128)(2,1)} %collective-permute-done.9.w2.refs_3_.refs_8_, ...), custom_call_target="tpu_custom_call" | custom-call | flops 3221225472 | bytes 1 | tf_op jit(solution)/shard_map/expand/pallas_call | solution.py:773
  980.0 5.7 outer.33
  988.8 5.1 collective-permute-done.67
  999.3 13.8 %expand.15 = (f32[256,2048]{1,0:T(8,128)}, bf16[256,2048]{1,0:T(8,128)(2,1)}) custom-call(bf16[512,1536]{1,0:T(8,128)(2,1)} %get-tuple-element.345.refs_0_, bf16[4096,512]{1,0:T(8,128)(2,1)} %join.11.w0.refs_1_.refs_6_, bf16[4096,512]{1,0:T(8,128)(2,1)} %join.13.w1.refs_2_.refs_7_, bf16[4096,512]{1,0:T(8,128)(2,1)} %collective-permute-done.9.w2.refs_3_.refs_8_, ...), custom_call_target="tpu_custom_call" | custom-call | flops 3221225472 | bytes 1 | tf_op jit(solution)/shard_map/expand/pallas_call | solution.py:773
  1018.8 6.0 outer.34
  1036.3 16.5 %collective-permute-done.69 = bf16[256,2048]{1,0:T(8,128)(2,1)} collective-permute-done((bf16[256,2048]{1,0:T(8,128)(2,1)}, bf16[256,2048]{1,0:T(8,128)(2,1)}, u32[]{:S(2)}, u32[]{:S(2)}) %collective-permute-start.69) | collective-permute-done | bytes 1048608 | tf_op jit(solution)/shard_map/ppermute | solution.py:900
  1053.9 6.0 outer.37
  1072.1 11.4 collective-permute-done.85
  1091.7 11.1 collective-permute-done.76
  1110.1 12.6 %collective-permute-done.84 = bf16[768,512]{1,0:T(8,128)(2,1)S(1)} collective-permute-done((bf16[768,512]{1,0:T(8,128)(2,1)S(1)}, bf16[768,512]{1,0:T(8,128)(2,1)S(1)}, u32[]{:S(2)}, u32[]{:S(2)}) %collective-permute-start.84) | collective-permute-done | bytes 786464 | tf_op jit(solution)/shard_map/ppermute | solution.py:900
  1129.9 23.5 %collective-permute-done.77 = bf16[256,2048]{1,0:T(8,128)(2,1)} collective-permute-done((bf16[256,2048]{1,0:T(8,128)(2,1)}, bf16[256,2048]{1,0:T(8,128)(2,1)}, u32[]{:S(2)}, u32[]{:S(2)}) %collective-permute-start.77) | collective-permute-done | bytes 1048608 | tf_op jit(solution)/shard_map/ppermute | solution.py:900
  1157.4 29.2 %collective-permute-done.86 = bf16[704,512]{1,0:T(8,128)(2,1)S(1)} collective-permute-done((bf16[704,512]{1,0:T(8,128)(2,1)}, bf16[704,512]{1,0:T(8,128)(2,1)S(1)}, u32[]{:S(2)}, u32[]{:S(2)}) %collective-permute-start.86) | collective-permute-done | bytes 720928 | tf_op jit(solution)/shard_map/ppermute | solution.py:900
  1189.4 10.5 collective-permute-done.87
  1203.9 7.8 collective-permute-done.88
  1216.0 6.2 copy.50
  (517 shorter events, 349.1 us)
Async XLA Ops:
  5.2 26.3 %collective-permute-start.4 = (bf16[1024,512]{1,0:T(8,128)(2,1)S(1)}, bf16[1024,512]{1,0:T(8,128)(2,1)}, u32[]{:S(2)}, u32[]{:S(2)}) collective-permute-start(bf16[1024,512]{1,0:T(8,128)(2,1)S(1)} %pad_maximum_fusion.11.refs_0_), channel_id=1, source_target_pairs={{0,8},{4,12},{8,0},{12,4},{1,9},{5,13},{9,1},{13,5},{2,10},{6,14},... | collective-permute-start | bytes 3145736 | tf_op jit(solution)/shard_map/ppermute | solution.py:900
  8.2 51.4 %collective-permute-start.1 = (bf16[1024,512]{1,0:T(8,128)(2,1)S(1)}, bf16[1024,512]{1,0:T(8,128)(2,1)}, u32[]{:S(2)}, u32[]{:S(2)}) collective-permute-start(bf16[1024,512]{1,0:T(8,128)(2,1)S(1)} %pad_maximum_fusion.11.refs_0_), channel_id=1, source_target_pairs={{0,2},{1,3},{2,0},{3,1},{4,6},{5,7},{6,4},{7,5},{8,10},{9,11},{10,... | collective-permute-start | bytes 3145736 | tf_op jit(solution)/shard_map/ppermute | solution.py:900
  14.0 45.7 %collective-permute-start = (bf16[256,2048]{1,0:T(8,128)(2,1)S(1)}, bf16[256,2048]{1,0:T(8,128)(2,1)S(1)}, u32[]{:S(2)}, u32[]{:S(2)}) collective-permute-start(bf16[256,2048]{1,0:T(8,128)(2,1)S(1)} %get-tuple-element.488), channel_id=1, source_target_pairs={{0,1},{1,0},{2,3},{3,2},{4,5},{5,4},{6,7},{7,6},{8,9},{9,8},{10,11... | collective-permute-start | bytes 3145736 | tf_op jit(solution)/shard_map/ppermute | solution.py:900
  31.5 29.1 %collective-permute-start.5 = (bf16[1024,512]{1,0:T(8,128)(2,1)}, bf16[1024,512]{1,0:T(8,128)(2,1)}, u32[]{:S(2)}, u32[]{:S(2)}) collective-permute-start(bf16[1024,512]{1,0:T(8,128)(2,1)} %collective-permute-done.4.refs_0_), channel_id=1, source_target_pairs={{0,16},{16,0},{1,17},{17,1},{2,18},{18,2},{3,19},{19,3},{4,20},{20... | collective-permute-start | bytes 3145736 | tf_op jit(solution)/shard_map/ppermute | solution.py:900
  69.7 46.8 %collective-permute-start.2 = (bf16[256,2048]{1,0:T(8,128)(2,1)}, bf16[256,2048]{1,0:T(8,128)(2,1)}, u32[]{:S(2)}, u32[]{:S(2)}) collective-permute-start(bf16[256,2048]{1,0:T(8,128)(2,1)} %get-tuple-element.200), channel_id=1, source_target_pairs={{0,2},{1,3},{2,0},{3,1},{4,6},{5,7},{6,4},{7,5},{8,10},{9,11},{10,... | collective-permute-start | bytes 3145736 | tf_op jit(solution)/shard_map/ppermute | solution.py:900
  70.3 46.2 %collective-permute-start.6 = (bf16[1024,512]{1,0:T(8,128)(2,1)}, bf16[1024,512]{1,0:T(8,128)(2,1)}, u32[]{:S(2)}, u32[]{:S(2)}) collective-permute-start(bf16[1024,512]{1,0:T(8,128)(2,1)} %collective-permute-done.1.refs_2_), channel_id=1, source_target_pairs={{0,16},{16,0},{1,17},{17,1},{2,18},{18,2},{3,19},{19,3},{4,20},{20... | collective-permute-start | bytes 3145736 | tf_op jit(solution)/shard_map/ppermute | solution.py:900
  84.4 38.9 %collective-permute-start.8 = (bf16[1024,512]{1,0:T(8,128)(2,1)}, bf16[1024,512]{1,0:T(8,128)(2,1)}, u32[]{:S(2)}, u32[]{:S(2)}) collective-permute-start(bf16[1024,512]{1,0:T(8,128)(2,1)} %collective-permute-done.7.refs_2_), channel_id=1, source_target_pairs={{0,16},{16,0},{1,17},{17,1},{2,18},{18,2},{3,19},{19,3},{4,20},{20... | collective-permute-start | bytes 3145736 | tf_op jit(solution)/shard_map/ppermute | solution.py:900
  89.6 46.4 %collective-permute-start.12 = (bf16[2112,512]{1,0:T(8,128)(2,1)}, bf16[2112,512]{1,0:T(8,128)(2,1)}, u32[]{:S(2)}, u32[]{:S(2)}) collective-permute-start(bf16[2112,512]{1,0:T(8,128)(2,1)} %pad_maximum_fusion.1), channel_id=1, source_target_pairs={{0,8},{4,12},{8,0},{12,4},{1,9},{5,13},{9,1},{13,5},{2,10},{6,14},... | collective-permute-start | bytes 6488072 | tf_op jit(solution)/shard_map/ppermute | solution.py:900
  123.3 68.0 %collective-permute-start.9 = (bf16[4096,512]{1,0:T(8,128)(2,1)}, bf16[4096,512]{1,0:T(8,128)(2,1)}, u32[]{:S(2)}, u32[]{:S(2)}) collective-permute-start(bf16[4096,512]{1,0:T(8,128)(2,1)} %join.11.w0.refs_1_.refs_6_), channel_id=1, source_target_pairs={{0,4},{4,0},{8,12},{12,8},{1,5},{5,1},{9,13},{13,9},{2,6},{6,2},{1... | collective-permute-start | bytes 12582920 | tf_op jit(solution)/shard_map/ppermute | solution.py:900
  130.1 61.2 %collective-permute-start.10 = (bf16[4096,512]{1,0:T(8,128)(2,1)}, bf16[4096,512]{1,0:T(8,128)(2,1)}, u32[]{:S(2)}, u32[]{:S(2)}) collective-permute-start(bf16[4096,512]{1,0:T(8,128)(2,1)} %join.13.w1.refs_2_.refs_7_), channel_id=1, source_target_pairs={{0,4},{4,0},{8,12},{12,8},{1,5},{5,1},{9,13},{13,9},{2,6},{6,2},{1... | collective-permute-start | bytes 12582920 | tf_op jit(solution)/shard_map/ppermute | solution.py:900
  136.1 54.7 %collective-permute-start.13 = (bf16[2112,512]{1,0:T(8,128)(2,1)}, bf16[2112,512]{1,0:T(8,128)(2,1)}, u32[]{:S(2)}, u32[]{:S(2)}) collective-permute-start(bf16[2112,512]{1,0:T(8,128)(2,1)} %collective-permute-done.12.refs_0_), channel_id=1, source_target_pairs={{0,16},{16,0},{1,17},{17,1},{2,18},{18,2},{3,19},{19,3},{4,20},{20... | collective-permute-start | bytes 6488072 | tf_op jit(solution)/shard_map/ppermute | solution.py:900
  137.1 30.3 %collective-permute-start.14 = (bf16[704,512]{1,0:T(8,128)(2,1)S(1)}, bf16[704,512]{1,0:T(8,128)(2,1)}, u32[]{:S(2)}, u32[]{:S(2)}) collective-permute-start(bf16[704,512]{1,0:T(8,128)(2,1)S(1)} %bitcast.155), channel_id=1, source_target_pairs={{0,2},{1,3},{2,0},{3,1},{4,6},{5,7},{6,4},{7,5},{8,10},{9,11},{10,... | collective-permute-start | bytes 2162696 | tf_op jit(solution)/shard_map/ppermute | solution.py:900
  137.3 37.8 %collective-permute-start.3 = (bf16[256,2048]{1,0:T(8,128)(2,1)}, bf16[256,2048]{1,0:T(8,128)(2,1)}, u32[]{:S(2)}, u32[]{:S(2)}) collective-permute-start(bf16[256,2048]{1,0:T(8,128)(2,1)} %collective-permute-done.2), channel_id=1, source_target_pairs={{0,1},{1,0},{2,3},{3,2},{4,5},{5,4},{6,7},{7,6},{8,9},{9,8},{10,11... | collective-permute-start | bytes 3145736 | tf_op jit(solution)/shard_map/ppermute | solution.py:900
  175.1 69.7 %collective-permute-start.18 = (bf16[704,512]{1,0:T(8,128)(2,1)}, bf16[704,512]{1,0:T(8,128)(2,1)}, u32[]{:S(2)}, u32[]{:S(2)}) collective-permute-start(bf16[704,512]{1,0:T(8,128)(2,1)} %bitcast.152), channel_id=1, source_target_pairs={{0,2},{1,3},{2,0},{3,1},{4,6},{5,7},{6,4},{7,5},{8,10},{9,11},{10,... | collective-permute-start | bytes 2162696 | tf_op jit(solution)/shard_map/ppermute | solution.py:900
  189.2 37.7 %collective-permute-start.16 = (bf16[704,512]{1,0:T(8,128)(2,1)}, bf16[704,512]{1,0:T(8,128)(2,1)}, u32[]{:S(2)}, u32[]{:S(2)}) collective-permute-start(bf16[704,512]{1,0:T(8,128)(2,1)} %collective-permute-done.14.refs_2_), channel_id=1, source_target_pairs={{0,16},{16,0},{1,17},{17,1},{2,18},{18,2},{3,19},{19,3},{4,20},{20... | collective-permute-start | bytes 2162696 | tf_op jit(solution)/shard_map/ppermute | solution.py:900
  190.7 54.0 %collective-permute-start.17 = (bf16[704,512]{1,0:T(8,128)(2,1)}, bf16[704,512]{1,0:T(8,128)(2,1)}, u32[]{:S(2)}, u32[]{:S(2)}) collective-permute-start(bf16[704,512]{1,0:T(8,128)(2,1)} %collective-permute-done.15.refs_2_), channel_id=1, source_target_pairs={{0,16},{16,0},{1,17},{17,1},{2,18},{18,2},{3,19},{19,3},{4,20},{20... | collective-permute-start | bytes 2162696 | tf_op jit(solution)/shard_map/ppermute | solution.py:900
  251.2 38.2 %collective-permute-start.19 = (bf16[256,2048]{1,0:T(8,128)(2,1)}, bf16[256,2048]{1,0:T(8,128)(2,1)}, u32[]{:S(2)}, u32[]{:S(2)}) collective-permute-start(bf16[256,2048]{1,0:T(8,128)(2,1)} %get-tuple-element.223), channel_id=1, source_target_pairs={{0,1},{1,0},{2,3},{3,2},{4,5},{5,4},{6,7},{7,6},{8,9},{9,8},{10,11... | collective-permute-start | bytes 3145736 | tf_op jit(solution)/shard_map/ppermute | solution.py:900
  251.4 43.0 %collective-permute-start.22 = (bf16[704,512]{1,0:T(8,128)(2,1)}, bf16[704,512]{1,0:T(8,128)(2,1)}, u32[]{:S(2)}, u32[]{:S(2)}) collective-permute-start(bf16[704,512]{1,0:T(8,128)(2,1)} %collective-permute-done.18.refs_2_), channel_id=1, source_target_pairs={{0,8},{4,12},{8,0},{12,4},{1,9},{5,13},{9,1},{13,5},{2,10},{6,14},... | collective-permute-start | bytes 2162696 | tf_op jit(solution)/shard_map/ppermute | solution.py:900
  252.2 42.1 %collective-permute-start.24 = (bf16[704,512]{1,0:T(8,128)(2,1)S(1)}, bf16[704,512]{1,0:T(8,128)(2,1)}, u32[]{:S(2)}, u32[]{:S(2)}) collective-permute-start(bf16[704,512]{1,0:T(8,128)(2,1)S(1)} %get-tuple-element.250.refs_0_), channel_id=1, source_target_pairs={{0,2},{1,3},{2,0},{3,1},{4,6},{5,7},{6,4},{7,5},{8,10},{9,11},{10,... | collective-permute-start | bytes 2162696 | tf_op jit(solution)/shard_map/ppermute | solution.py:900
  254.2 40.2 %collective-permute-start.23 = (bf16[704,512]{1,0:T(8,128)(2,1)}, bf16[704,512]{1,0:T(8,128)(2,1)}, u32[]{:S(2)}, u32[]{:S(2)}) collective-permute-start(bf16[704,512]{1,0:T(8,128)(2,1)} %collective-permute-done.18.refs_2_), channel_id=1, source_target_pairs={{0,16},{16,0},{1,17},{17,1},{2,18},{18,2},{3,19},{19,3},{4,20},{20... | collective-permute-start | bytes 2162696 | tf_op jit(solution)/shard_map/ppermute | solution.py:900
  302.5 39.0 %collective-permute-start.29 = (bf16[2816,512]{1,0:T(8,128)(2,1)}, bf16[2816,512]{1,0:T(8,128)(2,1)}, u32[]{:S(2)}, u32[]{:S(2)}) collective-permute-start(bf16[2816,512]{1,0:T(8,128)(2,1)} %join.15.refs_1_.refs_2_), channel_id=1, source_target_pairs={{0,4},{4,0},{8,12},{12,8},{1,5},{5,1},{9,13},{13,9},{2,6},{6,2},{1... | collective-permute-start | bytes 8650760 | tf_op jit(solution)/shard_map/ppermute | solution.py:900
  302.6 38.9 %collective-permute-start.28 = (bf16[2816,512]{1,0:T(8,128)(2,1)}, bf16[2816,512]{1,0:T(8,128)(2,1)}, u32[]{:S(2)}, u32[]{:S(2)}) collective-permute-start(bf16[2816,512]{1,0:T(8,128)(2,1)} %join.14.refs_0_.refs_1_), channel_id=1, source_target_pairs={{0,4},{4,0},{8,12},{12,8},{1,5},{5,1},{9,13},{13,9},{2,6},{6,2},{1... | collective-permute-start | bytes 8650760 | tf_op jit(solution)/shard_map/ppermute | solution.py:900
  341.6 71.5 %collective-permute-start.31 = (bf16[2816,512]{1,0:T(8,128)(2,1)}, bf16[2816,512]{1,0:T(8,128)(2,1)}, u32[]{:S(2)}, u32[]{:S(2)}) collective-permute-start(bf16[2816,512]{1,0:T(8,128)(2,1)} %join.17.refs_5_.refs_7_), channel_id=1, source_target_pairs={{0,4},{4,0},{8,12},{12,8},{1,5},{5,1},{9,13},{13,9},{2,6},{6,2},{1... | collective-permute-start | bytes 8650760 | tf_op jit(solution)/shard_map/ppermute | solution.py:900
  341.6 71.5 %collective-permute-start.30 = (bf16[2816,512]{1,0:T(8,128)(2,1)}, bf16[2816,512]{1,0:T(8,128)(2,1)}, u32[]{:S(2)}, u32[]{:S(2)}) collective-permute-start(bf16[2816,512]{1,0:T(8,128)(2,1)} %join.16.refs_4_.refs_6_), channel_id=1, source_target_pairs={{0,4},{4,0},{8,12},{12,8},{1,5},{5,1},{9,13},{13,9},{2,6},{6,2},{1... | collective-permute-start | bytes 8650760 | tf_op jit(solution)/shard_map/ppermute | solution.py:900
  342.1 25.5 %collective-permute-start.21 = (bf16[256,2048]{1,0:T(8,128)(2,1)S(1)}, bf16[256,2048]{1,0:T(8,128)(2,1)S(1)}, u32[]{:S(2)}, u32[]{:S(2)}) collective-permute-start(bf16[256,2048]{1,0:T(8,128)(2,1)S(1)} %get-tuple-element.227), channel_id=1, source_target_pairs={{0,1},{1,0},{2,3},{3,2},{4,5},{5,4},{6,7},{7,6},{8,9},{9,8},{10,11... | collective-permute-start | bytes 3145736 | tf_op jit(solution)/shard_map/ppermute | solution.py:900
  367.6 43.9 %collective-permute-start.32 = (bf16[256,2048]{1,0:T(8,128)(2,1)S(1)}, bf16[256,2048]{1,0:T(8,128)(2,1)S(1)}, u32[]{:S(2)}, u32[]{:S(2)}) collective-permute-start(bf16[256,2048]{1,0:T(8,128)(2,1)S(1)} %get-tuple-element.245), channel_id=1, source_target_pairs={{0,1},{1,0},{2,3},{3,2},{4,5},{5,4},{6,7},{7,6},{8,9},{9,8},{10,11... | collective-permute-start | bytes 3145736 | tf_op jit(solution)/shard_map/ppermute | solution.py:900
  370.6 63.5 %collective-permute-start.33 = (bf16[256,2048]{1,0:T(8,128)(2,1)}, bf16[256,2048]{1,0:T(8,128)(2,1)S(1)}, u32[]{:S(2)}, u32[]{:S(2)}) collective-permute-start(bf16[256,2048]{1,0:T(8,128)(2,1)} %dynamic-slice_bitcast_fusion), channel_id=1, source_target_pairs={{0,2},{1,3},{2,0},{3,1},{4,6},{5,7},{6,4},{7,5},{8,10},{9,11},{10,... | collective-permute-start | bytes 3145736 | tf_op jit(solution)/shard_map/ppermute | solution.py:900
  370.6 88.7 %collective-permute-start.34 = (bf16[704,512]{1,0:T(8,128)(2,1)}, bf16[704,512]{1,0:T(8,128)(2,1)}, u32[]{:S(2)}, u32[]{:S(2)}) collective-permute-start(bf16[704,512]{1,0:T(8,128)(2,1)} %collective-permute-done.25.refs_2_), channel_id=1, source_target_pairs={{0,16},{16,0},{1,17},{17,1},{2,18},{18,2},{3,19},{19,3},{4,20},{20... | collective-permute-start | bytes 2162696 | tf_op jit(solution)/shard_map/ppermute | solution.py:900
  485.8 25.5 %collective-permute-start.37 = (bf16[256,2048]{1,0:T(8,128)(2,1)}, bf16[256,2048]{1,0:T(8,128)(2,1)}, u32[]{:S(2)}, u32[]{:S(2)}) collective-permute-start(bf16[256,2048]{1,0:T(8,128)(2,1)} %get-tuple-element.258), channel_id=1, source_target_pairs={{0,1},{1,0},{2,3},{3,2},{4,5},{5,4},{6,7},{7,6},{8,9},{9,8},{10,11... | collective-permute-start | bytes 3145736 | tf_op jit(solution)/shard_map/ppermute | solution.py:900
  630.2 34.6 %collective-permute-start.44 = (bf16[2816,1024]{1,0:T(8,128)(2,1)}, bf16[2816,1024]{1,0:T(8,128)(2,1)}, u32[]{:S(2)}, u32[]{:S(2)}) collective-permute-start(bf16[2816,1024]{1,0:T(8,128)(2,1)} %outer.20), channel_id=1, source_target_pairs={{0,4},{4,0},{8,12},{12,8},{1,5},{5,1},{9,13},{13,9},{2,6},{6,2},{1... | collective-permute-start | bytes 17301512 | tf_op jit(solution)/shard_map/ppermute | solution.py:900
  630.2 25.9 %collective-permute-start.42 = (bf16[256,2048]{1,0:T(8,128)(2,1)}, bf16[256,2048]{1,0:T(8,128)(2,1)}, u32[]{:S(2)}, u32[]{:S(2)}) collective-permute-start(bf16[256,2048]{1,0:T(8,128)(2,1)} %get-tuple-element.274), channel_id=1, source_target_pairs={{0,1},{1,0},{2,3},{3,2},{4,5},{5,4},{6,7},{7,6},{8,9},{9,8},{10,11... | collective-permute-start | bytes 3145736 | tf_op jit(solution)/shard_map/ppermute | solution.py:900
  663.5 32.3 %collective-permute-start.43 = (bf16[256,2048]{1,0:T(8,128)(2,1)S(1)}, bf16[256,2048]{1,0:T(8,128)(2,1)}, u32[]{:S(2)}, u32[]{:S(2)}) collective-permute-start(bf16[256,2048]{1,0:T(8,128)(2,1)S(1)} %get-tuple-element.275), channel_id=1, source_target_pairs={{0,1},{1,0},{2,3},{3,2},{4,5},{5,4},{6,7},{7,6},{8,9},{9,8},{10,11... | collective-permute-start | bytes 3145736 | tf_op jit(solution)/shard_map/ppermute | solution.py:900
  673.0 33.2 %collective-permute-start.45 = (bf16[1408,512]{1,0:T(8,128)(2,1)}, bf16[1408,512]{1,0:T(8,128)(2,1)S(1)}, u32[]{:S(2)}, u32[]{:S(2)}) collective-permute-start(bf16[1408,512]{1,0:T(8,128)(2,1)} %get-tuple-element.287), channel_id=1, source_target_pairs={{0,8},{4,12},{8,0},{12,4},{1,9},{5,13},{9,1},{13,5},{2,10},{6,14},... | collective-permute-start | bytes 4325384 | tf_op jit(solution)/shard_map/ppermute | solution.py:900
  717.2 48.9 %collective-permute-start.48 = (bf16[2816,1024]{1,0:T(8,128)(2,1)}, bf16[2816,1024]{1,0:T(8,128)(2,1)}, u32[]{:S(2)}, u32[]{:S(2)}) collective-permute-start(bf16[2816,1024]{1,0:T(8,128)(2,1)} %outer.23), channel_id=1, source_target_pairs={{0,4},{4,0},{8,12},{12,8},{1,5},{5,1},{9,13},{13,9},{2,6},{6,2},{1... | collective-permute-start | bytes 17301512 | tf_op jit(solution)/shard_map/ppermute | solution.py:900
  717.2 62.1 %collective-permute-start.50 = (bf16[2816,1024]{1,0:T(8,128)(2,1)}, bf16[2816,1024]{1,0:T(8,128)(2,1)}, u32[]{:S(2)}, u32[]{:S(2)}) collective-permute-start(bf16[2816,1024]{1,0:T(8,128)(2,1)} %outer.22), channel_id=1, source_target_pairs={{0,4},{4,0},{8,12},{12,8},{1,5},{5,1},{9,13},{13,9},{2,6},{6,2},{1... | collective-permute-start | bytes 17301512 | tf_op jit(solution)/shard_map/ppermute | solution.py:900
  722.3 25.5 %collective-permute-start.46 = (bf16[256,2048]{1,0:T(8,128)(2,1)}, bf16[256,2048]{1,0:T(8,128)(2,1)}, u32[]{:S(2)}, u32[]{:S(2)}) collective-permute-start(bf16[256,2048]{1,0:T(8,128)(2,1)} %get-tuple-element.290), channel_id=1, source_target_pairs={{0,1},{1,0},{2,3},{3,2},{4,5},{5,4},{6,7},{7,6},{8,9},{9,8},{10,11... | collective-permute-start | bytes 3145736 | tf_op jit(solution)/shard_map/ppermute | solution.py:900
  730.0 49.3 %collective-permute-start.49 = (bf16[1408,512]{1,0:T(8,128)(2,1)}, bf16[1408,512]{1,0:T(8,128)(2,1)}, u32[]{:S(2)}, u32[]{:S(2)}) collective-permute-start(bf16[1408,512]{1,0:T(8,128)(2,1)} %get-tuple-element.282), channel_id=1, source_target_pairs={{0,8},{4,12},{8,0},{12,4},{1,9},{5,13},{9,1},{13,5},{2,10},{6,14},... | collective-permute-start | bytes 4325384 | tf_op jit(solution)/shard_map/ppermute | solution.py:900
  755.1 50.9 %collective-permute-start.47 = (bf16[256,2048]{1,0:T(8,128)(2,1)}, bf16[256,2048]{1,0:T(8,128)(2,1)}, u32[]{:S(2)}, u32[]{:S(2)}) collective-permute-start(bf16[256,2048]{1,0:T(8,128)(2,1)} %get-tuple-element.292), channel_id=1, source_target_pairs={{0,1},{1,0},{2,3},{3,2},{4,5},{5,4},{6,7},{7,6},{8,9},{9,8},{10,11... | collective-permute-start | bytes 3145736 | tf_op jit(solution)/shard_map/ppermute | solution.py:900
  755.9 44.6 %collective-permute-start.39 = (bf16[256,2048]{1,0:T(8,128)(2,1)}, bf16[256,2048]{1,0:T(8,128)(2,1)}, u32[]{:S(2)}, u32[]{:S(2)}) collective-permute-start(bf16[256,2048]{1,0:T(8,128)(2,1)} %get-tuple-element.475), channel_id=1, source_target_pairs={{0,2},{1,3},{2,0},{3,1},{4,6},{5,7},{6,4},{7,5},{8,10},{9,11},{10,... | collective-permute-start | bytes 3145736 | tf_op jit(solution)/shard_map/ppermute | solution.py:900
  787.6 60.3 %collective-permute-start.52 = (bf16[1408,512]{1,0:T(8,128)(2,1)}, bf16[1408,512]{1,0:T(8,128)(2,1)}, u32[]{:S(2)}, u32[]{:S(2)}) collective-permute-start(bf16[1408,512]{1,0:T(8,128)(2,1)} %get-tuple-element.308), channel_id=1, source_target_pairs={{0,8},{4,12},{8,0},{12,4},{1,9},{5,13},{9,1},{13,5},{2,10},{6,14},... | collective-permute-start | bytes 4325384 | tf_op jit(solution)/shard_map/ppermute | solution.py:900
  788.8 59.3 %collective-permute-start.51 = (bf16[704,1024]{1,0:T(8,128)(2,1)}, bf16[704,1024]{1,0:T(8,128)(2,1)}, u32[]{:S(2)}, u32[]{:S(2)}) collective-permute-start(bf16[704,1024]{1,0:T(8,128)(2,1)} %get-tuple-element.306), channel_id=1, source_target_pairs={{0,16},{16,0},{1,17},{17,1},{2,18},{18,2},{3,19},{19,3},{4,20},{20... | collective-permute-start | bytes 4325384 | tf_op jit(solution)/shard_map/ppermute | solution.py:900
  802.8 62.8 %collective-permute-start.53 = (bf16[704,1024]{1,0:T(8,128)(2,1)}, bf16[704,1024]{1,0:T(8,128)(2,1)}, u32[]{:S(2)}, u32[]{:S(2)}) collective-permute-start(bf16[704,1024]{1,0:T(8,128)(2,1)} %get-tuple-element.312), channel_id=1, source_target_pairs={{0,16},{16,0},{1,17},{17,1},{2,18},{18,2},{3,19},{19,3},{4,20},{20... | collective-permute-start | bytes 4325384 | tf_op jit(solution)/shard_map/ppermute | solution.py:900
  819.8 67.0 %collective-permute-start.58 = (bf16[512,1024]{1,0:T(8,128)(2,1)}, bf16[512,1024]{1,0:T(8,128)(2,1)}, u32[]{:S(2)}, u32[]{:S(2)}) collective-permute-start(bf16[512,1024]{1,0:T(8,128)(2,1)} %outer.26), channel_id=1, source_target_pairs={{0,4},{4,0},{8,12},{12,8},{1,5},{5,1},{9,13},{13,9},{2,6},{6,2},{1... | collective-permute-start | bytes 3145736 | tf_op jit(solution)/shard_map/ppermute | solution.py:900
  825.4 69.2 %collective-permute-start.54 = (bf16[1408,512]{1,0:T(8,128)(2,1)}, bf16[1408,512]{1,0:T(8,128)(2,1)}, u32[]{:S(2)}, u32[]{:S(2)}) collective-permute-start(bf16[1408,512]{1,0:T(8,128)(2,1)} %get-tuple-element.316), channel_id=1, source_target_pairs={{0,8},{4,12},{8,0},{12,4},{1,9},{5,13},{9,1},{13,5},{2,10},{6,14},... | collective-permute-start | bytes 4325384 | tf_op jit(solution)/shard_map/ppermute | solution.py:900
  847.9 65.8 %collective-permute-start.65 = (bf16[512,1024]{1,0:T(8,128)(2,1)}, bf16[512,1024]{1,0:T(8,128)(2,1)S(1)}, u32[]{:S(2)}, u32[]{:S(2)}) collective-permute-start(bf16[512,1024]{1,0:T(8,128)(2,1)} %outer.27), channel_id=1, source_target_pairs={{0,4},{4,0},{8,12},{12,8},{1,5},{5,1},{9,13},{13,9},{2,6},{6,2},{1... | collective-permute-start | bytes 3145736 | tf_op jit(solution)/shard_map/ppermute | solution.py:900
  865.1 40.7 %collective-permute-start.55 = (bf16[704,512]{1,0:T(8,128)(2,1)}, bf16[704,512]{1,0:T(8,128)(2,1)S(1)}, u32[]{:S(2)}, u32[]{:S(2)}) collective-permute-start(bf16[704,512]{1,0:T(8,128)(2,1)} %get-tuple-element.320), channel_id=1, source_target_pairs={{0,16},{16,0},{1,17},{17,1},{2,18},{18,2},{3,19},{19,3},{4,20},{20... | collective-permute-start | bytes 2162696 | tf_op jit(solution)/shard_map/ppermute | solution.py:900
  886.8 60.6 %collective-permute-start.59 = (bf16[1536,1024]{1,0:T(8,128)(2,1)}, bf16[1536,1024]{1,0:T(8,128)(2,1)}, u32[]{:S(2)}, u32[]{:S(2)}) collective-permute-start(bf16[1536,1024]{1,0:T(8,128)(2,1)} %outer.28), channel_id=1, source_target_pairs={{0,4},{4,0},{8,12},{12,8},{1,5},{5,1},{9,13},{13,9},{2,6},{6,2},{1... | collective-permute-start | bytes 9437192 | tf_op jit(solution)/shard_map/ppermute | solution.py:900
  913.7 64.9 %collective-permute-start.66 = (bf16[1536,1024]{1,0:T(8,128)(2,1)}, bf16[1536,1024]{1,0:T(8,128)(2,1)}, u32[]{:S(2)}, u32[]{:S(2)}) collective-permute-start(bf16[1536,1024]{1,0:T(8,128)(2,1)} %outer.31), channel_id=1, source_target_pairs={{0,4},{4,0},{8,12},{12,8},{1,5},{5,1},{9,13},{13,9},{2,6},{6,2},{1... | collective-permute-start | bytes 9437192 | tf_op jit(solution)/shard_map/ppermute | solution.py:900
  918.2 56.2 %collective-permute-start.63 = (bf16[704,512]{1,0:T(8,128)(2,1)}, bf16[704,512]{1,0:T(8,128)(2,1)}, u32[]{:S(2)}, u32[]{:S(2)}) collective-permute-start(bf16[704,512]{1,0:T(8,128)(2,1)} %get-tuple-element.339), channel_id=1, source_target_pairs={{0,16},{16,0},{1,17},{17,1},{2,18},{18,2},{3,19},{19,3},{4,20},{20... | collective-permute-start | bytes 2162696 | tf_op jit(solution)/shard_map/ppermute | solution.py:900
  944.7 41.0 %collective-permute-start.74 = (bf16[704,512]{1,0:T(8,128)(2,1)}, bf16[704,512]{1,0:T(8,128)(2,1)}, u32[]{:S(2)}, u32[]{:S(2)}) collective-permute-start(bf16[704,512]{1,0:T(8,128)(2,1)} %add_convert_fusion.12), channel_id=1, source_target_pairs={{0,2},{1,3},{2,0},{3,1},{4,6},{5,7},{6,4},{7,5},{8,10},{9,11},{10,... | collective-permute-start | bytes 2162696 | tf_op jit(solution)/shard_map/ppermute | solution.py:900
  953.0 65.8 %collective-permute-start.72 = (bf16[1536,512]{1,0:T(8,128)(2,1)}, bf16[1536,512]{1,0:T(8,128)(2,1)}, u32[]{:S(2)}, u32[]{:S(2)}) collective-permute-start(bf16[1536,512]{1,0:T(8,128)(2,1)} %outer.32), channel_id=1, source_target_pairs={{0,8},{4,12},{8,0},{12,4},{1,9},{5,13},{9,1},{13,5},{2,10},{6,14},... | collective-permute-start | bytes 4718600 | tf_op jit(solution)/shard_map/ppermute | solution.py:900
  974.1 25.2 %collective-permute-start.62 = (bf16[256,2048]{1,0:T(8,128)(2,1)}, bf16[256,2048]{1,0:T(8,128)(2,1)}, u32[]{:S(2)}, u32[]{:S(2)}) collective-permute-start(bf16[256,2048]{1,0:T(8,128)(2,1)} %get-tuple-element.337), channel_id=1, source_target_pairs={{0,1},{1,0},{2,3},{3,2},{4,5},{5,4},{6,7},{7,6},{8,9},{9,8},{10,11... | collective-permute-start | bytes 3145736 | tf_op jit(solution)/shard_map/ppermute | solution.py:900
  978.6 37.0 %collective-permute-start.70 = (bf16[704,512]{1,0:T(8,128)(2,1)}, bf16[704,512]{1,0:T(8,128)(2,1)}, u32[]{:S(2)}, u32[]{:S(2)}) collective-permute-start(bf16[704,512]{1,0:T(8,128)(2,1)} %get-tuple-element.350), channel_id=1, source_target_pairs={{0,16},{16,0},{1,17},{17,1},{2,18},{18,2},{3,19},{19,3},{4,20},{20... | collective-permute-start | bytes 2162696 | tf_op jit(solution)/shard_map/ppermute | solution.py:900
  985.7 67.1 %collective-permute-start.78 = (bf16[1536,512]{1,0:T(8,128)(2,1)}, bf16[1536,512]{1,0:T(8,128)(2,1)S(1)}, u32[]{:S(2)}, u32[]{:S(2)}) collective-permute-start(bf16[1536,512]{1,0:T(8,128)(2,1)} %outer.33), channel_id=1, source_target_pairs={{0,8},{4,12},{8,0},{12,4},{1,9},{5,13},{9,1},{13,5},{2,10},{6,14},... | collective-permute-start | bytes 4718600 | tf_op jit(solution)/shard_map/ppermute | solution.py:900
  993.9 35.5 %collective-permute-start.79 = (bf16[704,512]{1,0:T(8,128)(2,1)S(1)}, bf16[704,512]{1,0:T(8,128)(2,1)}, u32[]{:S(2)}, u32[]{:S(2)}) collective-permute-start(bf16[704,512]{1,0:T(8,128)(2,1)S(1)} %add_convert_fusion.11), channel_id=1, source_target_pairs={{0,16},{16,0},{1,17},{17,1},{2,18},{18,2},{3,19},{19,3},{4,20},{20... | collective-permute-start | bytes 2162696 | tf_op jit(solution)/shard_map/ppermute | solution.py:900
  1013.1 39.7 %collective-permute-start.69 = (bf16[256,2048]{1,0:T(8,128)(2,1)}, bf16[256,2048]{1,0:T(8,128)(2,1)}, u32[]{:S(2)}, u32[]{:S(2)}) collective-permute-start(bf16[256,2048]{1,0:T(8,128)(2,1)} %get-tuple-element.348), channel_id=1, source_target_pairs={{0,1},{1,0},{2,3},{3,2},{4,5},{5,4},{6,7},{7,6},{8,9},{9,8},{10,11... | collective-permute-start | bytes 3145736 | tf_op jit(solution)/shard_map/ppermute | solution.py:900
  1015.6 52.1 %collective-permute-start.75 = (bf16[704,512]{1,0:T(8,128)(2,1)}, bf16[704,512]{1,0:T(8,128)(2,1)}, u32[]{:S(2)}, u32[]{:S(2)}) collective-permute-start(bf16[704,512]{1,0:T(8,128)(2,1)} %add_convert_fusion.13), channel_id=1, source_target_pairs={{0,2},{1,3},{2,0},{3,1},{4,6},{5,7},{6,4},{7,5},{8,10},{9,11},{10,... | collective-permute-start | bytes 2162696 | tf_op jit(solution)/shard_map/ppermute | solution.py:900
  1028.1 32.6 %collective-permute-start.81 = (bf16[512,512]{1,0:T(8,128)(2,1)}, bf16[512,512]{1,0:T(8,128)(2,1)}, u32[]{:S(2)}, u32[]{:S(2)}) collective-permute-start(bf16[512,512]{1,0:T(8,128)(2,1)} %outer.35), channel_id=1, source_target_pairs={{0,8},{4,12},{8,0},{12,4},{1,9},{5,13},{9,1},{13,5},{2,10},{6,14},... | collective-permute-start | bytes 1572872 | tf_op jit(solution)/shard_map/ppermute | solution.py:900
  1029.3 34.6 %collective-permute-start.73 = (bf16[768,512]{1,0:T(8,128)(2,1)}, bf16[768,512]{1,0:T(8,128)(2,1)}, u32[]{:S(2)}, u32[]{:S(2)}) collective-permute-start(bf16[768,512]{1,0:T(8,128)(2,1)} %get-tuple-element.355), channel_id=1, source_target_pairs={{0,16},{16,0},{1,17},{17,1},{2,18},{18,2},{3,19},{19,3},{4,20},{20... | collective-permute-start | bytes 2359304 | tf_op jit(solution)/shard_map/ppermute | solution.py:900
  1060.0 30.4 %collective-permute-start.80 = (bf16[768,512]{1,0:T(8,128)(2,1)}, bf16[768,512]{1,0:T(8,128)(2,1)S(1)}, u32[]{:S(2)}, u32[]{:S(2)}) collective-permute-start(bf16[768,512]{1,0:T(8,128)(2,1)} %get-tuple-element.369), channel_id=1, source_target_pairs={{0,16},{16,0},{1,17},{17,1},{2,18},{18,2},{3,19},{19,3},{4,20},{20... | collective-permute-start | bytes 2359304 | tf_op jit(solution)/shard_map/ppermute | solution.py:900
  1067.7 35.1 %collective-permute-start.76 = (bf16[768,512]{1,0:T(8,128)(2,1)}, bf16[768,512]{1,0:T(8,128)(2,1)}, u32[]{:S(2)}, u32[]{:S(2)}) collective-permute-start(bf16[768,512]{1,0:T(8,128)(2,1)} %add_convert_fusion.7), channel_id=1, source_target_pairs={{0,2},{1,3},{2,0},{3,1},{4,6},{5,7},{6,4},{7,5},{8,10},{9,11},{10,... | collective-permute-start | bytes 2359304 | tf_op jit(solution)/shard_map/ppermute | solution.py:900
  1083.5 25.2 %collective-permute-start.89 = (bf16[704,512]{1,0:T(8,128)(2,1)S(1)}, bf16[704,512]{1,0:T(8,128)(2,1)}, u32[]{:S(2)}, u32[]{:S(2)}) collective-permute-start(bf16[704,512]{1,0:T(8,128)(2,1)S(1)} %add_convert_fusion.9), channel_id=1, source_target_pairs={{0,16},{16,0},{1,17},{17,1},{2,18},{18,2},{3,19},{19,3},{4,20},{20... | collective-permute-start | bytes 2162696 | tf_op jit(solution)/shard_map/ppermute | solution.py:900
  1106.1 47.3 %collective-permute-start.77 = (bf16[256,2048]{1,0:T(8,128)(2,1)}, bf16[256,2048]{1,0:T(8,128)(2,1)}, u32[]{:S(2)}, u32[]{:S(2)}) collective-permute-start(bf16[256,2048]{1,0:T(8,128)(2,1)} %add_convert_fusion.2), channel_id=1, source_target_pairs={{0,2},{1,3},{2,0},{3,1},{4,6},{5,7},{6,4},{7,5},{8,10},{9,11},{10,... | collective-permute-start | bytes 3145736 | tf_op jit(solution)/shard_map/ppermute | solution.py:900
  1153.4 33.2 %collective-permute-start.86 = (bf16[704,512]{1,0:T(8,128)(2,1)}, bf16[704,512]{1,0:T(8,128)(2,1)S(1)}, u32[]{:S(2)}, u32[]{:S(2)}) collective-permute-start(bf16[704,512]{1,0:T(8,128)(2,1)} %add_convert_fusion.10), channel_id=1, source_target_pairs={{0,2},{1,3},{2,0},{3,1},{4,6},{5,7},{6,4},{7,5},{8,10},{9,11},{10,... | collective-permute-start | bytes 2162696 | tf_op jit(solution)/shard_map/ppermute | solution.py:900
  (98 other events, 1978.7 us)

commit v2 on v1

--- a/solution.py
+++ b/solution.py
@@ -422,7 +422,7 @@
 
 
 def attend_back(
-    grad_context,
+    grad_contexts,
     qkv,
     log_totals,
     cos_table,
@@ -435,14 +435,15 @@
     head_dim,
 ):
     length = qkv.shape[0]
-    block = min(256, length)
+    block = min(256, length // 2)
     score_scale = head_dim ** (-0.5)
     half_dim = head_dim // 2
 
     def kernel(
         limit_ref,
         qkv_ref,
-        grad_ref,
+        grad_first,
+        grad_second,
         lse_ref,
         cos_ref,
         sin_ref,
@@ -461,7 +462,9 @@
         for start in range(0, length, block):
             rows = slice(start, start + block)
             query_block = qkv_ref[rows, :head_dim]
-            grad_block = grad_ref[rows, :]
+            grad_ref = grad_first if start < length // 2 else grad_second
+            shift = start % (length // 2)
+            grad_block = grad_ref[shift : shift + block, :]
             scores = (
                 lax.dot_general(
                     key_bf,
@@ -526,7 +529,8 @@
             grid=(heads,),
             in_specs=[
                 pl.BlockSpec((length, 3 * head_dim), lambda h, lim: (0, h)),
-                pl.BlockSpec((length, head_dim), lambda h, lim: (0, h + first)),
+                pl.BlockSpec((length // 2, head_dim), lambda h, lim: (0, h + first)),
+                pl.BlockSpec((length // 2, head_dim), lambda h, lim: (0, h + first)),
                 pl.BlockSpec((1, 1, length), lambda h, lim: (h, 0, 0)),
                 pl.BlockSpec((length, head_dim), fixed),
                 pl.BlockSpec((length, head_dim), fixed),
@@ -546,7 +550,7 @@
         compiler_params=pltpu.CompilerParams(vmem_limit_bytes=48 * 1024 * 1024),
         cost_estimate=paced(10 * heads * length * length * head_dim),
         name="attend_back",
-    )(limit, qkv, grad_context, log_totals, cos_table, sin_table, key_pos, query_pos)
+    )(limit, qkv, *grad_contexts, log_totals, cos_table, sin_table, key_pos, query_pos)
 
 
 def transposed_dot(left, right):
@@ -596,23 +600,6 @@
     )(*[array for array, _ in parts], *given)
 
 
-def pack(arrays):
-    total = sum(array.shape[0] for array in arrays)
-
-    def kernel(*refs):
-        row = 0
-        for ref in refs[:-1]:
-            refs[-1][row : row + ref.shape[0]] = ref[...]
-            row += ref.shape[0]
-
-    return pl.pallas_call(
-        kernel,
-        out_shape=jax.ShapeDtypeStruct((total, 128), arrays[0].dtype),
-        cost_estimate=paced(1),
-        name="pack",
-    )(*arrays)
-
-
 def block_of(count, sizes=(512, 256, 128)):
     for size in sizes:
         if count % size == 0:
@@ -621,15 +608,22 @@
 
 
 class Weight:
-    def __init__(self, arrays, start, count):
-        self.arrays = arrays
-        self.start = start
+    def __init__(self, arrays, count):
+        self.arrays = [array for array, _ in arrays]
+        self.starts = [start for _, start in arrays]
         self.count = count
-        self.part = arrays[0].shape[1]
+        self.part = self.arrays[0].shape[1]
         self.width = 4 * self.part
 
+    def rows(self, first, count):
+        moved = [start + first for start in self.starts]
+        return Weight(list(zip(self.arrays, moved)), count)
+
     def row_specs(self, block):
-        return [pl.BlockSpec((block, self.part), lambda j: (self.start // block + j, 0))] * 4
+        def spec(start):
+            return pl.BlockSpec((block, self.part), lambda j: (start // block + j, 0))
+
+        return [spec(start) for start in self.starts]
 
 
 def project_block(rows_ref, weight_refs):
@@ -641,36 +635,58 @@
     return total
 
 
-def project(rows, weight, bias, kind):
-    count, width = rows.shape
+def gather_rows(piece_refs, rows_ref):
+    @pl.when(pl.program_id(0) == 0)
+    def _():
+        row = 0
+        for ref in piece_refs:
+            rows_ref[row : row + ref.shape[0]] = ref[...]
+            row += ref.shape[0]
+
+
+def piece_specs(pieces):
+    return [pl.BlockSpec(piece.shape, lambda j: (0, 0)) for piece in pieces]
+
+
+def project(pieces, weight, bias, kind):
+    width = pieces[0].shape[1]
+    count = sum(piece.shape[0] for piece in pieces)
     features = weight.count
     block = block_of(features)
-
-    def kernel(rows_ref, w0, w1, w2, w3, bias_ref, out_ref):
+    given = len(pieces)
+
+    def kernel(*refs):
+        gather_rows(refs[:given], refs[-1])
+        w0, w1, w2, w3, bias_ref, out_ref, rows_ref = refs[given:]
         result = project_block(rows_ref, (w0, w1, w2, w3))
         out_ref[...] = (result + bias_ref[...]).astype(kind)
 
     return pl.pallas_call(
         kernel,
         grid=(features // block,),
-        in_specs=[pl.BlockSpec((count, width), lambda j: (0, 0))]
+        in_specs=piece_specs(pieces)
         + weight.row_specs(block)
         + [pl.BlockSpec((1, block), lambda j: (0, j))],
         out_specs=pl.BlockSpec((count, block), lambda j: (0, j)),
         out_shape=jax.ShapeDtypeStruct((count, features), kind),
+        scratch_shapes=[pltpu.VMEM((count, width), jnp.bfloat16)],
         compiler_params=pltpu.CompilerParams(vmem_limit_bytes=VMEM_BYTES),
         cost_estimate=paced(2 * count * width * features),
         name="project",
-    )(rows, *weight.arrays, bias)
-
-
-def ff_forward(rows, gate_weight, upper_weight, bias_gate, bias_upper):
-    count, width = rows.shape
+    )(*pieces, *weight.arrays, bias)
+
+
+def ff_forward(pieces, gate_weight, upper_weight, bias_gate, bias_upper):
+    width = pieces[0].shape[1]
+    count = sum(piece.shape[0] for piece in pieces)
     features = gate_weight.count
     block = block_of(features)
-
-    def kernel(rows_ref, *refs):
-        bg_ref, bu_ref, gate_ref, upper_ref, hid_ref = refs[8:]
+    given = len(pieces)
+
+    def kernel(*refs):
+        gather_rows(refs[:given], refs[-1])
+        refs = refs[given:]
+        bg_ref, bu_ref, gate_ref, upper_ref, hid_ref, rows_ref = refs[8:]
         gate = project_block(rows_ref, refs[:4]) + bg_ref[...]
         upper = project_block(rows_ref, refs[4:8]) + bu_ref[...]
         gate_ref[...] = gate.astype(jnp.bfloat16)
@@ -681,25 +697,30 @@
     return pl.pallas_call(
         kernel,
         grid=(features // block,),
-        in_specs=[pl.BlockSpec((count, width), lambda j: (0, 0))]
+        in_specs=piece_specs(pieces)
         + gate_weight.row_specs(block)
         + upper_weight.row_specs(block)
         + [pl.BlockSpec((1, block), lambda j: (0, j))] * 2,
         out_specs=[pl.BlockSpec((count, block), lambda j: (0, j))] * 3,
         out_shape=[out, out, out],
+        scratch_shapes=[pltpu.VMEM((count, width), jnp.bfloat16)],
         compiler_params=pltpu.CompilerParams(vmem_limit_bytes=VMEM_BYTES),
         cost_estimate=paced(4 * count * width * features),
         name="ff_forward",
-    )(rows, *gate_weight.arrays, *upper_weight.arrays, bias_gate, bias_upper)
-
-
-def ff_back(rows, down_weight, gate, upper):
-    count, width = rows.shape
+    )(*pieces, *gate_weight.arrays, *upper_weight.arrays, bias_gate, bias_upper)
+
+
+def ff_back(pieces, down_weight, gate, upper):
+    width = pieces[0].shape[1]
+    count = sum(piece.shape[0] for piece in pieces)
     features = down_weight.count
     block = block_of(features)
     factor = (2.0 / math.pi) ** 0.5
-
-    def kernel(rows_ref, w0, w1, w2, w3, gate_ref, upper_ref, gg_ref, gu_ref, sg_ref, su_ref):
+    given = len(pieces)
+
+    def kernel(*refs):
+        gather_rows(refs[:given], refs[-1])
+        w0, w1, w2, w3, gate_ref, upper_ref, gg_ref, gu_ref, sg_ref, su_ref, rows_ref = refs[given:]
         grad = project_block(rows_ref, (w0, w1, w2, w3))
         value = gate_ref[...].astype(jnp.float32)
         square = value * value
@@ -720,20 +741,21 @@
     return pl.pallas_call(
         kernel,
         grid=(features // block,),
-        in_specs=[pl.BlockSpec((count, width), lambda j: (0, 0))]
+        in_specs=piece_specs(pieces)
         + down_weight.row_specs(block)
         + [pl.BlockSpec((count, block), lambda j: (0, j))] * 2,
         out_specs=[pl.BlockSpec((count, block), lambda j: (0, j))] * 2
         + [pl.BlockSpec((1, block), lambda j: (0, j))] * 2,
         out_shape=[out, out, row, row],
+        scratch_shapes=[pltpu.VMEM((count, width), jnp.bfloat16)],
         compiler_params=pltpu.CompilerParams(vmem_limit_bytes=VMEM_BYTES),
         cost_estimate=paced(3 * count * width * features),
         name="ff_back",
-    )(rows, *down_weight.arrays, gate, upper)
+    )(*pieces, *down_weight.arrays, gate, upper)
 
 
 def expand(*pairs):
-    count = pairs[0][0].shape[0]
+    count = pairs[0][0][2]
     width = pairs[0][1].width
     part = width // 4
     own = count // 2
@@ -761,13 +783,19 @@
     def column(weight, which):
         return pl.BlockSpec(
             (weight.count, block),
-            lambda j: (weight.start // weight.count, jnp.clip(j - cuts * which, 0, cuts - 1)),
+            lambda j: (
+                weight.starts[which] // weight.count,
+                jnp.clip(j - cuts * which, 0, cuts - 1),
+            ),
         )
 
     specs = []
     operands = []
-    for features, weight in pairs:
-        specs.append(pl.BlockSpec((count, weight.count), lambda j: (0, 0)))
+    def row_block(depth, row):
+        return pl.BlockSpec((count, depth), lambda j: (row, 0))
+
+    for (features, row, _), weight in pairs:
+        specs.append(row_block(weight.count, row))
         specs += [column(weight, which) for which in range(4)]
         operands += [features, *weight.arrays]
     return pl.pallas_call(
@@ -787,21 +815,24 @@
 
 def outer(features, rights, start, columns, parts, added=(), pieces=(), steps=2):
     chunks = len(features)
-    count = rights[0][2]
+    count = features[0][2]
+    given = len(rights)
     total = features[0][0].shape[1]
     block = total // steps
     rows = total // parts
 
     def kernel(*refs):
+        gather_rows(refs[chunks : chunks + given], refs[-1])
         result = None
         for chunk in range(chunks):
-            product = rows_outer(refs[chunk][...], refs[chunks + chunk][...])
+            rows_here = refs[-1][chunk * count : (chunk + 1) * count]
+            product = rows_outer(refs[chunk][...], rows_here)
             result = product if result is None else result + product
-        first = 2 * chunks
+        first = chunks + given
         for ref in refs[first : first + len(added)]:
             result = result + ref[...].astype(jnp.float32)
         first += len(added)
-        outs = refs[first + len(pieces) :]
+        outs = refs[first + len(pieces) : -1]
         if parts == 1:
             outs[0][...] = result.astype(jnp.bfloat16)
             return
@@ -834,17 +865,18 @@
         kernel,
         grid=(steps,),
         in_specs=[pl.BlockSpec((count, block), across(row)) for _, row, _ in features]
-        + [pl.BlockSpec((count, columns), at(row, start // columns)) for _, row, _ in rights]
+        + [pl.BlockSpec((right.shape[0], columns), at(0, start // columns)) for right in rights]
         + [pl.BlockSpec((block, columns), along(column // columns)) for _, column in added]
         + [pl.BlockSpec((block, columns), at(0, 0))] * len(pieces),
         out_specs=out_specs,
         out_shape=[jax.ShapeDtypeStruct((rows, columns), jnp.bfloat16)] * parts,
+        scratch_shapes=[pltpu.VMEM((chunks * count, columns), jnp.bfloat16)],
         compiler_params=pltpu.CompilerParams(vmem_limit_bytes=VMEM_BYTES),
-        cost_estimate=paced(3 * chunks * count * total * columns),
+        cost_estimate=paced(6 * chunks * count * total * columns),
         name="outer",
     )(
         *[array for array, _, _ in features],
-        *[array for array, _, _ in rights],
+        *rights,
         *[array for array, _ in added],
         *pieces,
     )
@@ -890,26 +922,21 @@
     layer = lax.axis_index("tensor")
     item_slot = layer >> 1
 
-    def along(axis, step, depth=2):
+    def along(axis, step):
         moves = [(i, i ^ step) for i in range(lax.axis_size(axis))]
-        sent = []
-
-        def move(values):
-            if len(sent) >= depth:
-                values = after(values, sent[-depth])
-            sent.append(lax.ppermute(values, axis, moves))
-            return sent[-1]
+
+        def move(values, gate=()):
+            if gate:
+                values = after(values, *gate)
+            return lax.ppermute(values, axis, moves)
 
         return move
 
     over_x = along("obj", 1)
     over_y = along("dp", 2)
     over_core = along("dp", 1)
-    swap = along("tensor", 1, 1)
-    over_far = along("tensor", 2, 1)
-    back_x = along("obj", 1, 2)
-    back_y = along("dp", 2, 2)
-    back_far = along("tensor", 2, 1)
+    swap = along("tensor", 1)
+    over_far = along("tensor", 2)
 
     def to_local(values):
         parts = [
@@ -926,14 +953,14 @@
             parts.append(lax.dynamic_slice_in_dim(values, at * block_width, block_width, -1))
         return jnp.concatenate(parts, axis=-1)
 
-    def away(values):
+    def away(values, gate=()):
         stays = lax.dynamic_index_in_dim(values, item_slot, 0, keepdims=False)
         leaves = lax.dynamic_index_in_dim(values, 1 - item_slot, 0, keepdims=False)
-        return [stays, over_far(leaves)]
-
-    def home(values):
+        return [stays, over_far(leaves, gate)]
+
+    def home(values, gate=()):
         stays, leaves = values
-        came = back_far(leaves)
+        came = over_far(leaves, gate)
         first = jnp.where(item_slot == 0, stays, came)
         second = jnp.where(item_slot == 0, came, stays)
         return from_local(jnp.stack([first, second])), came
@@ -967,50 +994,48 @@
             self.rest = jnp.concatenate([half[1] for half in halves], axis=0)
             self.counts = [half[0].shape[0] for half in halves]
 
-        def to_far(self):
-            self.far = over_far(self.mine)
-
-        def far_to_y(self):
-            self.far_y = over_y(self.far)
-
-        def far_to_x(self):
-            self.other_far = over_x(self.far)
-
-        def both_to_x(self):
-            self.other_far_y = over_x(self.far_y)
-
-        def joined(self, parts, wait):
-            total = 4 * sum(self.counts)
+        def to_far(self, gate=()):
+            self.far = over_far(self.mine, gate)
+
+        def far_to_y(self, gate=()):
+            self.far_y = over_y(self.far, gate)
+
+        def far_to_x(self, gate=()):
+            self.other_far = over_x(self.far, gate)
+
+        def both_to_x(self, gate=()):
+            self.other_far_y = over_x(self.far_y, gate)
+
+        def blocks(self, wait=(), wait_next=()):
+            near = [(self.mine, 0), (self.rest, 0), (self.far, 0), (self.other_far, 0)]
+            next_y = [self.near_y, self.other_y, (self.far_y, 0), (self.other_far_y, 0)]
+            total = 8 * sum(self.counts)
             target = None
-            first = 0
-            for count in self.counts:
-                rest = [(array, start + first) for array, start in parts[1:]]
-                target = turn(
-                    lambda array: join(
-                        [(array, parts[0][1] + first)] + rest, count, target, total, 4 * first
-                    ),
-                    parts[0][0],
-                    wait=wait,
-                )
-                first += count
-            return target
-
-        def blocks(self, wait=()):
-            near = self.joined(
-                [(self.mine, 0), (self.rest, 0), (self.far, 0), (self.other_far, 0)], wait
-            )
-            next_y = self.joined(
-                [self.near_y, self.other_y, (self.far_y, 0), (self.other_far_y, 0)], ()
-            )
-            self.near = near, over_core(near)
-            self.next = next_y, over_core(next_y)
+            for half, parts in enumerate((near, next_y)):
+                first = 0
+                for count in self.counts:
+                    rest = [(array, start + first) for array, start in parts[1:]]
+                    target = turn(
+                        lambda array: join(
+                            [(array, parts[0][1] + first)] + rest,
+                            count,
+                            target,
+                            total,
+                            8 * first + 4 * half * count,
+                        ),
+                        parts[0][0],
+                        wait=(wait, wait_next)[half],
+                    )
+                    first += count
+            self.joined = target, over_core(target)
 
         def weights(self):
-            arrays = (self.near[0], self.next[0], self.near[1], self.next[1])
             first = 0
             result = []
             for count in self.counts:
-                result.append(Weight(arrays, 4 * first, 4 * count))
+                starts = (8 * first, 8 * first + 4 * count)
+                arrays = [(array, start) for array in self.joined for start in starts]
+                result.append(Weight(arrays, 4 * count))
                 first += count
             return result
 
@@ -1037,37 +1062,23 @@
             sent = self.part(
                 block_width, block_width, 2, added=[(self.came, block_width)], wait=wait
             )
-            far = back_y(sent[1])
-            self.came_y = [back_y(sent[0]), far]
+            far = over_y(sent[1])
+            self.came_y = [over_y(sent[0]), far]
 
         def to_x(self, wait=()):
             near, near_sent, far, far_sent = self.part(
                 0, block_width, 4, added=[(self.came, 0)], pieces=self.came_y, wait=wait
             )
-            self.far = (far, back_x(far_sent))
-            self.near = (near, back_x(near_sent))
-
-        def to_x_first(self, wait=()):
-            near, near_sent, far, far_sent = self.part(
-                0, 2 * block_width, 4, added=[(self.came, 0)], wait=wait
-            )
-            self.wide_far = (far, back_x(far_sent))
-            self.wide_near = (near, back_x(near_sent))
-
-        def to_y_next(self):
-            def onward(pair):
-                summed = add(*pair)
-                return summed[:, :block_width], back_y(summed[:, block_width:])
-
-            self.far = onward(self.wide_far)
-            self.near = onward(self.wide_near)
-
-        def to_far(self):
-            self.came_far = back_far(add(*self.far))
+            self.far = (far, over_x(far_sent))
+            self.near = (near, over_x(near_sent))
+
+        def to_far(self, gate=()):
+            self.came_far = over_far(add(*self.far), gate)
 
         def finish(self):
             self.mine = add(*self.near, self.came_far)
-            return sides(self.mine, back_x(self.mine)).astype(wide)
+            self.other = over_x(self.mine)
+            return sides(self.mine, self.other).astype(wide)
 
     class HalfReduction:
         def __init__(self, features, rights):
@@ -1096,13 +1107,13 @@
             (sent,) = self.part(
                 block_width, block_width, 1, added=[(self.came, block_width)], wait=wait
             )
-            self.came_y = back_y(sent)
+            self.came_y = over_y(sent)
 
         def to_x(self, wait=()):
             kept, sent = self.part(
                 0, block_width, 2, added=[(self.came, 0), (self.came_y, 0)], wait=wait
             )
-            self.pair = (kept, back_x(sent))
+            self.pair = (kept, over_x(sent))
 
     def add(*values):
         total = values[0].astype(wide)
@@ -1168,36 +1179,39 @@
     third = Gathering(up_rows[1])
     late = Gathering(w_down)
 
-    early.to_far()
+    early.to_far((far_bias,))
     early_y = over_y(early.mine)
     leaving = to_local(tokens[0])
     stays = lax.dynamic_index_in_dim(leaving, item_slot, 0, keepdims=False)
     came_tokens = [swap(stays)]
-    others = (middle, third, late)
-    others_y = over_y(jnp.concatenate([part.mine for part in others], axis=0))
     early_other_y = over_x(early_y)
     early.near_y = early_y, 0
     early.other_y = early_other_y, 0
-    early.far = after(early.far, came_tokens[0], early_other_y)
-    own_tokens = away(leaving)
+    others = (middle, third)
+    others_mine = jnp.concatenate([part.mine for part in others], axis=0)
+    early.far = after(early.far, early_other_y, others_mine, stays, late.mine)
     early.far_to_y()
     early.far_to_x()
-    middle.to_far()
     early.both_to_x()
-    early.blocks(wait=(own_tokens[1],))
+    own_tokens = away(leaving, (early.far,))
+    others_y = over_y(others_mine, (early.far,))
     came_tokens.append(swap(own_tokens[1]))
-    others_other_y = over_x(others_y)
+    early.blocks(wait=(came_tokens[0],), wait_next=(own_tokens[1], others_y))
+    middle.to_far((came_tokens[1],))
+    others_other_y = over_x(others_y, latest)
+    late_y = over_y(late.mine, latest)
     first_row = 0
     for part in others:
         part.near_y = others_y, first_row
         part.other_y = others_other_y, first_row
         first_row += part.counts[0]
-    third.to_far()
     full_qkv, full_dense = early.weights()
-    token_rows = jnp.concatenate(
-        [part for i in range(CHUNKS) for part in (own_tokens[i], came_tokens[i])], axis=0
-    )
-    projected = turn(project, token_rows, full_qkv, bias_qkv, jnp.float32)
+    token_rows = [part for i in range(CHUNKS) for part in (own_tokens[i], came_tokens[i])]
+
+    def turn_rows(work, pieces, *rest, wait=()):
+        return turn(lambda first: work([first] + pieces[1:], *rest), pieces[0], wait=wait)
+
+    projected = turn_rows(project, token_rows, full_qkv, bias_qkv, jnp.float32)
 
     def attend_heads(first, wait):
         return turn(
@@ -1214,19 +1228,21 @@
             wait=wait,
         )
 
-    middle.far_to_y()
-    middle.far_to_x()
-    near_heads = attend_heads(0, (others_other_y,))
-    late.to_far()
-    far_heads = attend_heads(shard_heads, (middle.far_y, middle.other_far))
-    middle.both_to_x()
-    third.far_to_y()
-    third.far_to_x()
+    third.to_far((projected,))
+    near_heads = attend_heads(0, (late_y,))
+    late_other_y = over_x(late_y, latest)
+    late.near_y = late_y, 0
+    late.other_y = late_other_y, 0
+    middle.far_to_y(latest)
+    middle.far_to_x(latest)
+    far_heads = attend_heads(shard_heads, (others_other_y, middle.far))
+    middle.both_to_x(latest)
+    late.to_far(latest)
 
     step = 2 * share_rows
     half_heads = shard_heads * head_dim
-    dense_near = Weight(full_dense.arrays, full_dense.start, half_heads)
-    dense_far = Weight(full_dense.arrays, full_dense.start + half_heads, half_heads)
+    dense_near = full_dense.rows(0, half_heads)
+    dense_far = full_dense.rows(half_heads, half_heads)
     states = [dict() for _ in range(CHUNKS)]
 
     def normalize(values):
@@ -1243,22 +1259,22 @@
         )
 
     for i, state in enumerate(states):
-        rows = slice(i * step, (i + 1) * step)
         own, other = turn(
-            lambda n, f: expand((n, dense_near), (f, dense_far)),
-            near_heads[0][rows],
-            far_heads[0][rows],
-            wait=(middle.other_far_y, third.far) if i == 0 else (),
+            lambda n, f: expand(((n, i, step), dense_near), ((f, i, step), dense_far)),
+            near_heads[0],
+            far_heads[0],
+            wait=(middle.far_y, middle.other_far)
+            if i == 0
+            else (middle.other_far_y,),
         )
         state["dense"] = own, swap(other)
-    third.both_to_x()
-    middle.blocks(wait=(third.far_y, third.other_far, late.far))
-    late.far_to_y()
-    late.far_to_x()
-    late.both_to_x()
-    own_cotangent = away(to_local(masked))
+    third.far_to_y(latest)
+    third.far_to_x(latest)
+    third.both_to_x(latest)
     for i, state in enumerate(states):
         own, came = state["dense"]
+        if i:
+            came = after(came, states[0]["norm_bf"])
         attn = own + came.astype(wide) + bias_dense
         first = ALPHA * own_tokens[i].astype(wide) + attn
         normal, scale = normalize(first)
@@ -1266,12 +1282,23 @@
         norm_bf = norm_one.astype(narrow)
         state["one"] = normal, scale, norm_one
         state["norm_bf"] = norm_bf
-        state["norm_rows"] = jnp.concatenate([norm_bf, swap(norm_bf)], axis=0)
-    third.blocks(wait=[s["norm_bf"] for s in states] + [late.far_y, late.other_far])
+        state["came_norm"] = swap(norm_bf, (states[0]["came_norm"],) if i else ())
+        state["norm_rows"] = [norm_bf, state["came_norm"]]
+    middle.blocks(
+        wait=[s["norm_bf"] for s in states]
+        + [states[0]["came_norm"], third.far_y, third.other_far, late.far, late_other_y]
+    )
+    late.far_to_y((states[1]["norm_bf"],))
+    late.far_to_x((states[1]["norm_bf"],))
+    late.both_to_x(latest)
+    own_cotangent = away(to_local(masked), latest)
+    third.blocks()
     (full_gate,) = middle.weights()
     (full_upper,) = third.weights()
+    late.blocks(wait=(states[1]["came_norm"],))
+    (full_down,) = late.weights()
     for i, state in enumerate(states):
-        state["ff"] = turn(
+        state["ff"] = turn_rows(
             ff_forward,
             state["norm_rows"],
             full_gate,
@@ -1280,13 +1307,15 @@
             bias_upper,
             wait=(own_cotangent[1],) if i == 1 else (),
         )
-    late.blocks()
-    (full_down,) = late.weights()
-    for state in states:
-        own, other = turn(lambda r: expand((r, full_down)), state["ff"][2])
+        own, other = turn(
+            lambda r: expand(((r, 0, step), full_down)),
+            state["ff"][2],
+        )
         state["down"] = own, swap(other)
     for i, state in enumerate(states):
         own, came = state["down"]
+        if i:
+            came = after(came, states[0]["grad_mlp"])
         mlp = own + came.astype(wide) + bias_down
         normal, scale = normalize(ALPHA * state["one"][2] + mlp)
         state["out"] = (normal * gain_two + shift_two).astype(narrow)
@@ -1294,24 +1323,24 @@
         grad_second = normalize_back(grad_out, gain_two, normal, scale)
         grad_mlp = grad_second.astype(narrow)
         state["second"] = grad_second
-        state["came_mlp"] = swap(grad_mlp)
-        state["mlp_rows"] = jnp.concatenate([grad_mlp, state["came_mlp"]], axis=0)
+        state["grad_mlp"] = grad_mlp
+        state["came_mlp"] = swap(grad_mlp, (states[0]["came_mlp"],) if i else ())
+        state["mlp_rows"] = [grad_mlp, state["came_mlp"]]
         state["vectors_two"] = (
             jnp.sum(grad_mlp.astype(wide), axis=0),
             jnp.sum(grad_out * normal, axis=0),
             jnp.sum(grad_out, axis=0),
         )
 
-    layer_out, sent_out = home([s["out"] for s in states])
 
     def back_ff(state, wait=()):
-        state["back"] = turn(
+        state["back"] = turn_rows(
             ff_back, state["mlp_rows"], full_down, state["ff"][0], state["ff"][1], wait=wait
         )
 
     def back_up(state, wait=()):
         own, other = turn(
-            lambda g, u: expand((g, full_gate), (u, full_upper)),
+            lambda g, u: expand(((g, 0, step), full_gate), ((u, 0, step), full_upper)),
             state["back"][0],
             state["back"][1],
             wait=wait,
@@ -1327,7 +1356,7 @@
         state["first"] = grad_first
         state["grad_attn"] = grad_attn
         state["came_attn"] = swap(grad_attn)
-        state["attn_rows"] = jnp.concatenate([grad_attn, state["came_attn"]], axis=0)
+        state["attn_rows"] = [grad_attn, state["came_attn"]]
         state["vectors_one"] = (
             jnp.sum(grad_attn.astype(wide), axis=0),
             jnp.sum(grad_norm * normal, axis=0),
@@ -1337,43 +1366,42 @@
     def chunks_of(pick):
         return [(pick(state), 0, step) for state in states]
 
-    back_ff(states[0])
+    def rows_of(name):
+        return [piece for state in states for piece in state[name]]
+
+    back_ff(states[0], wait=(states[1]["out"],))
     back_up(states[0], wait=(states[1]["came_mlp"],))
-    down = Reduction(chunks_of(lambda s: s["ff"][2]), chunks_of(lambda s: s["mlp_rows"]))
+    down = Reduction(chunks_of(lambda s: s["ff"][2]), rows_of("mlp_rows"))
     down.to_core()
     back_ff(states[1])
     down.to_y(wait=(states[0]["norm_grad"][1],))
     back_one(states[0])
     back_up(states[1], wait=(states[0]["grad_attn"],))
-    norm_all = chunks_of(lambda s: s["norm_rows"])
+    norm_all = rows_of("norm_rows")
     gate = Reduction(chunks_of(lambda s: s["back"][0]), norm_all)
     upper = Reduction(chunks_of(lambda s: s["back"][1]), norm_all)
-    gate.to_core(wait=(states[0]["came_attn"],))
-    upper.to_core(wait=(down.came_y[1],))
+    gate.to_core()
+    layer_out, sent_out = home([s["out"] for s in states], latest)
+    upper.to_core()
     back_one(states[1])
     zero_row = jnp.zeros((1, heads * head_dim), wide)
 
     def back_dense(state, wait=()):
-        return turn(project, state["attn_rows"], full_dense, zero_row, narrow, wait=wait)
+        return turn_rows(project, state["attn_rows"], full_dense, zero_row, narrow, wait=wait)
 
     context_grads = [back_dense(states[0], wait=(states[1]["norm_grad"][1],))]
-    upper.to_x_first(wait=(states[1]["grad_attn"],))
-    gate.to_y(wait=(down.came_y[0],))
-    context_grads.append(back_dense(states[1]))
+    gate.to_y(wait=(states[1]["grad_attn"],))
+    down.to_x()
     dense_grads = [
-        HalfReduction(
-            [(part[0], i, step) for i in range(CHUNKS)], chunks_of(lambda s: s["attn_rows"])
-        )
+        HalfReduction([(part[0], i, step) for i in range(CHUNKS)], rows_of("attn_rows"))
         for part in (near_heads, far_heads)
     ]
-    dense_grads[1].to_core(wait=(sent_out,))
-    dense_grads[0].to_core()
-    context_grad = jnp.concatenate(context_grads, axis=0)
+    context_grads.append(back_dense(states[1]))
 
     def back_heads(saved, first, wait=()):
-        return turn(
+        return turn_rows(
             attend_back,
-            context_grad,
+            context_grads,
             saved[1],
             saved[2],
             cos_table,
@@ -1391,13 +1419,12 @@
         return [(array, i, step) for i in range(CHUNKS)]
 
     grad_far, bias_far = back_heads(far_heads, shard_heads)
-    qkv_far = HalfReduction(both_chunks(grad_far), both_chunks(token_rows))
-    qkv_far.to_core(wait=(upper.wide_far[1], gate.came_y[1]))
-    down.to_x()
-    grad_near, bias_near = back_heads(near_heads, 0, wait=(upper.wide_near[1],))
-    upper.to_y_next()
-    qkv_near = HalfReduction(both_chunks(grad_near), both_chunks(token_rows))
-
+    qkv_far = HalfReduction(both_chunks(grad_far), token_rows)
+    qkv_far.to_core(wait=(gate.came_y[1], down.far[1], sent_out))
+    upper.to_y()
+    down.to_far()
+    grad_near, bias_near = back_heads(near_heads, 0, wait=(down.near[1],))
+    qkv_near = HalfReduction(both_chunks(grad_near), token_rows)
     grad_bias_qkv = jnp.concatenate([bias_near, bias_far], axis=0)
     grad_bias_gate = sum(s["back"][2] for s in states)
     grad_bias_upper = sum(s["back"][3] for s in states)
@@ -1417,52 +1444,36 @@
     ordered = jnp.zeros_like(stacked)
     for position in range(4):
         ordered = jnp.where(targets == position, stacked[:, position : position + 1], ordered)
-    def columns(values):
-        rows = values.reshape(-1, 128)
-        return jnp.pad(rows, ((0, -rows.shape[0] % 8), (0, 0)))
-
-    small = [
-        columns(ordered),
-        columns(spread(grad_bias_qkv)),
-        columns(spread(grad_bias_gate)),
-        columns(spread(grad_bias_upper)),
-    ]
-    packed = pack(small)
-    sums = [packed]
-    for axis, hop in (("obj", 1), ("dp", 1), ("dp", 2), ("tensor", 1), ("tensor", 2)):
-        moves = [(i, i ^ hop) for i in range(lax.axis_size(axis))]
-        sums.append(sums[-1] + lax.ppermute(sums[-1], axis, moves))
-
-    gate.to_x(wait=(gate.came_y[0],))
-    down.to_far()
-    qkv_near.to_core(wait=(down.far[1],))
-    qkv_far.to_y(wait=(upper.far[1], sums[1]))
+    vectors = (
+        ordered.reshape(6, width),
+        spread(grad_bias_qkv),
+        spread(grad_bias_gate),
+        spread(grad_bias_upper),
+    )
+    totals = lax.psum(vectors, ("obj", "dp", "tensor"))
+
+    gate.to_x(wait=(qkv_far.came,))
+    qkv_near.to_core(wait=(down.came_far,) + vectors)
+    qkv_far.to_y()
+    sum_down = down.finish()
     half_count = full_qkv.count // 2
-    weight_near = Weight(full_qkv.arrays, 0, half_count)
-    weight_far = Weight(full_qkv.arrays, half_count, half_count)
+    weight_near = full_qkv.rows(0, half_count)
+    weight_far = full_qkv.rows(half_count, half_count)
 
     def back_qkv(i, wait=()):
-        rows = slice(i * step, (i + 1) * step)
         own, other = turn(
-            lambda n, f: expand((n, weight_near), (f, weight_far)),
-            grad_near[rows],
-            grad_far[rows],
+            lambda n, f: expand(((n, i, step), weight_near), ((f, i, step), weight_far)),
+            grad_near,
+            grad_far,
             wait=wait,
         )
         states[i]["source"] = own, swap(other)
 
-    back_qkv(0, wait=(upper.near[1], sums[2]))
-    qkv_near.to_y(wait=(down.near[1], sums[3]))
-    sum_down = down.finish()
-    back_qkv(1, wait=(states[0]["source"][1], gate.far[1], sums[4]))
-    gate.to_far()
-    qkv_far.to_x(wait=(gate.near[1], sums[5]))
-    dense_grads[1].to_y()
-    dense_grads[0].to_y()
-    came_qkv = back_far(add(*qkv_far.pair))
-    qkv_near.to_x(wait=(states[1]["source"][1],))
-    dense_grads[1].to_x()
-    dense_grads[0].to_x()
+    back_qkv(1)
+    gate.to_far(latest)
+    qkv_near.to_y(wait=(upper.came_y[0], gate.near[1]))
+    back_qkv(0, wait=(down.other,))
+    upper.to_x(wait=(states[1]["source"][1],))
     grad_inputs, _ = home(
         [
             (s["source"][0] + s["source"][1].astype(wide) + ALPHA * s["first"]).astype(narrow)
@@ -1470,22 +1481,24 @@
         ]
     )
     grad_inputs = grad_inputs.astype(wide)
+    dense_grads[1].to_core(wait=(gate.came_far,))
+    dense_grads[0].to_core()
+    qkv_far.to_x(wait=(qkv_far.came_y, states[0]["source"][1]))
     sum_gate = gate.finish()
+    dense_grads[1].to_y()
+    dense_grads[0].to_y()
+    came_qkv = over_far(add(*qkv_far.pair))
     upper.to_far()
+    qkv_near.to_x(wait=(qkv_near.came_y,))
+    dense_grads[1].to_x()
+    dense_grads[0].to_x()
     mine_qkv = add(*qkv_near.pair, came_qkv)
-    sum_qkv = sides(mine_qkv, back_x(mine_qkv)).astype(wide)
-    came_dense = back_far(add(*dense_grads[1].pair))
+    sum_qkv = sides(mine_qkv, over_x(mine_qkv)).astype(wide)
     sum_upper = upper.finish()
+    came_dense = over_far(add(*dense_grads[1].pair))
     mine_dense = add(*dense_grads[0].pair, came_dense)
-    sum_dense = sides(mine_dense, back_x(mine_dense)).astype(wide)
-    norm_total = sums[-1][: small[0].shape[0]].reshape(6, width)
-    flat_totals = []
-    row = small[0].shape[0]
-    for part, count in zip(small[1:], (n_qkv, shard_hidden, shard_hidden)):
-        rows = sums[-1][row : row + count * n_tensor // 128]
-        flat_totals.append(rows.reshape(-1))
-        row += part.shape[0]
-    total_qkv, total_gate, total_upper = flat_totals
+    sum_dense = sides(mine_dense, over_x(mine_dense)).astype(wide)
+    norm_total, total_qkv, total_gate, total_upper = [after(t, mine_dense) for t in totals]
 
     def own_shard(total, count):
         return lax.dynamic_slice_in_dim(total, layer * count, count)

time: 1230 us -> 1100 us (0.89)
  waiting for transfers between devices: 476 us -> 378 us
  other arithmetic: 111 us -> 77.8 us
  starting transfers between devices: 95 us -> 76.5 us
  between operations: 5.77 us -> 19.4 us
    ppermute x90 -> x83, waiting for transfers between devices: 472 us -> 371 us  [move(): return lax.ppermute(values, axis, moves)]
    ppermute x90 -> x83, starting transfers between devices: 95 us -> 73.8 us  [move(): return lax.ppermute(values, axis, moves)]
    concatenate x9 -> x1, other arithmetic: 20.9 us -> 2.3 us  [pair_shards(): others_mine = jnp.concatenate([part.mine for part in others], axis=0)]
    unnamed x145 -> x195, local copies, waits for them, and re-layouts: 25.8 us -> 34.3 us
    pallas_call x20 -> x21, Pallas kernels: 141 us -> 146 us  [outer(): pl.pallas_call(kernel, grid=(steps,), in_specs=[pl.BlockSpec((count, bloc...]
    pallas_call x8 -> x7, Pallas kernels: 110 us -> 109 us  [the longest x2 42.4 us: ff_forward(): pl.pallas_call(kernel, grid=(features // block,), in_specs=piece_specs(pi...]
  transfers between devices with their start and end apart: 91 -> 85, of which waited for: 38 -> 33; matrix products, arithmetic and copies ran while one was open for 11% -> 10% of each run, Pallas kernels for 33% -> 35%
where the time goes in v2:
time: 1100 us; the launch traced here: 1090 us
  Pallas kernels  472 us (43%)
  waiting for transfers between devices  378 us (34%)
  other arithmetic  77.8 us (7%)
  starting transfers between devices  76.5 us (7%)
  local copies, waits for them, and re-layouts  63.7 us (6%)
  between operations  19.4 us (2%)
    ppermute x83, waiting for transfers between devices, move(): return lax.ppermute(values, axis, moves)  371 us
    pallas_call x21, Pallas kernels, outer(): pl.pallas_call(kernel, grid=(steps,), in_specs=[pl.BlockSpec((count, bloc...  146 us
    pallas_call x8, Pallas kernels, expand(): pl.pallas_call(kernel, grid=(4 * cuts,), in_specs=specs, out_specs=[pl.Bl...  110 us
    ppermute x83, starting transfers between devices, move(): return lax.ppermute(values, axis, moves)  73.8 us
    pallas_call x2, Pallas kernels, ff_forward(): pl.pallas_call(kernel, grid=(features // block,), in_specs=piece_specs(pi...  42.4 us
    pallas_call x2, Pallas kernels, attend_back(): pl.pallas_call(kernel, grid_spec=pltpu.PrefetchScalarGridSpec(num_scalar_...  38.9 us
    pallas_call x10, Pallas kernels, join(): pl.pallas_call(kernel, grid=(steps, 4), in_specs=[source(first) for _, fi...  37.2 us
    pallas_call x2, Pallas kernels, ff_back(): pl.pallas_call(kernel, grid=(features // block,), in_specs=piece_specs(pi...  34.9 us
  transfers between devices with their start and end apart: 85, of which 33 were waited for; matrix products, arithmetic and copies ran while one was open for 10% of the time, Pallas kernels for 35%

profile of v2, /device:TPU:0, one launch (start us, length us, event | category | flops | bytes accessed | tf_op | source)
XLA Modules:
  0.0 1086.7 jit_solution(2593756890727369196)
XLA Ops:
  22.7 14.6 %collective-permute-done.refs_0_ = bf16[1024,512]{1,0:T(8,128)(2,1)S(1)} collective-permute-done((bf16[1024,512]{1,0:T(8,128)(2,1)S(1)}, bf16[1024,512]{1,0:T(8,128)(2,1)S(1)}, u32[]{:S(2)}, u32[]{:S(2)}) %collective-permute-start) | collective-permute-done | bytes 1048608 | tf_op jit(solution)/shard_map/ppermute | solution.py:931
  49.6 20.5 %collective-permute-done.3.refs_2_ = bf16[1024,512]{1,0:T(8,128)(2,1)} collective-permute-done((bf16[1024,512]{1,0:T(8,128)(2,1)S(1)}, bf16[1024,512]{1,0:T(8,128)(2,1)}, u32[]{:S(2)}, u32[]{:S(2)}) %collective-permute-start.3) | collective-permute-done | bytes 1048608 | tf_op jit(solution)/shard_map/ppermute | solution.py:931
  75.5 21.0 %collective-permute-done.8.refs_2_ = bf16[1024,512]{1,0:T(8,128)(2,1)S(1)} collective-permute-done((bf16[1024,512]{1,0:T(8,128)(2,1)}, bf16[1024,512]{1,0:T(8,128)(2,1)S(1)}, u32[]{:S(2)}, u32[]{:S(2)}) %collective-permute-start.8) | collective-permute-done | bytes 1048608 | tf_op jit(solution)/shard_map/ppermute | solution.py:931
  99.0 17.4 %collective-permute-done.1.refs_1_.refs_3_ = bf16[256,2048]{1,0:T(8,128)(2,1)S(1)} collective-permute-done((bf16[256,2048]{1,0:T(8,128)(2,1)S(1)}, bf16[256,2048]{1,0:T(8,128)(2,1)S(1)}, u32[]{:S(2)}, u32[]{:S(2)}) %collective-permute-start.1) | collective-permute-done | bytes 1048608 | tf_op jit(solution)/shard_map/ppermute | solution.py:931
  139.2 19.2 %collective-permute-done.10.refs_3_.refs_5_ = bf16[256,2048]{1,0:T(8,128)(2,1)S(1)} collective-permute-done((bf16[256,2048]{1,0:T(8,128)(2,1)S(1)}, bf16[256,2048]{1,0:T(8,128)(2,1)S(1)}, u32[]{:S(2)}, u32[]{:S(2)}) %collective-permute-start.10) | collective-permute-done | bytes 1048608 | tf_op jit(solution)/shard_map/ppermute | solution.py:931
  159.6 19.2 %project.3.proj_ref = f32[1024,3072]{1,0:T(8,128)} custom-call(bf16[256,2048]{1,0:T(8,128)(2,1)} %copy-done.24, bf16[256,2048]{1,0:T(8,128)(2,1)} %copy-done.28, bf16[256,2048]{1,0:T(8,128)(2,1)} %copy-done.26, bf16[256,2048]{1,0:T(8,128)(2,1)} %copy-done.29, bf16[8192,512]{1,0:T(8,128)(2,1)} %join.13.refs_4_.refs_5_.refs_1_.refs_2_.refs_6_.refs_7_.refs_3_, ...), custom_call_target="tpu_custom_call" | custom-call | flops 6442450944 | bytes 1 | tf_op jit(solution)/shard_map/project/pallas_call | solution.py:664
  178.8 15.3 %attend.2 = (bf16[1024,512]{1,0:T(8,128)(2,1)S(1)}, bf16[1024,1536]{1,0:T(8,128)(2,1)S(1)}, f32[4,1,1024]{2,1,0:T(1,128)S(1)}) custom-call(s32[1]{0:T(128)} %bitcast.6.limit_ref, f32[1024,3072]{1,0:T(8,128)} %project.3.proj_ref, f32[1024,128]{1,0:T(8,128)S(1)} %pad_maximum_fusion.5.cos_ref, f32[1024,128]{1,0:T(8,128)S(1)} %pad_maximum_fusion.6.sin_ref, ...), custom_call_target="tpu_custom_call" | custom-call | flops 2147483648 | bytes 1 | tf_op jit(solution)/shard_map/attend/pallas_call | solution.py:395
  199.0 14.8 %attend.3 = (bf16[1024,512]{1,0:T(8,128)(2,1)S(1)}, bf16[1024,1536]{1,0:T(8,128)(2,1)S(1)}, f32[4,1,1024]{2,1,0:T(1,128)S(1)}) custom-call(s32[1]{0:T(128)} %bitcast.6.limit_ref, f32[1024,3072]{1,0:T(8,128)} %project.3.proj_ref, f32[1024,128]{1,0:T(8,128)S(1)} %pad_maximum_fusion.5.cos_ref, f32[1024,128]{1,0:T(8,128)S(1)} %pad_maximum_fusion.6.sin_ref, ...), custom_call_target="tpu_custom_call" | custom-call | flops 2147483648 | bytes 1 | tf_op jit(solution)/shard_map/attend/pallas_call | solution.py:395
  218.3 6.6 expand.8
  231.9 13.9 %collective-permute-done.18.refs_3_ = bf16[704,512]{1,0:T(8,128)(2,1)S(1)} collective-permute-done((bf16[704,512]{1,0:T(8,128)(2,1)S(1)}, bf16[704,512]{1,0:T(8,128)(2,1)S(1)}, u32[]{:S(2)}, u32[]{:S(2)}) %collective-permute-start.18) | collective-permute-done | bytes 720928 | tf_op jit(solution)/shard_map/ppermute | solution.py:931
  246.6 6.7 expand.9
  253.3 12.6 %collective-permute-done.21.refs_2_ = bf16[704,512]{1,0:T(8,128)(2,1)} collective-permute-done((bf16[704,512]{1,0:T(8,128)(2,1)S(1)}, bf16[704,512]{1,0:T(8,128)(2,1)}, u32[]{:S(2)}, u32[]{:S(2)}) %collective-permute-start.21) | collective-permute-done | bytes 720928 | tf_op jit(solution)/shard_map/ppermute | solution.py:931
  274.5 29.7 %collective-permute-done.19 = bf16[256,2048]{1,0:T(8,128)(2,1)S(1)} collective-permute-done((bf16[256,2048]{1,0:T(8,128)(2,1)}, bf16[256,2048]{1,0:T(8,128)(2,1)S(1)}, u32[]{:S(2)}, u32[]{:S(2)}) %collective-permute-start.19) | collective-permute-done | bytes 1048608 | tf_op jit(solution)/shard_map/ppermute | solution.py:931
  308.3 19.1 %collective-permute-done.20.refs_1_.refs_3_ = bf16[256,2048]{1,0:T(8,128)(2,1)S(1)} collective-permute-done((bf16[256,2048]{1,0:T(8,128)(2,1)S(1)}, bf16[256,2048]{1,0:T(8,128)(2,1)S(1)}, u32[]{:S(2)}, u32[]{:S(2)}) %collective-permute-start.20) | collective-permute-done | bytes 1048608 | tf_op jit(solution)/shard_map/ppermute | solution.py:931
  350.2 4.2 join.18.refs_4_
  354.5 5.9 collective-permute-done.30.refs_3_
  372.7 21.0 %ff_forward.2 = (bf16[512,2816]{1,0:T(8,128)(2,1)}, bf16[512,2816]{1,0:T(8,128)(2,1)}, bf16[512,2816]{1,0:T(8,128)(2,1)}) custom-call(bf16[256,2048]{1,0:T(8,128)(2,1)} %copy-done.33, bf16[256,2048]{1,0:T(8,128)(2,1)} %copy-done.35, bf16[5632,512]{1,0:T(8,128)(2,1)} %join.15.refs_2_.refs_3_.refs_1_, bf16[5632,512]{1,0:T(8,128)(2,1)} %join.15.refs_2_.refs_3_.refs_1_, ...), custom_call_target="tpu_custom_call" | custom-call | flops 5905580032 | bytes 1 | tf_op jit(solution)/shard_map/ff_forward/pallas_call | solution.py:697
  393.7 12.9 %expand.10 = (f32[256,2048]{1,0:T(8,128)}, bf16[256,2048]{1,0:T(8,128)(2,1)}) custom-call(bf16[512,2816]{1,0:T(8,128)(2,1)} %get-tuple-element.236.refs_0_, bf16[5632,512]{1,0:T(8,128)(2,1)} %join.19.refs_1_.refs_2_.refs_3_, bf16[5632,512]{1,0:T(8,128)(2,1)} %join.19.refs_1_.refs_2_.refs_3_, ...), custom_call_target="tpu_custom_call" | custom-call | flops 2952790016 | bytes 1 | tf_op jit(solution)/shard_map/expand/pallas_call | solution.py:801
  407.6 12.7 %collective-permute-done.35 = bf16[256,2048]{1,0:T(8,128)(2,1)S(1)} collective-permute-done((bf16[256,2048]{1,0:T(8,128)(2,1)S(1)}, bf16[256,2048]{1,0:T(8,128)(2,1)S(1)}, u32[]{:S(2)}, u32[]{:S(2)}) %collective-permute-start.35) | collective-permute-done | bytes 1048608 | tf_op jit(solution)/shard_map/ppermute | solution.py:931
  420.3 21.4 %ff_forward.3 = (bf16[512,2816]{1,0:T(8,128)(2,1)}, bf16[512,2816]{1,0:T(8,128)(2,1)}, bf16[512,2816]{1,0:T(8,128)(2,1)}) custom-call(bf16[256,2048]{1,0:T(8,128)(2,1)} %copy-done.34, bf16[256,2048]{1,0:T(8,128)(2,1)} %copy-done.36, bf16[5632,512]{1,0:T(8,128)(2,1)} %join.15.refs_2_.refs_3_.refs_1_, bf16[5632,512]{1,0:T(8,128)(2,1)} %join.15.refs_2_.refs_3_.refs_1_, ...), custom_call_target="tpu_custom_call" | custom-call | flops 5905580032 | bytes 1 | tf_op jit(solution)/shard_map/ff_forward/pallas_call | solution.py:697
  441.7 13.0 %expand.11 = (f32[256,2048]{1,0:T(8,128)}, bf16[256,2048]{1,0:T(8,128)(2,1)}) custom-call(bf16[512,2816]{1,0:T(8,128)(2,1)} %get-tuple-element.206.refs_0_.refs_1_, bf16[5632,512]{1,0:T(8,128)(2,1)} %join.19.refs_1_.refs_2_.refs_3_, bf16[5632,512]{1,0:T(8,128)(2,1)} %join.19.refs_1_.refs_2_.refs_3_, ...), custom_call_target="tpu_custom_call" | custom-call | flops 2952790016 | bytes 1 | tf_op jit(solution)/shard_map/expand/pallas_call | solution.py:801
  465.4 15.6 %collective-permute-done.36 = bf16[256,2048]{1,0:T(8,128)(2,1)S(1)} collective-permute-done((bf16[256,2048]{1,0:T(8,128)(2,1)}, bf16[256,2048]{1,0:T(8,128)(2,1)S(1)}, u32[]{:S(2)}, u32[]{:S(2)}) %collective-permute-start.36) | collective-permute-done | bytes 1048608 | tf_op jit(solution)/shard_map/ppermute | solution.py:931
  485.8 16.4 %collective-permute-done.37.refs_1_.refs_3_ = bf16[256,2048]{1,0:T(8,128)(2,1)S(1)} collective-permute-done((bf16[256,2048]{1,0:T(8,128)(2,1)S(1)}, bf16[256,2048]{1,0:T(8,128)(2,1)S(1)}, u32[]{:S(2)}, u32[]{:S(2)}) %collective-permute-start.37) | collective-permute-done | bytes 1048608 | tf_op jit(solution)/shard_map/ppermute | solution.py:931
  503.4 17.4 %ff_back.2 = (bf16[512,2816]{1,0:T(8,128)(2,1)}, bf16[512,2816]{1,0:T(8,128)(2,1)}, f32[1,2816]{1,0:T(1,128)}, f32[1,2816]{1,0:T(1,128)}) custom-call(bf16[256,2048]{1,0:T(8,128)(2,1)} %copy-done.39, bf16[256,2048]{1,0:T(8,128)(2,1)} %copy-done.47, bf16[5632,512]{1,0:T(8,128)(2,1)} %join.19.refs_1_.refs_2_.refs_3_, ...), custom_call_target="tpu_custom_call" | custom-call | flops 4429185024 | bytes 1 | tf_op jit(solution)/shard_map/ff_back/pallas_call | solution.py:741
  520.9 6.4 collective-permute-done.38.refs_5_.refs_1_
  527.2 21.6 %expand.12 = (f32[256,2048]{1,0:T(8,128)}, bf16[256,2048]{1,0:T(8,128)(2,1)}) custom-call(bf16[512,2816]{1,0:T(8,128)(2,1)} %get-tuple-element.252.refs_0_, bf16[5632,512]{1,0:T(8,128)(2,1)} %join.15.refs_2_.refs_3_.refs_1_, bf16[5632,512]{1,0:T(8,128)(2,1)} %join.15.refs_2_.refs_3_.refs_1_, ...), custom_call_target="tpu_custom_call" | custom-call | flops 5905580032 | bytes 1 | tf_op jit(solution)/shard_map/expand/pallas_call | solution.py:801
  548.8 10.6 outer.21
  560.0 17.4 %ff_back.3 = (bf16[512,2816]{1,0:T(8,128)(2,1)}, bf16[512,2816]{1,0:T(8,128)(2,1)}, f32[1,2816]{1,0:T(1,128)}, f32[1,2816]{1,0:T(1,128)}) custom-call(bf16[256,2048]{1,0:T(8,128)(2,1)} %get-tuple-element.218.refs_4_.refs_0_, bf16[256,2048]{1,0:T(8,128)(2,1)} %copy-done.48, bf16[5632,512]{1,0:T(8,128)(2,1)} %join.19.refs_1_.refs_2_.refs_3_, ...), custom_call_target="tpu_custom_call" | custom-call | flops 4429185024 | bytes 1 | tf_op jit(solution)/shard_map/ff_back/pallas_call | solution.py:741
  577.5 7.7 collective-permute-done.39
  585.2 4.2 multiply_reduce_fusion.2
  591.6 8.8 outer.22
  600.4 21.3 %expand.13 = (f32[256,2048]{1,0:T(8,128)}, bf16[256,2048]{1,0:T(8,128)(2,1)}) custom-call(bf16[512,2816]{1,0:T(8,128)(2,1)} %get-tuple-element.224.refs_0_.refs_1_, bf16[5632,512]{1,0:T(8,128)(2,1)} %join.15.refs_2_.refs_3_.refs_1_, bf16[5632,512]{1,0:T(8,128)(2,1)} %join.15.refs_2_.refs_3_.refs_1_, ...), custom_call_target="tpu_custom_call" | custom-call | flops 5905580032 | bytes 1 | tf_op jit(solution)/shard_map/expand/pallas_call | solution.py:801
  621.8 10.6 outer.23
  636.6 10.5 outer.24
  647.2 11.6 %collective-permute-done.42 = bf16[256,2048]{1,0:T(8,128)(2,1)} collective-permute-done((bf16[256,2048]{1,0:T(8,128)(2,1)}, bf16[256,2048]{1,0:T(8,128)(2,1)}, u32[]{:S(2)}, u32[]{:S(2)}) %collective-permute-start.42) | collective-permute-done | bytes 1048608 | tf_op jit(solution)/shard_map/ppermute | solution.py:931
  665.3 15.6 %collective-permute-done.43.refs_1_.refs_3_ = bf16[256,2048]{1,0:T(8,128)(2,1)} collective-permute-done((bf16[256,2048]{1,0:T(8,128)(2,1)S(1)}, bf16[256,2048]{1,0:T(8,128)(2,1)}, u32[]{:S(2)}, u32[]{:S(2)}) %collective-permute-start.43) | collective-permute-done | bytes 1048608 | tf_op jit(solution)/shard_map/ppermute | solution.py:931
  682.1 6.3 project.4.grad_first
  688.4 8.4 outer.25
  700.6 9.4 outer.26
  711.0 6.3 project.5.grad_second
  718.5 19.7 %attend_back.2 = (bf16[1024,1536]{1,0:T(8,128)(2,1)}, f32[4,1,384]{2,1,0:T(1,128)S(1)}) custom-call(s32[1]{0:T(128)} %bitcast.6.limit_ref, bf16[1024,1536]{1,0:T(8,128)(2,1)} %copy-done.14, bf16[512,1024]{1,0:T(8,128)(2,1)S(1)} %copy-done.8, bf16[512,1024]{1,0:T(8,128)(2,1)S(1)} %copy-done.9, f32[4,1,1024]{2,1,0:T(1,128)S(1)} %get-tuple-element.241.lse_ref, ...), custom_call_target="tpu_custom_call" | custom-call | flops 2684354560 | bytes 1 | tf_op jit(solution)/shard_map/attend_back/pallas_call | solution.py:525
  738.2 9.0 collective-permute-done.41
  748.0 7.6 outer.27
  763.0 8.3 outer.28
  771.3 6.6 collective-permute-done.51
  779.1 19.2 %attend_back.3 = (bf16[1024,1536]{1,0:T(8,128)(2,1)}, f32[4,1,384]{2,1,0:T(1,128)S(1)}) custom-call(s32[1]{0:T(128)} %bitcast.6.limit_ref, bf16[1024,1536]{1,0:T(8,128)(2,1)} %copy-done.13, bf16[512,1024]{1,0:T(8,128)(2,1)S(1)} %copy-done.8, bf16[512,1024]{1,0:T(8,128)(2,1)S(1)} %copy-done.10, f32[4,1,1024]{2,1,0:T(1,128)S(1)} %get-tuple-element.250.lse_ref, ...), custom_call_target="tpu_custom_call" | custom-call | flops 2684354560 | bytes 1 | tf_op jit(solution)/shard_map/attend_back/pallas_call | solution.py:525
  799.3 9.6 outer.29
  808.9 7.7 outer.30
  823.9 5.7 outer.31
  829.6 14.1 %expand.14 = (f32[256,2048]{1,0:T(8,128)}, bf16[256,2048]{1,0:T(8,128)(2,1)}) custom-call(bf16[1024,1536]{1,0:T(8,128)(2,1)} %get-tuple-element.283.refs_0_.refs_1_, bf16[8192,512]{1,0:T(8,128)(2,1)} %join.13.refs_4_.refs_5_.refs_1_.refs_2_.refs_6_.refs_7_.refs_3_, bf16[8192,512]{1,0:T(8,128)(2,1)} %join.13.refs_4_.refs_5_.refs_1_.refs_2_.refs_6_.refs_7_.refs_3_, ...), custom_call_target="tpu_custom_call" | custom-call | flops 3221225472 | bytes 1 | tf_op jit(solution)/shard_map/expand/pallas_call | solution.py:801
  847.5 6.9 collective-permute-done.58
  859.1 10.3 collective-permute-done.56
  870.9 8.8 collective-permute-done.64
  882.7 5.8 outer.32
  888.4 13.9 %expand.15 = (f32[256,2048]{1,0:T(8,128)}, bf16[256,2048]{1,0:T(8,128)(2,1)}) custom-call(bf16[1024,1536]{1,0:T(8,128)(2,1)} %get-tuple-element.283.refs_0_.refs_1_, bf16[8192,512]{1,0:T(8,128)(2,1)} %join.13.refs_4_.refs_5_.refs_1_.refs_2_.refs_6_.refs_7_.refs_3_, bf16[8192,512]{1,0:T(8,128)(2,1)} %join.13.refs_4_.refs_5_.refs_1_.refs_2_.refs_6_.refs_7_.refs_3_, ...), custom_call_target="tpu_custom_call" | custom-call | flops 3221225472 | bytes 1 | tf_op jit(solution)/shard_map/expand/pallas_call | solution.py:801
  902.3 9.8 outer.33
  936.3 28.1 %collective-permute-done.59 = bf16[256,2048]{1,0:T(8,128)(2,1)} collective-permute-done((bf16[256,2048]{1,0:T(8,128)(2,1)}, bf16[256,2048]{1,0:T(8,128)(2,1)}, u32[]{:S(2)}, u32[]{:S(2)}) %collective-permute-start.59) | collective-permute-done | bytes 1048608 | tf_op jit(solution)/shard_map/ppermute | solution.py:931
  965.6 6.0 outer.36
  987.9 6.0 outer.39
  998.5 4.5 collective-permute-done.82
  1018.9 16.4 %collective-permute-done.75 = bf16[256,512]{1,0:T(8,128)(2,1)S(1)} collective-permute-done((bf16[256,512]{1,0:T(8,128)(2,1)}, bf16[256,512]{1,0:T(8,128)(2,1)S(1)}, u32[]{:S(2)}, u32[]{:S(2)}) %collective-permute-start.75) | collective-permute-done | bytes 262176 | tf_op jit(solution)/shard_map/ppermute | solution.py:931
  1035.3 7.8 collective-permute-done.77
  1044.8 7.1 all-reduce.3.cloned.1.call-done
  1065.2 6.2 copy.54
  (529 shorter events, 274.4 us)
Async XLA Ops:
  7.2 1044.7 %all-reduce.3.cloned.1.call-start = ((), (), s32[]{:S(2)}) async-start(), calls=%async_computation | async-start | bytes 278528 | tf_op jit(solution)/shard_map/psum | solution.py:1453
  22.3 47.8 %collective-permute-start.3 = (bf16[1024,512]{1,0:T(8,128)(2,1)S(1)}, bf16[1024,512]{1,0:T(8,128)(2,1)}, u32[]{:S(2)}, u32[]{:S(2)}) collective-permute-start(bf16[1024,512]{1,0:T(8,128)(2,1)S(1)} %pad_maximum_fusion.3.refs_0_), channel_id=1, source_target_pairs={{0,2},{1,3},{2,0},{3,1},{4,6},{5,7},{6,4},{7,5},{8,10},{9,11},{10,... | collective-permute-start | bytes 3145736 | tf_op jit(solution)/shard_map/ppermute | solution.py:931
  37.3 32.8 %collective-permute-start.4 = (bf16[1024,512]{1,0:T(8,128)(2,1)S(1)}, bf16[1024,512]{1,0:T(8,128)(2,1)}, u32[]{:S(2)}, u32[]{:S(2)}) collective-permute-start(bf16[1024,512]{1,0:T(8,128)(2,1)S(1)} %collective-permute-done.refs_0_), channel_id=1, source_target_pairs={{0,16},{16,0},{1,17},{17,1},{2,18},{18,2},{3,19},{19,3},{4,20},{20... | collective-permute-start | bytes 3145736 | tf_op jit(solution)/shard_map/ppermute | solution.py:931
  70.1 26.3 %collective-permute-start.8 = (bf16[1024,512]{1,0:T(8,128)(2,1)}, bf16[1024,512]{1,0:T(8,128)(2,1)S(1)}, u32[]{:S(2)}, u32[]{:S(2)}) collective-permute-start(bf16[1024,512]{1,0:T(8,128)(2,1)} %collective-permute-done.3.refs_2_), channel_id=1, source_target_pairs={{0,8},{4,12},{8,0},{12,4},{1,9},{5,13},{9,1},{13,5},{2,10},{6,14},... | collective-permute-start | bytes 3145736 | tf_op jit(solution)/shard_map/ppermute | solution.py:931
  70.7 54.7 %collective-permute-start.7 = (bf16[1408,512]{1,0:T(8,128)(2,1)}, bf16[1408,512]{1,0:T(8,128)(2,1)}, u32[]{:S(2)}, u32[]{:S(2)}) collective-permute-start(bf16[1408,512]{1,0:T(8,128)(2,1)} %pad_maximum_fusion.2), channel_id=1, source_target_pairs={{0,8},{4,12},{8,0},{12,4},{1,9},{5,13},{9,1},{13,5},{2,10},{6,14},... | collective-permute-start | bytes 4325384 | tf_op jit(solution)/shard_map/ppermute | solution.py:931
  72.2 44.2 %collective-permute-start.1 = (bf16[256,2048]{1,0:T(8,128)(2,1)S(1)}, bf16[256,2048]{1,0:T(8,128)(2,1)S(1)}, u32[]{:S(2)}, u32[]{:S(2)}) collective-permute-start(bf16[256,2048]{1,0:T(8,128)(2,1)S(1)} %get-tuple-element.165.refs_0_.refs_2_), channel_id=1, source_target_pairs={{0,1},{1,0},{2,3},{3,2},{4,5},{5,4},{6,7},{7,6},{8,9},{9,8},{10,11... | collective-permute-start | bytes 3145736 | tf_op jit(solution)/shard_map/ppermute | solution.py:931
  72.2 45.3 %collective-permute-start.5 = (bf16[1024,512]{1,0:T(8,128)(2,1)}, bf16[1024,512]{1,0:T(8,128)(2,1)}, u32[]{:S(2)}, u32[]{:S(2)}) collective-permute-start(bf16[1024,512]{1,0:T(8,128)(2,1)} %collective-permute-done.3.refs_2_), channel_id=1, source_target_pairs={{0,16},{16,0},{1,17},{17,1},{2,18},{18,2},{3,19},{19,3},{4,20},{20... | collective-permute-start | bytes 3145736 | tf_op jit(solution)/shard_map/ppermute | solution.py:931
  73.7 50.7 %collective-permute-start.6 = (bf16[256,2048]{1,0:T(8,128)(2,1)}, bf16[256,2048]{1,0:T(8,128)(2,1)S(1)}, u32[]{:S(2)}, u32[]{:S(2)}) collective-permute-start(bf16[256,2048]{1,0:T(8,128)(2,1)} %get-tuple-element.161), channel_id=1, source_target_pairs={{0,2},{1,3},{2,0},{3,1},{4,6},{5,7},{6,4},{7,5},{8,10},{9,11},{10,... | collective-permute-start | bytes 3145736 | tf_op jit(solution)/shard_map/ppermute | solution.py:931
  96.5 28.9 %collective-permute-start.9 = (bf16[1024,512]{1,0:T(8,128)(2,1)S(1)}, bf16[1024,512]{1,0:T(8,128)(2,1)}, u32[]{:S(2)}, u32[]{:S(2)}) collective-permute-start(bf16[1024,512]{1,0:T(8,128)(2,1)S(1)} %collective-permute-done.8.refs_2_), channel_id=1, source_target_pairs={{0,16},{16,0},{1,17},{17,1},{2,18},{18,2},{3,19},{19,3},{4,20},{20... | collective-permute-start | bytes 3145736 | tf_op jit(solution)/shard_map/ppermute | solution.py:931
  132.2 27.4 %collective-permute-start.11 = (bf16[8192,512]{1,0:T(8,128)(2,1)}, bf16[8192,512]{1,0:T(8,128)(2,1)}, u32[]{:S(2)}, u32[]{:S(2)}) collective-permute-start(bf16[8192,512]{1,0:T(8,128)(2,1)} %join.13.refs_4_.refs_5_.refs_1_.refs_2_.refs_6_.refs_7_.refs_3_), channel_id=1, source_target_pairs={{0,4},{4,0},{8,12},{12,8},{1,5},{5,1},{9,13},{13,9},{2,6},{6,2},{1... | collective-permute-start | bytes 25165832 | tf_op jit(solution)/shard_map/ppermute | solution.py:931
  136.2 42.6 %collective-permute-start.12 = (bf16[704,512]{1,0:T(8,128)(2,1)}, bf16[704,512]{1,0:T(8,128)(2,1)}, u32[]{:S(2)}, u32[]{:S(2)}) collective-permute-start(bf16[704,512]{1,0:T(8,128)(2,1)} %get-tuple-element.192.refs_0_), channel_id=1, source_target_pairs={{0,8},{4,12},{8,0},{12,4},{1,9},{5,13},{9,1},{13,5},{2,10},{6,14},... | collective-permute-start | bytes 2162696 | tf_op jit(solution)/shard_map/ppermute | solution.py:931
  136.8 62.2 %collective-permute-start.13 = (bf16[1408,512]{1,0:T(8,128)(2,1)}, bf16[1408,512]{1,0:T(8,128)(2,1)}, u32[]{:S(2)}, u32[]{:S(2)}) collective-permute-start(bf16[1408,512]{1,0:T(8,128)(2,1)} %collective-permute-done.7.refs_0_), channel_id=1, source_target_pairs={{0,16},{16,0},{1,17},{17,1},{2,18},{18,2},{3,19},{19,3},{4,20},{20... | collective-permute-start | bytes 4325384 | tf_op jit(solution)/shard_map/ppermute | solution.py:931
  158.5 38.3 %collective-permute-start.14 = (bf16[704,512]{1,0:T(8,128)(2,1)}, bf16[704,512]{1,0:T(8,128)(2,1)S(1)}, u32[]{:S(2)}, u32[]{:S(2)}) collective-permute-start(bf16[704,512]{1,0:T(8,128)(2,1)} %bitcast.12.refs_0_), channel_id=1, source_target_pairs={{0,2},{1,3},{2,0},{3,1},{4,6},{5,7},{6,4},{7,5},{8,10},{9,11},{10,... | collective-permute-start | bytes 2162696 | tf_op jit(solution)/shard_map/ppermute | solution.py:931
  224.9 46.1 %collective-permute-start.17 = (bf16[256,2048]{1,0:T(8,128)(2,1)}, bf16[256,2048]{1,0:T(8,128)(2,1)S(1)}, u32[]{:S(2)}, u32[]{:S(2)}) collective-permute-start(bf16[256,2048]{1,0:T(8,128)(2,1)} %get-tuple-element.176), channel_id=1, source_target_pairs={{0,1},{1,0},{2,3},{3,2},{4,5},{5,4},{6,7},{7,6},{8,9},{9,8},{10,11... | collective-permute-start | bytes 3145736 | tf_op jit(solution)/shard_map/ppermute | solution.py:931
  227.3 38.6 %collective-permute-start.21 = (bf16[704,512]{1,0:T(8,128)(2,1)S(1)}, bf16[704,512]{1,0:T(8,128)(2,1)}, u32[]{:S(2)}, u32[]{:S(2)}) collective-permute-start(bf16[704,512]{1,0:T(8,128)(2,1)S(1)} %bitcast.165), channel_id=1, source_target_pairs={{0,2},{1,3},{2,0},{3,1},{4,6},{5,7},{6,4},{7,5},{8,10},{9,11},{10,... | collective-permute-start | bytes 2162696 | tf_op jit(solution)/shard_map/ppermute | solution.py:931
  228.3 77.9 %collective-permute-start.24 = (bf16[704,512]{1,0:T(8,128)(2,1)}, bf16[704,512]{1,0:T(8,128)(2,1)}, u32[]{:S(2)}, u32[]{:S(2)}) collective-permute-start(bf16[704,512]{1,0:T(8,128)(2,1)} %get-tuple-element.192.refs_0_), channel_id=1, source_target_pairs={{0,2},{1,3},{2,0},{3,1},{4,6},{5,7},{6,4},{7,5},{8,10},{9,11},{10,... | collective-permute-start | bytes 2162696 | tf_op jit(solution)/shard_map/ppermute | solution.py:931
  230.4 99.7 %collective-permute-start.25 = (bf16[704,512]{1,0:T(8,128)(2,1)}, bf16[704,512]{1,0:T(8,128)(2,1)}, u32[]{:S(2)}, u32[]{:S(2)}) collective-permute-start(bf16[704,512]{1,0:T(8,128)(2,1)} %collective-permute-done.12.refs_0_), channel_id=1, source_target_pairs={{0,16},{16,0},{1,17},{17,1},{2,18},{18,2},{3,19},{19,3},{4,20},{20... | collective-permute-start | bytes 2162696 | tf_op jit(solution)/shard_map/ppermute | solution.py:931
  265.9 64.6 %collective-permute-start.23 = (bf16[704,512]{1,0:T(8,128)(2,1)}, bf16[704,512]{1,0:T(8,128)(2,1)}, u32[]{:S(2)}, u32[]{:S(2)}) collective-permute-start(bf16[704,512]{1,0:T(8,128)(2,1)} %collective-permute-done.21.refs_2_), channel_id=1, source_target_pairs={{0,16},{16,0},{1,17},{17,1},{2,18},{18,2},{3,19},{19,3},{4,20},{20... | collective-permute-start | bytes 2162696 | tf_op jit(solution)/shard_map/ppermute | solution.py:931
  266.4 41.4 %collective-permute-start.22 = (bf16[704,512]{1,0:T(8,128)(2,1)}, bf16[704,512]{1,0:T(8,128)(2,1)}, u32[]{:S(2)}, u32[]{:S(2)}) collective-permute-start(bf16[704,512]{1,0:T(8,128)(2,1)} %collective-permute-done.21.refs_2_), channel_id=1, source_target_pairs={{0,8},{4,12},{8,0},{12,4},{1,9},{5,13},{9,1},{13,5},{2,10},{6,14},... | collective-permute-start | bytes 2162696 | tf_op jit(solution)/shard_map/ppermute | solution.py:931
  271.0 33.2 %collective-permute-start.19 = (bf16[256,2048]{1,0:T(8,128)(2,1)}, bf16[256,2048]{1,0:T(8,128)(2,1)S(1)}, u32[]{:S(2)}, u32[]{:S(2)}) collective-permute-start(bf16[256,2048]{1,0:T(8,128)(2,1)} %get-tuple-element.180), channel_id=1, source_target_pairs={{0,1},{1,0},{2,3},{3,2},{4,5},{5,4},{6,7},{7,6},{8,9},{9,8},{10,11... | collective-permute-start | bytes 3145736 | tf_op jit(solution)/shard_map/ppermute | solution.py:931
  306.2 31.9 %collective-permute-start.29 = (bf16[704,512]{1,0:T(8,128)(2,1)}, bf16[704,512]{1,0:T(8,128)(2,1)}, u32[]{:S(2)}, u32[]{:S(2)}) collective-permute-start(bf16[704,512]{1,0:T(8,128)(2,1)} %collective-permute-done.24.refs_2_), channel_id=1, source_target_pairs={{0,8},{4,12},{8,0},{12,4},{1,9},{5,13},{9,1},{13,5},{2,10},{6,14},... | collective-permute-start | bytes 2162696 | tf_op jit(solution)/shard_map/ppermute | solution.py:931
  307.8 38.1 %collective-permute-start.26 = (bf16[704,512]{1,0:T(8,128)(2,1)}, bf16[704,512]{1,0:T(8,128)(2,1)}, u32[]{:S(2)}, u32[]{:S(2)}) collective-permute-start(bf16[704,512]{1,0:T(8,128)(2,1)} %collective-permute-done.22.refs_2_), channel_id=1, source_target_pairs={{0,16},{16,0},{1,17},{17,1},{2,18},{18,2},{3,19},{19,3},{4,20},{20... | collective-permute-start | bytes 2162696 | tf_op jit(solution)/shard_map/ppermute | solution.py:931
  342.0 30.7 %collective-permute-start.31 = (bf16[5632,512]{1,0:T(8,128)(2,1)}, bf16[5632,512]{1,0:T(8,128)(2,1)}, u32[]{:S(2)}, u32[]{:S(2)}) collective-permute-start(bf16[5632,512]{1,0:T(8,128)(2,1)} %join.15.refs_2_.refs_3_.refs_1_), channel_id=1, source_target_pairs={{0,4},{4,0},{8,12},{12,8},{1,5},{5,1},{9,13},{13,9},{2,6},{6,2},{1... | collective-permute-start | bytes 17301512 | tf_op jit(solution)/shard_map/ppermute | solution.py:931
  364.3 29.4 %collective-permute-start.33 = (bf16[5632,512]{1,0:T(8,128)(2,1)}, bf16[5632,512]{1,0:T(8,128)(2,1)}, u32[]{:S(2)}, u32[]{:S(2)}) collective-permute-start(bf16[5632,512]{1,0:T(8,128)(2,1)} %join.19.refs_1_.refs_2_.refs_3_), channel_id=1, source_target_pairs={{0,4},{4,0},{8,12},{12,8},{1,5},{5,1},{9,13},{13,9},{2,6},{6,2},{1... | collective-permute-start | bytes 17301512 | tf_op jit(solution)/shard_map/ppermute | solution.py:931
  371.3 49.0 %collective-permute-start.35 = (bf16[256,2048]{1,0:T(8,128)(2,1)S(1)}, bf16[256,2048]{1,0:T(8,128)(2,1)S(1)}, u32[]{:S(2)}, u32[]{:S(2)}) collective-permute-start(bf16[256,2048]{1,0:T(8,128)(2,1)S(1)} %dynamic-slice_bitcast_fusion), channel_id=1, source_target_pairs={{0,2},{1,3},{2,0},{3,1},{4,6},{5,7},{6,4},{7,5},{8,10},{9,11},{10,... | collective-permute-start | bytes 3145736 | tf_op jit(solution)/shard_map/ppermute | solution.py:931
  406.6 48.2 %collective-permute-start.34 = (bf16[256,2048]{1,0:T(8,128)(2,1)}, bf16[256,2048]{1,0:T(8,128)(2,1)S(1)}, u32[]{:S(2)}, u32[]{:S(2)}) collective-permute-start(bf16[256,2048]{1,0:T(8,128)(2,1)} %get-tuple-element.201), channel_id=1, source_target_pairs={{0,1},{1,0},{2,3},{3,2},{4,5},{5,4},{6,7},{7,6},{8,9},{9,8},{10,11... | collective-permute-start | bytes 3145736 | tf_op jit(solution)/shard_map/ppermute | solution.py:931
  454.7 26.3 %collective-permute-start.36 = (bf16[256,2048]{1,0:T(8,128)(2,1)}, bf16[256,2048]{1,0:T(8,128)(2,1)S(1)}, u32[]{:S(2)}, u32[]{:S(2)}) collective-permute-start(bf16[256,2048]{1,0:T(8,128)(2,1)} %get-tuple-element.208), channel_id=1, source_target_pairs={{0,1},{1,0},{2,3},{3,2},{4,5},{5,4},{6,7},{7,6},{8,9},{9,8},{10,11... | collective-permute-start | bytes 3145736 | tf_op jit(solution)/shard_map/ppermute | solution.py:931
  463.3 38.8 %collective-permute-start.37 = (bf16[256,2048]{1,0:T(8,128)(2,1)S(1)}, bf16[256,2048]{1,0:T(8,128)(2,1)S(1)}, u32[]{:S(2)}, u32[]{:S(2)}) collective-permute-start(bf16[256,2048]{1,0:T(8,128)(2,1)S(1)} %get-tuple-element.210.refs_0_.refs_2_), channel_id=1, source_target_pairs={{0,1},{1,0},{2,3},{3,2},{4,5},{5,4},{6,7},{7,6},{8,9},{9,8},{10,11... | collective-permute-start | bytes 3145736 | tf_op jit(solution)/shard_map/ppermute | solution.py:931
  559.4 32.2 %collective-permute-start.40 = (bf16[2816,1024]{1,0:T(8,128)(2,1)}, bf16[2816,1024]{1,0:T(8,128)(2,1)}, u32[]{:S(2)}, u32[]{:S(2)}) collective-permute-start(bf16[2816,1024]{1,0:T(8,128)(2,1)} %outer.21), channel_id=1, source_target_pairs={{0,4},{4,0},{8,12},{12,8},{1,5},{5,1},{9,13},{13,9},{2,6},{6,2},{1... | collective-permute-start | bytes 17301512 | tf_op jit(solution)/shard_map/ppermute | solution.py:931
  632.3 56.1 %collective-permute-start.44 = (bf16[2816,1024]{1,0:T(8,128)(2,1)}, bf16[2816,1024]{1,0:T(8,128)(2,1)}, u32[]{:S(2)}, u32[]{:S(2)}) collective-permute-start(bf16[2816,1024]{1,0:T(8,128)(2,1)} %outer.23), channel_id=1, source_target_pairs={{0,4},{4,0},{8,12},{12,8},{1,5},{5,1},{9,13},{13,9},{2,6},{6,2},{1... | collective-permute-start | bytes 17301512 | tf_op jit(solution)/shard_map/ppermute | solution.py:931
  632.5 26.3 %collective-permute-start.42 = (bf16[256,2048]{1,0:T(8,128)(2,1)}, bf16[256,2048]{1,0:T(8,128)(2,1)}, u32[]{:S(2)}, u32[]{:S(2)}) collective-permute-start(bf16[256,2048]{1,0:T(8,128)(2,1)} %get-tuple-element.231), channel_id=1, source_target_pairs={{0,1},{1,0},{2,3},{3,2},{4,5},{5,4},{6,7},{7,6},{8,9},{9,8},{10,11... | collective-permute-start | bytes 3145736 | tf_op jit(solution)/shard_map/ppermute | solution.py:931
  633.2 47.7 %collective-permute-start.43 = (bf16[256,2048]{1,0:T(8,128)(2,1)S(1)}, bf16[256,2048]{1,0:T(8,128)(2,1)}, u32[]{:S(2)}, u32[]{:S(2)}) collective-permute-start(bf16[256,2048]{1,0:T(8,128)(2,1)S(1)} %get-tuple-element.232.refs_0_.refs_2_), channel_id=1, source_target_pairs={{0,1},{1,0},{2,3},{3,2},{4,5},{5,4},{6,7},{7,6},{8,9},{9,8},{10,11... | collective-permute-start | bytes 3145736 | tf_op jit(solution)/shard_map/ppermute | solution.py:931
  634.6 66.0 %collective-permute-start.45 = (bf16[1408,512]{1,0:T(8,128)(2,1)}, bf16[1408,512]{1,0:T(8,128)(2,1)}, u32[]{:S(2)}, u32[]{:S(2)}) collective-permute-start(bf16[1408,512]{1,0:T(8,128)(2,1)} %get-tuple-element.223), channel_id=1, source_target_pairs={{0,8},{4,12},{8,0},{12,4},{1,9},{5,13},{9,1},{13,5},{2,10},{6,14},... | collective-permute-start | bytes 4325384 | tf_op jit(solution)/shard_map/ppermute | solution.py:931
  636.0 63.2 %collective-permute-start.46 = (bf16[1408,512]{1,0:T(8,128)(2,1)}, bf16[1408,512]{1,0:T(8,128)(2,1)}, u32[]{:S(2)}, u32[]{:S(2)}) collective-permute-start(bf16[1408,512]{1,0:T(8,128)(2,1)} %get-tuple-element.237), channel_id=1, source_target_pairs={{0,8},{4,12},{8,0},{12,4},{1,9},{5,13},{9,1},{13,5},{2,10},{6,14},... | collective-permute-start | bytes 4325384 | tf_op jit(solution)/shard_map/ppermute | solution.py:931
  658.8 104.2 %collective-permute-start.50 = (bf16[2816,1024]{1,0:T(8,128)(2,1)}, bf16[2816,1024]{1,0:T(8,128)(2,1)}, u32[]{:S(2)}, u32[]{:S(2)}) collective-permute-start(bf16[2816,1024]{1,0:T(8,128)(2,1)} %outer.24), channel_id=1, source_target_pairs={{0,4},{4,0},{8,12},{12,8},{1,5},{5,1},{9,13},{13,9},{2,6},{6,2},{1... | collective-permute-start | bytes 17301512 | tf_op jit(solution)/shard_map/ppermute | solution.py:931
  680.9 30.1 %collective-permute-start.47 = (bf16[256,2048]{1,0:T(8,128)(2,1)}, bf16[256,2048]{1,0:T(8,128)(2,1)}, u32[]{:S(2)}, u32[]{:S(2)}) collective-permute-start(bf16[256,2048]{1,0:T(8,128)(2,1)} %get-tuple-element.239.refs_0_.refs_4_), channel_id=1, source_target_pairs={{0,1},{1,0},{2,3},{3,2},{4,5},{5,4},{6,7},{7,6},{8,9},{9,8},{10,11... | collective-permute-start | bytes 3145736 | tf_op jit(solution)/shard_map/ppermute | solution.py:931
  696.9 50.3 %collective-permute-start.48 = (bf16[1408,512]{1,0:T(8,128)(2,1)}, bf16[1408,512]{1,0:T(8,128)(2,1)}, u32[]{:S(2)}, u32[]{:S(2)}) collective-permute-start(bf16[1408,512]{1,0:T(8,128)(2,1)} %get-tuple-element.243), channel_id=1, source_target_pairs={{0,8},{4,12},{8,0},{12,4},{1,9},{5,13},{9,1},{13,5},{2,10},{6,14},... | collective-permute-start | bytes 4325384 | tf_op jit(solution)/shard_map/ppermute | solution.py:931
  699.3 47.9 %collective-permute-start.41 = (bf16[256,2048]{1,0:T(8,128)(2,1)}, bf16[256,2048]{1,0:T(8,128)(2,1)}, u32[]{:S(2)}, u32[]{:S(2)}) collective-permute-start(bf16[256,2048]{1,0:T(8,128)(2,1)} %get-tuple-element.228), channel_id=1, source_target_pairs={{0,2},{1,3},{2,0},{3,1},{4,6},{5,7},{6,4},{7,5},{8,10},{9,11},{10,... | collective-permute-start | bytes 3145736 | tf_op jit(solution)/shard_map/ppermute | solution.py:931
  710.0 37.2 %collective-permute-start.49 = (bf16[704,512]{1,0:T(8,128)(2,1)}, bf16[704,512]{1,0:T(8,128)(2,1)S(1)}, u32[]{:S(2)}, u32[]{:S(2)}) collective-permute-start(bf16[704,512]{1,0:T(8,128)(2,1)} %get-tuple-element.244), channel_id=1, source_target_pairs={{0,16},{16,0},{1,17},{17,1},{2,18},{18,2},{3,19},{19,3},{4,20},{20... | collective-permute-start | bytes 2162696 | tf_op jit(solution)/shard_map/ppermute | solution.py:931
  755.6 43.7 %collective-permute-start.52 = (bf16[1536,1024]{1,0:T(8,128)(2,1)}, bf16[1536,1024]{1,0:T(8,128)(2,1)}, u32[]{:S(2)}, u32[]{:S(2)}) collective-permute-start(bf16[1536,1024]{1,0:T(8,128)(2,1)} %outer.27), channel_id=1, source_target_pairs={{0,4},{4,0},{8,12},{12,8},{1,5},{5,1},{9,13},{13,9},{2,6},{6,2},{1... | collective-permute-start | bytes 9437192 | tf_op jit(solution)/shard_map/ppermute | solution.py:931
  757.8 41.6 %collective-permute-start.53 = (bf16[1408,512]{1,0:T(8,128)(2,1)}, bf16[1408,512]{1,0:T(8,128)(2,1)}, u32[]{:S(2)}, u32[]{:S(2)}) collective-permute-start(bf16[1408,512]{1,0:T(8,128)(2,1)} %get-tuple-element.235), channel_id=1, source_target_pairs={{0,8},{4,12},{8,0},{12,4},{1,9},{5,13},{9,1},{13,5},{2,10},{6,14},... | collective-permute-start | bytes 4325384 | tf_op jit(solution)/shard_map/ppermute | solution.py:931
  763.0 46.0 %collective-permute-start.54 = (bf16[704,512]{1,0:T(8,128)(2,1)}, bf16[704,512]{1,0:T(8,128)(2,1)S(1)}, u32[]{:S(2)}, u32[]{:S(2)}) collective-permute-start(bf16[704,512]{1,0:T(8,128)(2,1)} %add_convert_fusion.11), channel_id=1, source_target_pairs={{0,2},{1,3},{2,0},{3,1},{4,6},{5,7},{6,4},{7,5},{8,10},{9,11},{10,... | collective-permute-start | bytes 2162696 | tf_op jit(solution)/shard_map/ppermute | solution.py:931
  816.7 66.0 %collective-permute-start.57 = (bf16[1536,1024]{1,0:T(8,128)(2,1)}, bf16[1536,1024]{1,0:T(8,128)(2,1)}, u32[]{:S(2)}, u32[]{:S(2)}) collective-permute-start(bf16[1536,1024]{1,0:T(8,128)(2,1)} %outer.30), channel_id=1, source_target_pairs={{0,4},{4,0},{8,12},{12,8},{1,5},{5,1},{9,13},{13,9},{2,6},{6,2},{1... | collective-permute-start | bytes 9437192 | tf_op jit(solution)/shard_map/ppermute | solution.py:931
  819.0 38.0 %collective-permute-start.55 = (bf16[1408,512]{1,0:T(8,128)(2,1)}, bf16[1408,512]{1,0:T(8,128)(2,1)}, u32[]{:S(2)}, u32[]{:S(2)}) collective-permute-start(bf16[1408,512]{1,0:T(8,128)(2,1)} %get-tuple-element.247), channel_id=1, source_target_pairs={{0,8},{4,12},{8,0},{12,4},{1,9},{5,13},{9,1},{13,5},{2,10},{6,14},... | collective-permute-start | bytes 4325384 | tf_op jit(solution)/shard_map/ppermute | solution.py:931
  821.8 32.6 %collective-permute-start.58 = (bf16[704,512]{1,0:T(8,128)(2,1)S(1)}, bf16[704,512]{1,0:T(8,128)(2,1)}, u32[]{:S(2)}, u32[]{:S(2)}) collective-permute-start(bf16[704,512]{1,0:T(8,128)(2,1)S(1)} %add_convert_fusion.10), channel_id=1, source_target_pairs={{0,16},{16,0},{1,17},{17,1},{2,18},{18,2},{3,19},{19,3},{4,20},{20... | collective-permute-start | bytes 2162696 | tf_op jit(solution)/shard_map/ppermute | solution.py:931
  823.1 46.3 %collective-permute-start.56 = (bf16[704,512]{1,0:T(8,128)(2,1)}, bf16[704,512]{1,0:T(8,128)(2,1)}, u32[]{:S(2)}, u32[]{:S(2)}) collective-permute-start(bf16[704,512]{1,0:T(8,128)(2,1)} %get-tuple-element.265), channel_id=1, source_target_pairs={{0,16},{16,0},{1,17},{17,1},{2,18},{18,2},{3,19},{19,3},{4,20},{20... | collective-permute-start | bytes 2162696 | tf_op jit(solution)/shard_map/ppermute | solution.py:931
  845.8 33.8 %collective-permute-start.64 = (bf16[704,512]{1,0:T(8,128)(2,1)}, bf16[704,512]{1,0:T(8,128)(2,1)}, u32[]{:S(2)}, u32[]{:S(2)}) collective-permute-start(bf16[704,512]{1,0:T(8,128)(2,1)} %add_convert_fusion.9), channel_id=1, source_target_pairs={{0,2},{1,3},{2,0},{3,1},{4,6},{5,7},{6,4},{7,5},{8,10},{9,11},{10,... | collective-permute-start | bytes 2162696 | tf_op jit(solution)/shard_map/ppermute | solution.py:931
  854.4 48.0 %collective-permute-start.62 = (bf16[1408,512]{1,0:T(8,128)(2,1)}, bf16[1408,512]{1,0:T(8,128)(2,1)}, u32[]{:S(2)}, u32[]{:S(2)}) collective-permute-start(bf16[1408,512]{1,0:T(8,128)(2,1)} %get-tuple-element.272), channel_id=1, source_target_pairs={{0,8},{4,12},{8,0},{12,4},{1,9},{5,13},{9,1},{13,5},{2,10},{6,14},... | collective-permute-start | bytes 4325384 | tf_op jit(solution)/shard_map/ppermute | solution.py:931
  857.0 45.3 %collective-permute-start.60 = (bf16[256,2048]{1,0:T(8,128)(2,1)}, bf16[256,2048]{1,0:T(8,128)(2,1)S(1)}, u32[]{:S(2)}, u32[]{:S(2)}) collective-permute-start(bf16[256,2048]{1,0:T(8,128)(2,1)} %get-tuple-element.270), channel_id=1, source_target_pairs={{0,1},{1,0},{2,3},{3,2},{4,5},{5,4},{6,7},{7,6},{8,9},{9,8},{10,11... | collective-permute-start | bytes 3145736 | tf_op jit(solution)/shard_map/ppermute | solution.py:931
  869.4 65.5 %collective-permute-start.65 = (bf16[1536,512]{1,0:T(8,128)(2,1)}, bf16[1536,512]{1,0:T(8,128)(2,1)}, u32[]{:S(2)}, u32[]{:S(2)}) collective-permute-start(bf16[1536,512]{1,0:T(8,128)(2,1)} %outer.31), channel_id=1, source_target_pairs={{0,8},{4,12},{8,0},{12,4},{1,9},{5,13},{9,1},{13,5},{2,10},{6,14},... | collective-permute-start | bytes 4718600 | tf_op jit(solution)/shard_map/ppermute | solution.py:931
  881.3 45.6 %collective-permute-start.79 = (bf16[704,512]{1,0:T(8,128)(2,1)S(1)}, bf16[704,512]{1,0:T(8,128)(2,1)}, u32[]{:S(2)}, u32[]{:S(2)}) collective-permute-start(bf16[704,512]{1,0:T(8,128)(2,1)S(1)} %add_convert_fusion.8), channel_id=1, source_target_pairs={{0,16},{16,0},{1,17},{17,1},{2,18},{18,2},{3,19},{19,3},{4,20},{20... | collective-permute-start | bytes 2162696 | tf_op jit(solution)/shard_map/ppermute | solution.py:931
  916.0 64.5 %collective-permute-start.61 = (bf16[256,2048]{1,0:T(8,128)(2,1)}, bf16[256,2048]{1,0:T(8,128)(2,1)}, u32[]{:S(2)}, u32[]{:S(2)}) collective-permute-start(bf16[256,2048]{1,0:T(8,128)(2,1)} %add_convert_fusion), channel_id=1, source_target_pairs={{0,2},{1,3},{2,0},{3,1},{4,6},{5,7},{6,4},{7,5},{8,10},{9,11},{10,... | collective-permute-start | bytes 3145736 | tf_op jit(solution)/shard_map/ppermute | solution.py:931
  916.0 48.3 %collective-permute-start.59 = (bf16[256,2048]{1,0:T(8,128)(2,1)}, bf16[256,2048]{1,0:T(8,128)(2,1)}, u32[]{:S(2)}, u32[]{:S(2)}) collective-permute-start(bf16[256,2048]{1,0:T(8,128)(2,1)} %get-tuple-element.269), channel_id=1, source_target_pairs={{0,1},{1,0},{2,3},{3,2},{4,5},{5,4},{6,7},{7,6},{8,9},{9,8},{10,11... | collective-permute-start | bytes 3145736 | tf_op jit(solution)/shard_map/ppermute | solution.py:931
  926.9 44.8 %collective-permute-start.66 = (bf16[512,1024]{1,0:T(8,128)(2,1)}, bf16[512,1024]{1,0:T(8,128)(2,1)S(1)}, u32[]{:S(2)}, u32[]{:S(2)}) collective-permute-start(bf16[512,1024]{1,0:T(8,128)(2,1)} %outer.34), channel_id=1, source_target_pairs={{0,4},{4,0},{8,12},{12,8},{1,5},{5,1},{9,13},{13,9},{2,6},{6,2},{1... | collective-permute-start | bytes 3145736 | tf_op jit(solution)/shard_map/ppermute | solution.py:931
  930.5 45.4 %collective-permute-start.67 = (bf16[512,1024]{1,0:T(8,128)(2,1)}, bf16[512,1024]{1,0:T(8,128)(2,1)}, u32[]{:S(2)}, u32[]{:S(2)}) collective-permute-start(bf16[512,1024]{1,0:T(8,128)(2,1)} %outer.35), channel_id=1, source_target_pairs={{0,4},{4,0},{8,12},{12,8},{1,5},{5,1},{9,13},{13,9},{2,6},{6,2},{1... | collective-permute-start | bytes 3145736 | tf_op jit(solution)/shard_map/ppermute | solution.py:931
  935.0 52.1 %collective-permute-start.68 = (bf16[1536,512]{1,0:T(8,128)(2,1)}, bf16[1536,512]{1,0:T(8,128)(2,1)}, u32[]{:S(2)}, u32[]{:S(2)}) collective-permute-start(bf16[1536,512]{1,0:T(8,128)(2,1)} %outer.32), channel_id=1, source_target_pairs={{0,8},{4,12},{8,0},{12,4},{1,9},{5,13},{9,1},{13,5},{2,10},{6,14},... | collective-permute-start | bytes 4718600 | tf_op jit(solution)/shard_map/ppermute | solution.py:931
  964.4 34.1 %collective-permute-start.80 = (bf16[704,512]{1,0:T(8,128)(2,1)}, bf16[704,512]{1,0:T(8,128)(2,1)}, u32[]{:S(2)}, u32[]{:S(2)}) collective-permute-start(bf16[704,512]{1,0:T(8,128)(2,1)} %get-tuple-element.295), channel_id=1, source_target_pairs={{0,16},{16,0},{1,17},{17,1},{2,18},{18,2},{3,19},{19,3},{4,20},{20... | collective-permute-start | bytes 2162696 | tf_op jit(solution)/shard_map/ppermute | solution.py:931
  971.7 31.4 %collective-permute-start.82 = (bf16[704,512]{1,0:T(8,128)(2,1)}, bf16[704,512]{1,0:T(8,128)(2,1)}, u32[]{:S(2)}, u32[]{:S(2)}) collective-permute-start(bf16[704,512]{1,0:T(8,128)(2,1)} %add_convert_fusion.7), channel_id=1, source_target_pairs={{0,2},{1,3},{2,0},{3,1},{4,6},{5,7},{6,4},{7,5},{8,10},{9,11},{10,... | collective-permute-start | bytes 2162696 | tf_op jit(solution)/shard_map/ppermute | solution.py:931
  987.1 29.5 %collective-permute-start.70 = (bf16[768,512]{1,0:T(8,128)(2,1)}, bf16[768,512]{1,0:T(8,128)(2,1)}, u32[]{:S(2)}, u32[]{:S(2)}) collective-permute-start(bf16[768,512]{1,0:T(8,128)(2,1)} %get-tuple-element.286), channel_id=1, source_target_pairs={{0,16},{16,0},{1,17},{17,1},{2,18},{18,2},{3,19},{19,3},{4,20},{20... | collective-permute-start | bytes 2359304 | tf_op jit(solution)/shard_map/ppermute | solution.py:931
  1004.7 52.5 %collective-permute-start.83 = (bf16[704,512]{1,0:T(8,128)(2,1)S(1)}, bf16[704,512]{1,0:T(8,128)(2,1)}, u32[]{:S(2)}, u32[]{:S(2)}) collective-permute-start(bf16[704,512]{1,0:T(8,128)(2,1)S(1)} %add_convert_fusion.6), channel_id=1, source_target_pairs={{0,16},{16,0},{1,17},{17,1},{2,18},{18,2},{3,19},{19,3},{4,20},{20... | collective-permute-start | bytes 2162696 | tf_op jit(solution)/shard_map/ppermute | solution.py:931
  1010.9 47.6 %collective-permute-start.69 = (bf16[768,512]{1,0:T(8,128)(2,1)}, bf16[768,512]{1,0:T(8,128)(2,1)}, u32[]{:S(2)}, u32[]{:S(2)}) collective-permute-start(bf16[768,512]{1,0:T(8,128)(2,1)} %get-tuple-element.285), channel_id=1, source_target_pairs={{0,16},{16,0},{1,17},{17,1},{2,18},{18,2},{3,19},{19,3},{4,20},{20... | collective-permute-start | bytes 2359304 | tf_op jit(solution)/shard_map/ppermute | solution.py:931
  1013.6 29.5 %collective-permute-start.77 = (bf16[256,512]{1,0:T(8,128)(2,1)S(1)}, bf16[256,512]{1,0:T(8,128)(2,1)S(1)}, u32[]{:S(2)}, u32[]{:S(2)}) collective-permute-start(bf16[256,512]{1,0:T(8,128)(2,1)S(1)} %add_convert_fusion.13), channel_id=1, source_target_pairs={{0,2},{1,3},{2,0},{3,1},{4,6},{5,7},{6,4},{7,5},{8,10},{9,11},{10,... | collective-permute-start | bytes 786440 | tf_op jit(solution)/shard_map/ppermute | solution.py:931
  1018.8 39.7 %collective-permute-start.71 = (bf16[768,512]{1,0:T(8,128)(2,1)}, bf16[768,512]{1,0:T(8,128)(2,1)}, u32[]{:S(2)}, u32[]{:S(2)}) collective-permute-start(bf16[768,512]{1,0:T(8,128)(2,1)} %add_convert_fusion.5), channel_id=1, source_target_pairs={{0,2},{1,3},{2,0},{3,1},{4,6},{5,7},{6,4},{7,5},{8,10},{9,11},{10,... | collective-permute-start | bytes 2359304 | tf_op jit(solution)/shard_map/ppermute | solution.py:931
  1043.2 28.2 %collective-permute-start.78 = (bf16[256,512]{1,0:T(8,128)(2,1)S(1)}, bf16[256,512]{1,0:T(8,128)(2,1)S(1)}, u32[]{:S(2)}, u32[]{:S(2)}) collective-permute-start(bf16[256,512]{1,0:T(8,128)(2,1)S(1)} %add_convert_fusion.12), channel_id=1, source_target_pairs={{0,16},{16,0},{1,17},{17,1},{2,18},{18,2},{3,19},{19,3},{4,20},{20... | collective-permute-start | bytes 786440 | tf_op jit(solution)/shard_map/ppermute | solution.py:931
  (109 other events, 1767.6 us)
Sparse Core Ops, SparseCore 0:
  859.2 192.5 all-reduce.2

commit v3 on v2

--- a/solution.py
+++ b/solution.py
@@ -714,27 +714,29 @@
     width = pieces[0].shape[1]
     count = sum(piece.shape[0] for piece in pieces)
     features = down_weight.count
-    block = block_of(features)
+    block = features // 2 if features % 256 == 0 else features
     factor = (2.0 / math.pi) ** 0.5
     given = len(pieces)
 
     def kernel(*refs):
         gather_rows(refs[:given], refs[-1])
         w0, w1, w2, w3, gate_ref, upper_ref, gg_ref, gu_ref, sg_ref, su_ref, rows_ref = refs[given:]
-        grad = project_block(rows_ref, (w0, w1, w2, w3))
-        value = gate_ref[...].astype(jnp.float32)
-        square = value * value
-        bend = jnp.tanh(factor * value * (1.0 + 0.044715 * square))
-        lift = 0.5 * (1.0 + bend)
-        slope = lift + 0.5 * value * (1.0 - bend * bend) * (
-            factor * (1.0 + 3.0 * 0.044715 * square)
-        )
-        grad_gate = (grad * upper_ref[...].astype(jnp.float32) * slope).astype(jnp.bfloat16)
-        grad_upper = (grad * (value * lift)).astype(jnp.bfloat16)
-        gg_ref[...] = grad_gate
-        gu_ref[...] = grad_upper
-        sg_ref[...] = jnp.sum(grad_gate.astype(jnp.float32), axis=0, keepdims=True)
-        su_ref[...] = jnp.sum(grad_upper.astype(jnp.float32), axis=0, keepdims=True)
+        for start in range(0, block, 512):
+            part = slice(start, min(start + 512, block))
+            grad = project_block(rows_ref, [ref.at[part] for ref in (w0, w1, w2, w3)])
+            value = gate_ref[:, part].astype(jnp.float32)
+            square = value * value
+            bend = jnp.tanh(factor * value * (1.0 + 0.044715 * square))
+            lift = 0.5 * (1.0 + bend)
+            slope = lift + 0.5 * value * (1.0 - bend * bend) * (
+                factor * (1.0 + 3.0 * 0.044715 * square)
+            )
+            grad_gate = (grad * upper_ref[:, part].astype(jnp.float32) * slope).astype(jnp.bfloat16)
+            grad_upper = (grad * (value * lift)).astype(jnp.bfloat16)
+            gg_ref[:, part] = grad_gate
+            gu_ref[:, part] = grad_upper
+            sg_ref[:, part] = jnp.sum(grad_gate.astype(jnp.float32), axis=0, keepdims=True)
+            su_ref[:, part] = jnp.sum(grad_upper.astype(jnp.float32), axis=0, keepdims=True)
 
     out = jax.ShapeDtypeStruct((count, features), jnp.bfloat16)
     row = jax.ShapeDtypeStruct((1, features), jnp.float32)
@@ -1481,9 +1483,9 @@
         ]
     )
     grad_inputs = grad_inputs.astype(wide)
+    qkv_far.to_x(wait=(qkv_far.came_y, states[0]["source"][1]))
     dense_grads[1].to_core(wait=(gate.came_far,))
     dense_grads[0].to_core()
-    qkv_far.to_x(wait=(qkv_far.came_y, states[0]["source"][1]))
     sum_gate = gate.finish()
     dense_grads[1].to_y()
     dense_grads[0].to_y()

time: 1100 us -> 1090 us (level)
    unnamed x195 -> x199, local copies, waits for them, and re-layouts: 34.3 us -> 33.5 us
where the time goes in v3:
time: 1090 us; the launch traced here: 1080 us
  Pallas kernels  473 us (43%)
  waiting for transfers between devices  374 us (34%)
  other arithmetic  77.7 us (7%)
  starting transfers between devices  74.9 us (7%)
  local copies, waits for them, and re-layouts  62.9 us (6%)
  between operations  19.5 us (2%)
    ppermute x83, waiting for transfers between devices, move(): return lax.ppermute(values, axis, moves)  374 us
    pallas_call x21, Pallas kernels, outer(): pl.pallas_call(kernel, grid=(steps,), in_specs=[pl.BlockSpec((count, bloc...  146 us
    pallas_call x8, Pallas kernels, expand(): pl.pallas_call(kernel, grid=(4 * cuts,), in_specs=specs, out_specs=[pl.Bl...  110 us
    ppermute x83, starting transfers between devices, move(): return lax.ppermute(values, axis, moves)  72.3 us
    pallas_call x2, Pallas kernels, ff_forward(): pl.pallas_call(kernel, grid=(features // block,), in_specs=piece_specs(pi...  42.4 us
    pallas_call x2, Pallas kernels, attend_back(): pl.pallas_call(kernel, grid_spec=pltpu.PrefetchScalarGridSpec(num_scalar_...  38.9 us
    pallas_call x10, Pallas kernels, join(): pl.pallas_call(kernel, grid=(steps, 4), in_specs=[source(first) for _, fi...  37.2 us
    pallas_call x2, Pallas kernels, ff_back(): pl.pallas_call(kernel, grid=(features // block,), in_specs=piece_specs(pi...  36.5 us
  transfers between devices with their start and end apart: 85, of which 33 were waited for; matrix products, arithmetic and copies ran while one was open for 10% of the time, Pallas kernels for 35%

profile of v3, /device:TPU:0, one launch (start us, length us, event | category | flops | bytes accessed | tf_op | source)
XLA Modules:
  0.0 1082.2 jit_solution(17350833589178089009)
XLA Ops:
  22.7 14.6 %collective-permute-done.refs_0_ = bf16[1024,512]{1,0:T(8,128)(2,1)S(1)} collective-permute-done((bf16[1024,512]{1,0:T(8,128)(2,1)S(1)}, bf16[1024,512]{1,0:T(8,128)(2,1)S(1)}, u32[]{:S(2)}, u32[]{:S(2)}) %collective-permute-start) | collective-permute-done | bytes 1048608 | tf_op jit(solution)/shard_map/ppermute | solution.py:933
  49.6 20.5 %collective-permute-done.3.refs_2_ = bf16[1024,512]{1,0:T(8,128)(2,1)} collective-permute-done((bf16[1024,512]{1,0:T(8,128)(2,1)S(1)}, bf16[1024,512]{1,0:T(8,128)(2,1)}, u32[]{:S(2)}, u32[]{:S(2)}) %collective-permute-start.3) | collective-permute-done | bytes 1048608 | tf_op jit(solution)/shard_map/ppermute | solution.py:933
  75.5 21.0 %collective-permute-done.8.refs_2_ = bf16[1024,512]{1,0:T(8,128)(2,1)S(1)} collective-permute-done((bf16[1024,512]{1,0:T(8,128)(2,1)}, bf16[1024,512]{1,0:T(8,128)(2,1)S(1)}, u32[]{:S(2)}, u32[]{:S(2)}) %collective-permute-start.8) | collective-permute-done | bytes 1048608 | tf_op jit(solution)/shard_map/ppermute | solution.py:933
  99.0 17.4 %collective-permute-done.1.refs_1_.refs_3_ = bf16[256,2048]{1,0:T(8,128)(2,1)S(1)} collective-permute-done((bf16[256,2048]{1,0:T(8,128)(2,1)S(1)}, bf16[256,2048]{1,0:T(8,128)(2,1)S(1)}, u32[]{:S(2)}, u32[]{:S(2)}) %collective-permute-start.1) | collective-permute-done | bytes 1048608 | tf_op jit(solution)/shard_map/ppermute | solution.py:933
  139.3 19.2 %collective-permute-done.10.refs_3_.refs_5_ = bf16[256,2048]{1,0:T(8,128)(2,1)S(1)} collective-permute-done((bf16[256,2048]{1,0:T(8,128)(2,1)S(1)}, bf16[256,2048]{1,0:T(8,128)(2,1)S(1)}, u32[]{:S(2)}, u32[]{:S(2)}) %collective-permute-start.10) | collective-permute-done | bytes 1048608 | tf_op jit(solution)/shard_map/ppermute | solution.py:933
  159.6 19.2 %project.3.proj_ref = f32[1024,3072]{1,0:T(8,128)} custom-call(bf16[256,2048]{1,0:T(8,128)(2,1)} %copy-done.24, bf16[256,2048]{1,0:T(8,128)(2,1)} %copy-done.28, bf16[256,2048]{1,0:T(8,128)(2,1)} %copy-done.26, bf16[256,2048]{1,0:T(8,128)(2,1)} %copy-done.29, bf16[8192,512]{1,0:T(8,128)(2,1)} %join.13.refs_4_.refs_5_.refs_1_.refs_2_.refs_6_.refs_7_.refs_3_, ...), custom_call_target="tpu_custom_call" | custom-call | flops 6442450944 | bytes 1 | tf_op jit(solution)/shard_map/project/pallas_call | solution.py:664
  178.8 15.0 %attend.2 = (bf16[1024,512]{1,0:T(8,128)(2,1)S(1)}, bf16[1024,1536]{1,0:T(8,128)(2,1)S(1)}, f32[4,1,1024]{2,1,0:T(1,128)S(1)}) custom-call(s32[1]{0:T(128)} %bitcast.6.limit_ref, f32[1024,3072]{1,0:T(8,128)} %project.3.proj_ref, f32[1024,128]{1,0:T(8,128)S(1)} %pad_maximum_fusion.5.cos_ref, f32[1024,128]{1,0:T(8,128)S(1)} %pad_maximum_fusion.6.sin_ref, ...), custom_call_target="tpu_custom_call" | custom-call | flops 2147483648 | bytes 1 | tf_op jit(solution)/shard_map/attend/pallas_call | solution.py:395
  198.8 14.8 %attend.3 = (bf16[1024,512]{1,0:T(8,128)(2,1)S(1)}, bf16[1024,1536]{1,0:T(8,128)(2,1)S(1)}, f32[4,1,1024]{2,1,0:T(1,128)S(1)}) custom-call(s32[1]{0:T(128)} %bitcast.6.limit_ref, f32[1024,3072]{1,0:T(8,128)} %project.3.proj_ref, f32[1024,128]{1,0:T(8,128)S(1)} %pad_maximum_fusion.5.cos_ref, f32[1024,128]{1,0:T(8,128)S(1)} %pad_maximum_fusion.6.sin_ref, ...), custom_call_target="tpu_custom_call" | custom-call | flops 2147483648 | bytes 1 | tf_op jit(solution)/shard_map/attend/pallas_call | solution.py:395
  218.0 6.6 expand.8
  231.6 13.9 %collective-permute-done.18.refs_3_ = bf16[704,512]{1,0:T(8,128)(2,1)S(1)} collective-permute-done((bf16[704,512]{1,0:T(8,128)(2,1)S(1)}, bf16[704,512]{1,0:T(8,128)(2,1)S(1)}, u32[]{:S(2)}, u32[]{:S(2)}) %collective-permute-start.18) | collective-permute-done | bytes 720928 | tf_op jit(solution)/shard_map/ppermute | solution.py:933
  246.3 6.9 expand.9
  253.2 12.3 %collective-permute-done.21.refs_2_ = bf16[704,512]{1,0:T(8,128)(2,1)} collective-permute-done((bf16[704,512]{1,0:T(8,128)(2,1)S(1)}, bf16[704,512]{1,0:T(8,128)(2,1)}, u32[]{:S(2)}, u32[]{:S(2)}) %collective-permute-start.21) | collective-permute-done | bytes 720928 | tf_op jit(solution)/shard_map/ppermute | solution.py:933
  274.2 29.6 %collective-permute-done.19 = bf16[256,2048]{1,0:T(8,128)(2,1)S(1)} collective-permute-done((bf16[256,2048]{1,0:T(8,128)(2,1)}, bf16[256,2048]{1,0:T(8,128)(2,1)S(1)}, u32[]{:S(2)}, u32[]{:S(2)}) %collective-permute-start.19) | collective-permute-done | bytes 1048608 | tf_op jit(solution)/shard_map/ppermute | solution.py:933
  308.0 19.1 %collective-permute-done.20.refs_1_.refs_3_ = bf16[256,2048]{1,0:T(8,128)(2,1)S(1)} collective-permute-done((bf16[256,2048]{1,0:T(8,128)(2,1)S(1)}, bf16[256,2048]{1,0:T(8,128)(2,1)S(1)}, u32[]{:S(2)}, u32[]{:S(2)}) %collective-permute-start.20) | collective-permute-done | bytes 1048608 | tf_op jit(solution)/shard_map/ppermute | solution.py:933
  354.2 5.9 collective-permute-done.30.refs_3_
  372.4 21.1 %ff_forward.2 = (bf16[512,2816]{1,0:T(8,128)(2,1)}, bf16[512,2816]{1,0:T(8,128)(2,1)}, bf16[512,2816]{1,0:T(8,128)(2,1)}) custom-call(bf16[256,2048]{1,0:T(8,128)(2,1)} %copy-done.33, bf16[256,2048]{1,0:T(8,128)(2,1)} %copy-done.35, bf16[5632,512]{1,0:T(8,128)(2,1)} %join.15.refs_2_.refs_3_.refs_1_, bf16[5632,512]{1,0:T(8,128)(2,1)} %join.15.refs_2_.refs_3_.refs_1_, ...), custom_call_target="tpu_custom_call" | custom-call | flops 5905580032 | bytes 1 | tf_op jit(solution)/shard_map/ff_forward/pallas_call | solution.py:697
  393.5 12.9 %expand.10 = (f32[256,2048]{1,0:T(8,128)}, bf16[256,2048]{1,0:T(8,128)(2,1)}) custom-call(bf16[512,2816]{1,0:T(8,128)(2,1)} %get-tuple-element.236.refs_0_, bf16[5632,512]{1,0:T(8,128)(2,1)} %join.19.refs_1_.refs_2_.refs_3_, bf16[5632,512]{1,0:T(8,128)(2,1)} %join.19.refs_1_.refs_2_.refs_3_, ...), custom_call_target="tpu_custom_call" | custom-call | flops 2952790016 | bytes 1 | tf_op jit(solution)/shard_map/expand/pallas_call | solution.py:803
  407.4 12.7 %collective-permute-done.35 = bf16[256,2048]{1,0:T(8,128)(2,1)S(1)} collective-permute-done((bf16[256,2048]{1,0:T(8,128)(2,1)S(1)}, bf16[256,2048]{1,0:T(8,128)(2,1)S(1)}, u32[]{:S(2)}, u32[]{:S(2)}) %collective-permute-start.35) | collective-permute-done | bytes 1048608 | tf_op jit(solution)/shard_map/ppermute | solution.py:933
  420.1 21.3 %ff_forward.3 = (bf16[512,2816]{1,0:T(8,128)(2,1)}, bf16[512,2816]{1,0:T(8,128)(2,1)}, bf16[512,2816]{1,0:T(8,128)(2,1)}) custom-call(bf16[256,2048]{1,0:T(8,128)(2,1)} %copy-done.34, bf16[256,2048]{1,0:T(8,128)(2,1)} %copy-done.36, bf16[5632,512]{1,0:T(8,128)(2,1)} %join.15.refs_2_.refs_3_.refs_1_, bf16[5632,512]{1,0:T(8,128)(2,1)} %join.15.refs_2_.refs_3_.refs_1_, ...), custom_call_target="tpu_custom_call" | custom-call | flops 5905580032 | bytes 1 | tf_op jit(solution)/shard_map/ff_forward/pallas_call | solution.py:697
  441.4 13.0 %expand.11 = (f32[256,2048]{1,0:T(8,128)}, bf16[256,2048]{1,0:T(8,128)(2,1)}) custom-call(bf16[512,2816]{1,0:T(8,128)(2,1)} %get-tuple-element.206.refs_0_.refs_1_, bf16[5632,512]{1,0:T(8,128)(2,1)} %join.19.refs_1_.refs_2_.refs_3_, bf16[5632,512]{1,0:T(8,128)(2,1)} %join.19.refs_1_.refs_2_.refs_3_, ...), custom_call_target="tpu_custom_call" | custom-call | flops 2952790016 | bytes 1 | tf_op jit(solution)/shard_map/expand/pallas_call | solution.py:803
  465.1 15.6 %collective-permute-done.36 = bf16[256,2048]{1,0:T(8,128)(2,1)S(1)} collective-permute-done((bf16[256,2048]{1,0:T(8,128)(2,1)}, bf16[256,2048]{1,0:T(8,128)(2,1)S(1)}, u32[]{:S(2)}, u32[]{:S(2)}) %collective-permute-start.36) | collective-permute-done | bytes 1048608 | tf_op jit(solution)/shard_map/ppermute | solution.py:933
  485.4 16.4 %collective-permute-done.37.refs_1_.refs_3_ = bf16[256,2048]{1,0:T(8,128)(2,1)S(1)} collective-permute-done((bf16[256,2048]{1,0:T(8,128)(2,1)S(1)}, bf16[256,2048]{1,0:T(8,128)(2,1)S(1)}, u32[]{:S(2)}, u32[]{:S(2)}) %collective-permute-start.37) | collective-permute-done | bytes 1048608 | tf_op jit(solution)/shard_map/ppermute | solution.py:933
  503.1 18.2 %ff_back.2 = (bf16[512,2816]{1,0:T(8,128)(2,1)}, bf16[512,2816]{1,0:T(8,128)(2,1)}, f32[1,2816]{1,0:T(1,128)}, f32[1,2816]{1,0:T(1,128)}) custom-call(bf16[256,2048]{1,0:T(8,128)(2,1)} %copy-done.39, bf16[256,2048]{1,0:T(8,128)(2,1)} %copy-done.49, bf16[5632,512]{1,0:T(8,128)(2,1)} %join.19.refs_1_.refs_2_.refs_3_, ...), custom_call_target="tpu_custom_call" | custom-call | flops 4429185024 | bytes 1 | tf_op jit(solution)/shard_map/ff_back/pallas_call | solution.py:743
  521.3 5.6 collective-permute-done.38.refs_5_.refs_1_
  526.9 21.4 %expand.12 = (f32[256,2048]{1,0:T(8,128)}, bf16[256,2048]{1,0:T(8,128)(2,1)}) custom-call(bf16[512,2816]{1,0:T(8,128)(2,1)} %get-tuple-element.252.refs_0_, bf16[5632,512]{1,0:T(8,128)(2,1)} %join.15.refs_2_.refs_3_.refs_1_, bf16[5632,512]{1,0:T(8,128)(2,1)} %join.15.refs_2_.refs_3_.refs_1_, ...), custom_call_target="tpu_custom_call" | custom-call | flops 5905580032 | bytes 1 | tf_op jit(solution)/shard_map/expand/pallas_call | solution.py:803
  548.3 10.6 outer.21
  559.5 18.4 %ff_back.3 = (bf16[512,2816]{1,0:T(8,128)(2,1)}, bf16[512,2816]{1,0:T(8,128)(2,1)}, f32[1,2816]{1,0:T(1,128)}, f32[1,2816]{1,0:T(1,128)}) custom-call(bf16[256,2048]{1,0:T(8,128)(2,1)} %get-tuple-element.218.refs_4_.refs_0_, bf16[256,2048]{1,0:T(8,128)(2,1)} %copy-done.50, bf16[5632,512]{1,0:T(8,128)(2,1)} %join.19.refs_1_.refs_2_.refs_3_, ...), custom_call_target="tpu_custom_call" | custom-call | flops 4429185024 | bytes 1 | tf_op jit(solution)/shard_map/ff_back/pallas_call | solution.py:743
  577.9 6.8 collective-permute-done.39
  591.0 8.8 outer.22
  599.7 21.3 %expand.13 = (f32[256,2048]{1,0:T(8,128)}, bf16[256,2048]{1,0:T(8,128)(2,1)}) custom-call(bf16[512,2816]{1,0:T(8,128)(2,1)} %get-tuple-element.224.refs_0_.refs_1_, bf16[5632,512]{1,0:T(8,128)(2,1)} %join.15.refs_2_.refs_3_.refs_1_, bf16[5632,512]{1,0:T(8,128)(2,1)} %join.15.refs_2_.refs_3_.refs_1_, ...), custom_call_target="tpu_custom_call" | custom-call | flops 5905580032 | bytes 1 | tf_op jit(solution)/shard_map/expand/pallas_call | solution.py:803
  621.0 10.6 outer.23
  635.9 10.5 outer.24
  646.5 11.6 %collective-permute-done.42 = bf16[256,2048]{1,0:T(8,128)(2,1)} collective-permute-done((bf16[256,2048]{1,0:T(8,128)(2,1)}, bf16[256,2048]{1,0:T(8,128)(2,1)}, u32[]{:S(2)}, u32[]{:S(2)}) %collective-permute-start.42) | collective-permute-done | bytes 1048608 | tf_op jit(solution)/shard_map/ppermute | solution.py:933
  664.6 15.6 %collective-permute-done.43.refs_1_.refs_3_ = bf16[256,2048]{1,0:T(8,128)(2,1)} collective-permute-done((bf16[256,2048]{1,0:T(8,128)(2,1)S(1)}, bf16[256,2048]{1,0:T(8,128)(2,1)}, u32[]{:S(2)}, u32[]{:S(2)}) %collective-permute-start.43) | collective-permute-done | bytes 1048608 | tf_op jit(solution)/shard_map/ppermute | solution.py:933
  681.4 6.3 project.4.grad_first
  687.7 8.4 outer.25
  699.8 9.4 outer.26
  710.2 6.3 project.5.grad_second
  717.8 19.7 %attend_back.2 = (bf16[1024,1536]{1,0:T(8,128)(2,1)}, f32[4,1,384]{2,1,0:T(1,128)S(1)}) custom-call(s32[1]{0:T(128)} %bitcast.6.limit_ref, bf16[1024,1536]{1,0:T(8,128)(2,1)} %copy-done.14, bf16[512,1024]{1,0:T(8,128)(2,1)S(1)} %copy-done.8, bf16[512,1024]{1,0:T(8,128)(2,1)S(1)} %copy-done.9, f32[4,1,1024]{2,1,0:T(1,128)S(1)} %get-tuple-element.241.lse_ref, ...), custom_call_target="tpu_custom_call" | custom-call | flops 2684354560 | bytes 1 | tf_op jit(solution)/shard_map/attend_back/pallas_call | solution.py:525
  737.5 8.9 collective-permute-done.41
  747.3 7.6 outer.27
  762.0 8.3 outer.28
  770.3 6.9 collective-permute-done.51
  778.4 19.2 %attend_back.3 = (bf16[1024,1536]{1,0:T(8,128)(2,1)}, f32[4,1,384]{2,1,0:T(1,128)S(1)}) custom-call(s32[1]{0:T(128)} %bitcast.6.limit_ref, bf16[1024,1536]{1,0:T(8,128)(2,1)} %copy-done.13, bf16[512,1024]{1,0:T(8,128)(2,1)S(1)} %copy-done.8, bf16[512,1024]{1,0:T(8,128)(2,1)S(1)} %copy-done.10, f32[4,1,1024]{2,1,0:T(1,128)S(1)} %get-tuple-element.250.lse_ref, ...), custom_call_target="tpu_custom_call" | custom-call | flops 2684354560 | bytes 1 | tf_op jit(solution)/shard_map/attend_back/pallas_call | solution.py:525
  798.7 9.6 outer.29
  808.2 7.7 outer.30
  823.2 5.8 outer.31
  828.9 14.1 %expand.14 = (f32[256,2048]{1,0:T(8,128)}, bf16[256,2048]{1,0:T(8,128)(2,1)}) custom-call(bf16[1024,1536]{1,0:T(8,128)(2,1)} %get-tuple-element.283.refs_0_.refs_1_, bf16[8192,512]{1,0:T(8,128)(2,1)} %join.13.refs_4_.refs_5_.refs_1_.refs_2_.refs_6_.refs_7_.refs_3_, bf16[8192,512]{1,0:T(8,128)(2,1)} %join.13.refs_4_.refs_5_.refs_1_.refs_2_.refs_6_.refs_7_.refs_3_, ...), custom_call_target="tpu_custom_call" | custom-call | flops 3221225472 | bytes 1 | tf_op jit(solution)/shard_map/expand/pallas_call | solution.py:803
  846.8 6.9 collective-permute-done.58
  858.4 10.3 collective-permute-done.56
  870.2 8.9 collective-permute-done.65
  882.0 5.7 outer.32
  887.7 13.9 %expand.15 = (f32[256,2048]{1,0:T(8,128)}, bf16[256,2048]{1,0:T(8,128)(2,1)}) custom-call(bf16[1024,1536]{1,0:T(8,128)(2,1)} %get-tuple-element.283.refs_0_.refs_1_, bf16[8192,512]{1,0:T(8,128)(2,1)} %join.13.refs_4_.refs_5_.refs_1_.refs_2_.refs_6_.refs_7_.refs_3_, bf16[8192,512]{1,0:T(8,128)(2,1)} %join.13.refs_4_.refs_5_.refs_1_.refs_2_.refs_6_.refs_7_.refs_3_, ...), custom_call_target="tpu_custom_call" | custom-call | flops 3221225472 | bytes 1 | tf_op jit(solution)/shard_map/expand/pallas_call | solution.py:803
  901.6 9.8 outer.33
  920.6 9.1 collective-permute-done.81
  931.4 24.9 %collective-permute-done.59 = bf16[256,2048]{1,0:T(8,128)(2,1)} collective-permute-done((bf16[256,2048]{1,0:T(8,128)(2,1)}, bf16[256,2048]{1,0:T(8,128)(2,1)}, u32[]{:S(2)}, u32[]{:S(2)}) %collective-permute-start.59) | collective-permute-done | bytes 1048608 | tf_op jit(solution)/shard_map/ppermute | solution.py:933
  956.3 6.1 outer.34
  967.7 13.3 %collective-permute-done.61 = bf16[256,2048]{1,0:T(8,128)(2,1)} collective-permute-done((bf16[256,2048]{1,0:T(8,128)(2,1)}, bf16[256,2048]{1,0:T(8,128)(2,1)}, u32[]{:S(2)}, u32[]{:S(2)}) %collective-permute-start.61) | collective-permute-done | bytes 1048608 | tf_op jit(solution)/shard_map/ppermute | solution.py:933
  991.0 4.3 collective-permute-done.82
  1012.5 6.1 outer.39
  1028.3 6.5 copy.54
  1040.3 4.7 collective-permute-done.76
  1051.6 5.0 collective-permute-done.77
  1062.8 7.5 collective-permute-done.78
  (533 shorter events, 273.3 us)
Async XLA Ops:
  7.2 1050.3 %all-reduce.3.cloned.1.call-start = ((), (), s32[]{:S(2)}) async-start(), calls=%async_computation | async-start | bytes 278528 | tf_op jit(solution)/shard_map/psum | solution.py:1455
  11.1 26.2 %collective-permute-start = (bf16[1024,512]{1,0:T(8,128)(2,1)S(1)}, bf16[1024,512]{1,0:T(8,128)(2,1)S(1)}, u32[]{:S(2)}, u32[]{:S(2)}) collective-permute-start(bf16[1024,512]{1,0:T(8,128)(2,1)S(1)} %pad_maximum_fusion.3.refs_0_), channel_id=1, source_target_pairs={{0,8},{4,12},{8,0},{12,4},{1,9},{5,13},{9,1},{13,5},{2,10},{6,14},... | collective-permute-start | bytes 3145736 | tf_op jit(solution)/shard_map/ppermute | solution.py:933
  22.3 47.8 %collective-permute-start.3 = (bf16[1024,512]{1,0:T(8,128)(2,1)S(1)}, bf16[1024,512]{1,0:T(8,128)(2,1)}, u32[]{:S(2)}, u32[]{:S(2)}) collective-permute-start(bf16[1024,512]{1,0:T(8,128)(2,1)S(1)} %pad_maximum_fusion.3.refs_0_), channel_id=1, source_target_pairs={{0,2},{1,3},{2,0},{3,1},{4,6},{5,7},{6,4},{7,5},{8,10},{9,11},{10,... | collective-permute-start | bytes 3145736 | tf_op jit(solution)/shard_map/ppermute | solution.py:933
  37.3 32.9 %collective-permute-start.4 = (bf16[1024,512]{1,0:T(8,128)(2,1)S(1)}, bf16[1024,512]{1,0:T(8,128)(2,1)}, u32[]{:S(2)}, u32[]{:S(2)}) collective-permute-start(bf16[1024,512]{1,0:T(8,128)(2,1)S(1)} %collective-permute-done.refs_0_), channel_id=1, source_target_pairs={{0,16},{16,0},{1,17},{17,1},{2,18},{18,2},{3,19},{19,3},{4,20},{20... | collective-permute-start | bytes 3145736 | tf_op jit(solution)/shard_map/ppermute | solution.py:933
  70.2 26.3 %collective-permute-start.8 = (bf16[1024,512]{1,0:T(8,128)(2,1)}, bf16[1024,512]{1,0:T(8,128)(2,1)S(1)}, u32[]{:S(2)}, u32[]{:S(2)}) collective-permute-start(bf16[1024,512]{1,0:T(8,128)(2,1)} %collective-permute-done.3.refs_2_), channel_id=1, source_target_pairs={{0,8},{4,12},{8,0},{12,4},{1,9},{5,13},{9,1},{13,5},{2,10},{6,14},... | collective-permute-start | bytes 3145736 | tf_op jit(solution)/shard_map/ppermute | solution.py:933
  70.7 54.7 %collective-permute-start.7 = (bf16[1408,512]{1,0:T(8,128)(2,1)}, bf16[1408,512]{1,0:T(8,128)(2,1)}, u32[]{:S(2)}, u32[]{:S(2)}) collective-permute-start(bf16[1408,512]{1,0:T(8,128)(2,1)} %pad_maximum_fusion.2), channel_id=1, source_target_pairs={{0,8},{4,12},{8,0},{12,4},{1,9},{5,13},{9,1},{13,5},{2,10},{6,14},... | collective-permute-start | bytes 4325384 | tf_op jit(solution)/shard_map/ppermute | solution.py:933
  72.2 44.2 %collective-permute-start.1 = (bf16[256,2048]{1,0:T(8,128)(2,1)S(1)}, bf16[256,2048]{1,0:T(8,128)(2,1)S(1)}, u32[]{:S(2)}, u32[]{:S(2)}) collective-permute-start(bf16[256,2048]{1,0:T(8,128)(2,1)S(1)} %get-tuple-element.165.refs_0_.refs_2_), channel_id=1, source_target_pairs={{0,1},{1,0},{2,3},{3,2},{4,5},{5,4},{6,7},{7,6},{8,9},{9,8},{10,11... | collective-permute-start | bytes 3145736 | tf_op jit(solution)/shard_map/ppermute | solution.py:933
  72.2 45.3 %collective-permute-start.5 = (bf16[1024,512]{1,0:T(8,128)(2,1)}, bf16[1024,512]{1,0:T(8,128)(2,1)}, u32[]{:S(2)}, u32[]{:S(2)}) collective-permute-start(bf16[1024,512]{1,0:T(8,128)(2,1)} %collective-permute-done.3.refs_2_), channel_id=1, source_target_pairs={{0,16},{16,0},{1,17},{17,1},{2,18},{18,2},{3,19},{19,3},{4,20},{20... | collective-permute-start | bytes 3145736 | tf_op jit(solution)/shard_map/ppermute | solution.py:933
  73.7 50.7 %collective-permute-start.6 = (bf16[256,2048]{1,0:T(8,128)(2,1)}, bf16[256,2048]{1,0:T(8,128)(2,1)S(1)}, u32[]{:S(2)}, u32[]{:S(2)}) collective-permute-start(bf16[256,2048]{1,0:T(8,128)(2,1)} %get-tuple-element.161), channel_id=1, source_target_pairs={{0,2},{1,3},{2,0},{3,1},{4,6},{5,7},{6,4},{7,5},{8,10},{9,11},{10,... | collective-permute-start | bytes 3145736 | tf_op jit(solution)/shard_map/ppermute | solution.py:933
  96.5 28.9 %collective-permute-start.9 = (bf16[1024,512]{1,0:T(8,128)(2,1)S(1)}, bf16[1024,512]{1,0:T(8,128)(2,1)}, u32[]{:S(2)}, u32[]{:S(2)}) collective-permute-start(bf16[1024,512]{1,0:T(8,128)(2,1)S(1)} %collective-permute-done.8.refs_2_), channel_id=1, source_target_pairs={{0,16},{16,0},{1,17},{17,1},{2,18},{18,2},{3,19},{19,3},{4,20},{20... | collective-permute-start | bytes 3145736 | tf_op jit(solution)/shard_map/ppermute | solution.py:933
  132.2 27.4 %collective-permute-start.11 = (bf16[8192,512]{1,0:T(8,128)(2,1)}, bf16[8192,512]{1,0:T(8,128)(2,1)}, u32[]{:S(2)}, u32[]{:S(2)}) collective-permute-start(bf16[8192,512]{1,0:T(8,128)(2,1)} %join.13.refs_4_.refs_5_.refs_1_.refs_2_.refs_6_.refs_7_.refs_3_), channel_id=1, source_target_pairs={{0,4},{4,0},{8,12},{12,8},{1,5},{5,1},{9,13},{13,9},{2,6},{6,2},{1... | collective-permute-start | bytes 25165832 | tf_op jit(solution)/shard_map/ppermute | solution.py:933
  132.8 25.6 %collective-permute-start.10 = (bf16[256,2048]{1,0:T(8,128)(2,1)S(1)}, bf16[256,2048]{1,0:T(8,128)(2,1)S(1)}, u32[]{:S(2)}, u32[]{:S(2)}) collective-permute-start(bf16[256,2048]{1,0:T(8,128)(2,1)S(1)} %collective-permute-done.6.refs_2_.refs_4_), channel_id=1, source_target_pairs={{0,1},{1,0},{2,3},{3,2},{4,5},{5,4},{6,7},{7,6},{8,9},{9,8},{10,11... | collective-permute-start | bytes 3145736 | tf_op jit(solution)/shard_map/ppermute | solution.py:933
  136.2 42.6 %collective-permute-start.12 = (bf16[704,512]{1,0:T(8,128)(2,1)}, bf16[704,512]{1,0:T(8,128)(2,1)}, u32[]{:S(2)}, u32[]{:S(2)}) collective-permute-start(bf16[704,512]{1,0:T(8,128)(2,1)} %get-tuple-element.192.refs_0_), channel_id=1, source_target_pairs={{0,8},{4,12},{8,0},{12,4},{1,9},{5,13},{9,1},{13,5},{2,10},{6,14},... | collective-permute-start | bytes 2162696 | tf_op jit(solution)/shard_map/ppermute | solution.py:933
  136.8 62.0 %collective-permute-start.13 = (bf16[1408,512]{1,0:T(8,128)(2,1)}, bf16[1408,512]{1,0:T(8,128)(2,1)}, u32[]{:S(2)}, u32[]{:S(2)}) collective-permute-start(bf16[1408,512]{1,0:T(8,128)(2,1)} %collective-permute-done.7.refs_0_), channel_id=1, source_target_pairs={{0,16},{16,0},{1,17},{17,1},{2,18},{18,2},{3,19},{19,3},{4,20},{20... | collective-permute-start | bytes 4325384 | tf_op jit(solution)/shard_map/ppermute | solution.py:933
  158.5 38.1 %collective-permute-start.14 = (bf16[704,512]{1,0:T(8,128)(2,1)}, bf16[704,512]{1,0:T(8,128)(2,1)S(1)}, u32[]{:S(2)}, u32[]{:S(2)}) collective-permute-start(bf16[704,512]{1,0:T(8,128)(2,1)} %bitcast.12.refs_0_), channel_id=1, source_target_pairs={{0,2},{1,3},{2,0},{3,1},{4,6},{5,7},{6,4},{7,5},{8,10},{9,11},{10,... | collective-permute-start | bytes 2162696 | tf_op jit(solution)/shard_map/ppermute | solution.py:933
  224.6 46.1 %collective-permute-start.17 = (bf16[256,2048]{1,0:T(8,128)(2,1)}, bf16[256,2048]{1,0:T(8,128)(2,1)S(1)}, u32[]{:S(2)}, u32[]{:S(2)}) collective-permute-start(bf16[256,2048]{1,0:T(8,128)(2,1)} %get-tuple-element.176), channel_id=1, source_target_pairs={{0,1},{1,0},{2,3},{3,2},{4,5},{5,4},{6,7},{7,6},{8,9},{9,8},{10,11... | collective-permute-start | bytes 3145736 | tf_op jit(solution)/shard_map/ppermute | solution.py:933
  226.9 38.6 %collective-permute-start.21 = (bf16[704,512]{1,0:T(8,128)(2,1)S(1)}, bf16[704,512]{1,0:T(8,128)(2,1)}, u32[]{:S(2)}, u32[]{:S(2)}) collective-permute-start(bf16[704,512]{1,0:T(8,128)(2,1)S(1)} %bitcast.165), channel_id=1, source_target_pairs={{0,2},{1,3},{2,0},{3,1},{4,6},{5,7},{6,4},{7,5},{8,10},{9,11},{10,... | collective-permute-start | bytes 2162696 | tf_op jit(solution)/shard_map/ppermute | solution.py:933
  228.0 77.9 %collective-permute-start.24 = (bf16[704,512]{1,0:T(8,128)(2,1)}, bf16[704,512]{1,0:T(8,128)(2,1)}, u32[]{:S(2)}, u32[]{:S(2)}) collective-permute-start(bf16[704,512]{1,0:T(8,128)(2,1)} %get-tuple-element.192.refs_0_), channel_id=1, source_target_pairs={{0,2},{1,3},{2,0},{3,1},{4,6},{5,7},{6,4},{7,5},{8,10},{9,11},{10,... | collective-permute-start | bytes 2162696 | tf_op jit(solution)/shard_map/ppermute | solution.py:933
  230.0 99.7 %collective-permute-start.25 = (bf16[704,512]{1,0:T(8,128)(2,1)}, bf16[704,512]{1,0:T(8,128)(2,1)}, u32[]{:S(2)}, u32[]{:S(2)}) collective-permute-start(bf16[704,512]{1,0:T(8,128)(2,1)} %collective-permute-done.12.refs_0_), channel_id=1, source_target_pairs={{0,16},{16,0},{1,17},{17,1},{2,18},{18,2},{3,19},{19,3},{4,20},{20... | collective-permute-start | bytes 2162696 | tf_op jit(solution)/shard_map/ppermute | solution.py:933
  265.5 64.6 %collective-permute-start.23 = (bf16[704,512]{1,0:T(8,128)(2,1)}, bf16[704,512]{1,0:T(8,128)(2,1)}, u32[]{:S(2)}, u32[]{:S(2)}) collective-permute-start(bf16[704,512]{1,0:T(8,128)(2,1)} %collective-permute-done.21.refs_2_), channel_id=1, source_target_pairs={{0,16},{16,0},{1,17},{17,1},{2,18},{18,2},{3,19},{19,3},{4,20},{20... | collective-permute-start | bytes 2162696 | tf_op jit(solution)/shard_map/ppermute | solution.py:933
  266.0 41.4 %collective-permute-start.22 = (bf16[704,512]{1,0:T(8,128)(2,1)}, bf16[704,512]{1,0:T(8,128)(2,1)}, u32[]{:S(2)}, u32[]{:S(2)}) collective-permute-start(bf16[704,512]{1,0:T(8,128)(2,1)} %collective-permute-done.21.refs_2_), channel_id=1, source_target_pairs={{0,8},{4,12},{8,0},{12,4},{1,9},{5,13},{9,1},{13,5},{2,10},{6,14},... | collective-permute-start | bytes 2162696 | tf_op jit(solution)/shard_map/ppermute | solution.py:933
  270.7 33.2 %collective-permute-start.19 = (bf16[256,2048]{1,0:T(8,128)(2,1)}, bf16[256,2048]{1,0:T(8,128)(2,1)S(1)}, u32[]{:S(2)}, u32[]{:S(2)}) collective-permute-start(bf16[256,2048]{1,0:T(8,128)(2,1)} %get-tuple-element.180), channel_id=1, source_target_pairs={{0,1},{1,0},{2,3},{3,2},{4,5},{5,4},{6,7},{7,6},{8,9},{9,8},{10,11... | collective-permute-start | bytes 3145736 | tf_op jit(solution)/shard_map/ppermute | solution.py:933
  305.9 31.9 %collective-permute-start.29 = (bf16[704,512]{1,0:T(8,128)(2,1)}, bf16[704,512]{1,0:T(8,128)(2,1)}, u32[]{:S(2)}, u32[]{:S(2)}) collective-permute-start(bf16[704,512]{1,0:T(8,128)(2,1)} %collective-permute-done.24.refs_2_), channel_id=1, source_target_pairs={{0,8},{4,12},{8,0},{12,4},{1,9},{5,13},{9,1},{13,5},{2,10},{6,14},... | collective-permute-start | bytes 2162696 | tf_op jit(solution)/shard_map/ppermute | solution.py:933
  307.5 38.1 %collective-permute-start.26 = (bf16[704,512]{1,0:T(8,128)(2,1)}, bf16[704,512]{1,0:T(8,128)(2,1)}, u32[]{:S(2)}, u32[]{:S(2)}) collective-permute-start(bf16[704,512]{1,0:T(8,128)(2,1)} %collective-permute-done.22.refs_2_), channel_id=1, source_target_pairs={{0,16},{16,0},{1,17},{17,1},{2,18},{18,2},{3,19},{19,3},{4,20},{20... | collective-permute-start | bytes 2162696 | tf_op jit(solution)/shard_map/ppermute | solution.py:933
  341.7 30.7 %collective-permute-start.31 = (bf16[5632,512]{1,0:T(8,128)(2,1)}, bf16[5632,512]{1,0:T(8,128)(2,1)}, u32[]{:S(2)}, u32[]{:S(2)}) collective-permute-start(bf16[5632,512]{1,0:T(8,128)(2,1)} %join.15.refs_2_.refs_3_.refs_1_), channel_id=1, source_target_pairs={{0,4},{4,0},{8,12},{12,8},{1,5},{5,1},{9,13},{13,9},{2,6},{6,2},{1... | collective-permute-start | bytes 17301512 | tf_op jit(solution)/shard_map/ppermute | solution.py:933
  364.0 29.5 %collective-permute-start.33 = (bf16[5632,512]{1,0:T(8,128)(2,1)}, bf16[5632,512]{1,0:T(8,128)(2,1)}, u32[]{:S(2)}, u32[]{:S(2)}) collective-permute-start(bf16[5632,512]{1,0:T(8,128)(2,1)} %join.19.refs_1_.refs_2_.refs_3_), channel_id=1, source_target_pairs={{0,4},{4,0},{8,12},{12,8},{1,5},{5,1},{9,13},{13,9},{2,6},{6,2},{1... | collective-permute-start | bytes 17301512 | tf_op jit(solution)/shard_map/ppermute | solution.py:933
  371.0 49.0 %collective-permute-start.35 = (bf16[256,2048]{1,0:T(8,128)(2,1)S(1)}, bf16[256,2048]{1,0:T(8,128)(2,1)S(1)}, u32[]{:S(2)}, u32[]{:S(2)}) collective-permute-start(bf16[256,2048]{1,0:T(8,128)(2,1)S(1)} %dynamic-slice_bitcast_fusion), channel_id=1, source_target_pairs={{0,2},{1,3},{2,0},{3,1},{4,6},{5,7},{6,4},{7,5},{8,10},{9,11},{10,... | collective-permute-start | bytes 3145736 | tf_op jit(solution)/shard_map/ppermute | solution.py:933
  406.3 48.1 %collective-permute-start.34 = (bf16[256,2048]{1,0:T(8,128)(2,1)}, bf16[256,2048]{1,0:T(8,128)(2,1)S(1)}, u32[]{:S(2)}, u32[]{:S(2)}) collective-permute-start(bf16[256,2048]{1,0:T(8,128)(2,1)} %get-tuple-element.201), channel_id=1, source_target_pairs={{0,1},{1,0},{2,3},{3,2},{4,5},{5,4},{6,7},{7,6},{8,9},{9,8},{10,11... | collective-permute-start | bytes 3145736 | tf_op jit(solution)/shard_map/ppermute | solution.py:933
  454.4 26.3 %collective-permute-start.36 = (bf16[256,2048]{1,0:T(8,128)(2,1)}, bf16[256,2048]{1,0:T(8,128)(2,1)S(1)}, u32[]{:S(2)}, u32[]{:S(2)}) collective-permute-start(bf16[256,2048]{1,0:T(8,128)(2,1)} %get-tuple-element.208), channel_id=1, source_target_pairs={{0,1},{1,0},{2,3},{3,2},{4,5},{5,4},{6,7},{7,6},{8,9},{9,8},{10,11... | collective-permute-start | bytes 3145736 | tf_op jit(solution)/shard_map/ppermute | solution.py:933
  463.0 38.8 %collective-permute-start.37 = (bf16[256,2048]{1,0:T(8,128)(2,1)S(1)}, bf16[256,2048]{1,0:T(8,128)(2,1)S(1)}, u32[]{:S(2)}, u32[]{:S(2)}) collective-permute-start(bf16[256,2048]{1,0:T(8,128)(2,1)S(1)} %get-tuple-element.210.refs_0_.refs_2_), channel_id=1, source_target_pairs={{0,1},{1,0},{2,3},{3,2},{4,5},{5,4},{6,7},{7,6},{8,9},{9,8},{10,11... | collective-permute-start | bytes 3145736 | tf_op jit(solution)/shard_map/ppermute | solution.py:933
  502.8 24.1 %collective-permute-start.38 = (bf16[256,2048]{1,0:T(8,128)(2,1)}, bf16[256,2048]{1,0:T(8,128)(2,1)S(1)}, u32[]{:S(2)}, u32[]{:S(2)}) collective-permute-start(bf16[256,2048]{1,0:T(8,128)(2,1)} %get-tuple-element.218.refs_4_.refs_0_), channel_id=1, source_target_pairs={{0,1},{1,0},{2,3},{3,2},{4,5},{5,4},{6,7},{7,6},{8,9},{9,8},{10,11... | collective-permute-start | bytes 3145736 | tf_op jit(solution)/shard_map/ppermute | solution.py:933
  558.9 32.1 %collective-permute-start.40 = (bf16[2816,1024]{1,0:T(8,128)(2,1)}, bf16[2816,1024]{1,0:T(8,128)(2,1)}, u32[]{:S(2)}, u32[]{:S(2)}) collective-permute-start(bf16[2816,1024]{1,0:T(8,128)(2,1)} %outer.21), channel_id=1, source_target_pairs={{0,4},{4,0},{8,12},{12,8},{1,5},{5,1},{9,13},{13,9},{2,6},{6,2},{1... | collective-permute-start | bytes 17301512 | tf_op jit(solution)/shard_map/ppermute | solution.py:933
  558.9 25.8 %collective-permute-start.39 = (bf16[256,2048]{1,0:T(8,128)(2,1)}, bf16[256,2048]{1,0:T(8,128)(2,1)S(1)}, u32[]{:S(2)}, u32[]{:S(2)}) collective-permute-start(bf16[256,2048]{1,0:T(8,128)(2,1)} %get-tuple-element.221), channel_id=1, source_target_pairs={{0,1},{1,0},{2,3},{3,2},{4,5},{5,4},{6,7},{7,6},{8,9},{9,8},{10,11... | collective-permute-start | bytes 3145736 | tf_op jit(solution)/shard_map/ppermute | solution.py:933
  631.6 56.1 %collective-permute-start.44 = (bf16[2816,1024]{1,0:T(8,128)(2,1)}, bf16[2816,1024]{1,0:T(8,128)(2,1)}, u32[]{:S(2)}, u32[]{:S(2)}) collective-permute-start(bf16[2816,1024]{1,0:T(8,128)(2,1)} %outer.23), channel_id=1, source_target_pairs={{0,4},{4,0},{8,12},{12,8},{1,5},{5,1},{9,13},{13,9},{2,6},{6,2},{1... | collective-permute-start | bytes 17301512 | tf_op jit(solution)/shard_map/ppermute | solution.py:933
  631.8 26.3 %collective-permute-start.42 = (bf16[256,2048]{1,0:T(8,128)(2,1)}, bf16[256,2048]{1,0:T(8,128)(2,1)}, u32[]{:S(2)}, u32[]{:S(2)}) collective-permute-start(bf16[256,2048]{1,0:T(8,128)(2,1)} %get-tuple-element.231), channel_id=1, source_target_pairs={{0,1},{1,0},{2,3},{3,2},{4,5},{5,4},{6,7},{7,6},{8,9},{9,8},{10,11... | collective-permute-start | bytes 3145736 | tf_op jit(solution)/shard_map/ppermute | solution.py:933
  632.5 47.7 %collective-permute-start.43 = (bf16[256,2048]{1,0:T(8,128)(2,1)S(1)}, bf16[256,2048]{1,0:T(8,128)(2,1)}, u32[]{:S(2)}, u32[]{:S(2)}) collective-permute-start(bf16[256,2048]{1,0:T(8,128)(2,1)S(1)} %get-tuple-element.232.refs_0_.refs_2_), channel_id=1, source_target_pairs={{0,1},{1,0},{2,3},{3,2},{4,5},{5,4},{6,7},{7,6},{8,9},{9,8},{10,11... | collective-permute-start | bytes 3145736 | tf_op jit(solution)/shard_map/ppermute | solution.py:933
  633.9 66.0 %collective-permute-start.45 = (bf16[1408,512]{1,0:T(8,128)(2,1)}, bf16[1408,512]{1,0:T(8,128)(2,1)}, u32[]{:S(2)}, u32[]{:S(2)}) collective-permute-start(bf16[1408,512]{1,0:T(8,128)(2,1)} %get-tuple-element.223), channel_id=1, source_target_pairs={{0,8},{4,12},{8,0},{12,4},{1,9},{5,13},{9,1},{13,5},{2,10},{6,14},... | collective-permute-start | bytes 4325384 | tf_op jit(solution)/shard_map/ppermute | solution.py:933
  635.3 63.2 %collective-permute-start.46 = (bf16[1408,512]{1,0:T(8,128)(2,1)}, bf16[1408,512]{1,0:T(8,128)(2,1)}, u32[]{:S(2)}, u32[]{:S(2)}) collective-permute-start(bf16[1408,512]{1,0:T(8,128)(2,1)} %get-tuple-element.237), channel_id=1, source_target_pairs={{0,8},{4,12},{8,0},{12,4},{1,9},{5,13},{9,1},{13,5},{2,10},{6,14},... | collective-permute-start | bytes 4325384 | tf_op jit(solution)/shard_map/ppermute | solution.py:933
  658.1 103.9 %collective-permute-start.50 = (bf16[2816,1024]{1,0:T(8,128)(2,1)}, bf16[2816,1024]{1,0:T(8,128)(2,1)}, u32[]{:S(2)}, u32[]{:S(2)}) collective-permute-start(bf16[2816,1024]{1,0:T(8,128)(2,1)} %outer.24), channel_id=1, source_target_pairs={{0,4},{4,0},{8,12},{12,8},{1,5},{5,1},{9,13},{13,9},{2,6},{6,2},{1... | collective-permute-start | bytes 17301512 | tf_op jit(solution)/shard_map/ppermute | solution.py:933
  680.1 30.1 %collective-permute-start.47 = (bf16[256,2048]{1,0:T(8,128)(2,1)}, bf16[256,2048]{1,0:T(8,128)(2,1)}, u32[]{:S(2)}, u32[]{:S(2)}) collective-permute-start(bf16[256,2048]{1,0:T(8,128)(2,1)} %get-tuple-element.239.refs_0_.refs_4_), channel_id=1, source_target_pairs={{0,1},{1,0},{2,3},{3,2},{4,5},{5,4},{6,7},{7,6},{8,9},{9,8},{10,11... | collective-permute-start | bytes 3145736 | tf_op jit(solution)/shard_map/ppermute | solution.py:933
  696.2 50.3 %collective-permute-start.48 = (bf16[1408,512]{1,0:T(8,128)(2,1)}, bf16[1408,512]{1,0:T(8,128)(2,1)}, u32[]{:S(2)}, u32[]{:S(2)}) collective-permute-start(bf16[1408,512]{1,0:T(8,128)(2,1)} %get-tuple-element.243), channel_id=1, source_target_pairs={{0,8},{4,12},{8,0},{12,4},{1,9},{5,13},{9,1},{13,5},{2,10},{6,14},... | collective-permute-start | bytes 4325384 | tf_op jit(solution)/shard_map/ppermute | solution.py:933
  698.5 47.9 %collective-permute-start.41 = (bf16[256,2048]{1,0:T(8,128)(2,1)}, bf16[256,2048]{1,0:T(8,128)(2,1)}, u32[]{:S(2)}, u32[]{:S(2)}) collective-permute-start(bf16[256,2048]{1,0:T(8,128)(2,1)} %get-tuple-element.228), channel_id=1, source_target_pairs={{0,2},{1,3},{2,0},{3,1},{4,6},{5,7},{6,4},{7,5},{8,10},{9,11},{10,... | collective-permute-start | bytes 3145736 | tf_op jit(solution)/shard_map/ppermute | solution.py:933
  709.3 37.2 %collective-permute-start.49 = (bf16[704,512]{1,0:T(8,128)(2,1)}, bf16[704,512]{1,0:T(8,128)(2,1)S(1)}, u32[]{:S(2)}, u32[]{:S(2)}) collective-permute-start(bf16[704,512]{1,0:T(8,128)(2,1)} %get-tuple-element.244), channel_id=1, source_target_pairs={{0,16},{16,0},{1,17},{17,1},{2,18},{18,2},{3,19},{19,3},{4,20},{20... | collective-permute-start | bytes 2162696 | tf_op jit(solution)/shard_map/ppermute | solution.py:933
  754.9 43.7 %collective-permute-start.52 = (bf16[1536,1024]{1,0:T(8,128)(2,1)}, bf16[1536,1024]{1,0:T(8,128)(2,1)}, u32[]{:S(2)}, u32[]{:S(2)}) collective-permute-start(bf16[1536,1024]{1,0:T(8,128)(2,1)} %outer.27), channel_id=1, source_target_pairs={{0,4},{4,0},{8,12},{12,8},{1,5},{5,1},{9,13},{13,9},{2,6},{6,2},{1... | collective-permute-start | bytes 9437192 | tf_op jit(solution)/shard_map/ppermute | solution.py:933
  757.1 41.6 %collective-permute-start.53 = (bf16[1408,512]{1,0:T(8,128)(2,1)}, bf16[1408,512]{1,0:T(8,128)(2,1)}, u32[]{:S(2)}, u32[]{:S(2)}) collective-permute-start(bf16[1408,512]{1,0:T(8,128)(2,1)} %get-tuple-element.235), channel_id=1, source_target_pairs={{0,8},{4,12},{8,0},{12,4},{1,9},{5,13},{9,1},{13,5},{2,10},{6,14},... | collective-permute-start | bytes 4325384 | tf_op jit(solution)/shard_map/ppermute | solution.py:933
  762.0 46.3 %collective-permute-start.54 = (bf16[704,512]{1,0:T(8,128)(2,1)}, bf16[704,512]{1,0:T(8,128)(2,1)S(1)}, u32[]{:S(2)}, u32[]{:S(2)}) collective-permute-start(bf16[704,512]{1,0:T(8,128)(2,1)} %add_convert_fusion.11), channel_id=1, source_target_pairs={{0,2},{1,3},{2,0},{3,1},{4,6},{5,7},{6,4},{7,5},{8,10},{9,11},{10,... | collective-permute-start | bytes 2162696 | tf_op jit(solution)/shard_map/ppermute | solution.py:933
  816.0 66.0 %collective-permute-start.57 = (bf16[1536,1024]{1,0:T(8,128)(2,1)}, bf16[1536,1024]{1,0:T(8,128)(2,1)}, u32[]{:S(2)}, u32[]{:S(2)}) collective-permute-start(bf16[1536,1024]{1,0:T(8,128)(2,1)} %outer.30), channel_id=1, source_target_pairs={{0,4},{4,0},{8,12},{12,8},{1,5},{5,1},{9,13},{13,9},{2,6},{6,2},{1... | collective-permute-start | bytes 9437192 | tf_op jit(solution)/shard_map/ppermute | solution.py:933
  818.3 38.0 %collective-permute-start.55 = (bf16[1408,512]{1,0:T(8,128)(2,1)}, bf16[1408,512]{1,0:T(8,128)(2,1)}, u32[]{:S(2)}, u32[]{:S(2)}) collective-permute-start(bf16[1408,512]{1,0:T(8,128)(2,1)} %get-tuple-element.247), channel_id=1, source_target_pairs={{0,8},{4,12},{8,0},{12,4},{1,9},{5,13},{9,1},{13,5},{2,10},{6,14},... | collective-permute-start | bytes 4325384 | tf_op jit(solution)/shard_map/ppermute | solution.py:933
  819.0 24.0 %collective-permute-start.64 = (bf16[704,512]{1,0:T(8,128)(2,1)}, bf16[704,512]{1,0:T(8,128)(2,1)}, u32[]{:S(2)}, u32[]{:S(2)}) collective-permute-start(bf16[704,512]{1,0:T(8,128)(2,1)} %get-tuple-element.277), channel_id=1, source_target_pairs={{0,16},{16,0},{1,17},{17,1},{2,18},{18,2},{3,19},{19,3},{4,20},{20... | collective-permute-start | bytes 2162696 | tf_op jit(solution)/shard_map/ppermute | solution.py:933
  821.1 32.6 %collective-permute-start.58 = (bf16[704,512]{1,0:T(8,128)(2,1)S(1)}, bf16[704,512]{1,0:T(8,128)(2,1)}, u32[]{:S(2)}, u32[]{:S(2)}) collective-permute-start(bf16[704,512]{1,0:T(8,128)(2,1)S(1)} %add_convert_fusion.10), channel_id=1, source_target_pairs={{0,16},{16,0},{1,17},{17,1},{2,18},{18,2},{3,19},{19,3},{4,20},{20... | collective-permute-start | bytes 2162696 | tf_op jit(solution)/shard_map/ppermute | solution.py:933
  822.5 46.3 %collective-permute-start.56 = (bf16[704,512]{1,0:T(8,128)(2,1)}, bf16[704,512]{1,0:T(8,128)(2,1)}, u32[]{:S(2)}, u32[]{:S(2)}) collective-permute-start(bf16[704,512]{1,0:T(8,128)(2,1)} %get-tuple-element.265), channel_id=1, source_target_pairs={{0,16},{16,0},{1,17},{17,1},{2,18},{18,2},{3,19},{19,3},{4,20},{20... | collective-permute-start | bytes 2162696 | tf_op jit(solution)/shard_map/ppermute | solution.py:933
  845.2 33.9 %collective-permute-start.65 = (bf16[704,512]{1,0:T(8,128)(2,1)}, bf16[704,512]{1,0:T(8,128)(2,1)}, u32[]{:S(2)}, u32[]{:S(2)}) collective-permute-start(bf16[704,512]{1,0:T(8,128)(2,1)} %add_convert_fusion.9), channel_id=1, source_target_pairs={{0,2},{1,3},{2,0},{3,1},{4,6},{5,7},{6,4},{7,5},{8,10},{9,11},{10,... | collective-permute-start | bytes 2162696 | tf_op jit(solution)/shard_map/ppermute | solution.py:933
  853.7 47.9 %collective-permute-start.62 = (bf16[1408,512]{1,0:T(8,128)(2,1)}, bf16[1408,512]{1,0:T(8,128)(2,1)}, u32[]{:S(2)}, u32[]{:S(2)}) collective-permute-start(bf16[1408,512]{1,0:T(8,128)(2,1)} %get-tuple-element.272), channel_id=1, source_target_pairs={{0,8},{4,12},{8,0},{12,4},{1,9},{5,13},{9,1},{13,5},{2,10},{6,14},... | collective-permute-start | bytes 4325384 | tf_op jit(solution)/shard_map/ppermute | solution.py:933
  856.3 45.3 %collective-permute-start.60 = (bf16[256,2048]{1,0:T(8,128)(2,1)}, bf16[256,2048]{1,0:T(8,128)(2,1)S(1)}, u32[]{:S(2)}, u32[]{:S(2)}) collective-permute-start(bf16[256,2048]{1,0:T(8,128)(2,1)} %get-tuple-element.270), channel_id=1, source_target_pairs={{0,1},{1,0},{2,3},{3,2},{4,5},{5,4},{6,7},{7,6},{8,9},{9,8},{10,11... | collective-permute-start | bytes 3145736 | tf_op jit(solution)/shard_map/ppermute | solution.py:933
  868.7 62.6 %collective-permute-start.63 = (bf16[1536,512]{1,0:T(8,128)(2,1)}, bf16[1536,512]{1,0:T(8,128)(2,1)}, u32[]{:S(2)}, u32[]{:S(2)}) collective-permute-start(bf16[1536,512]{1,0:T(8,128)(2,1)} %outer.31), channel_id=1, source_target_pairs={{0,8},{4,12},{8,0},{12,4},{1,9},{5,13},{9,1},{13,5},{2,10},{6,14},... | collective-permute-start | bytes 4718600 | tf_op jit(solution)/shard_map/ppermute | solution.py:933
  880.7 37.4 %collective-permute-start.79 = (bf16[704,512]{1,0:T(8,128)(2,1)S(1)}, bf16[704,512]{1,0:T(8,128)(2,1)}, u32[]{:S(2)}, u32[]{:S(2)}) collective-permute-start(bf16[704,512]{1,0:T(8,128)(2,1)S(1)} %add_convert_fusion.8), channel_id=1, source_target_pairs={{0,16},{16,0},{1,17},{17,1},{2,18},{18,2},{3,19},{19,3},{4,20},{20... | collective-permute-start | bytes 2162696 | tf_op jit(solution)/shard_map/ppermute | solution.py:933
  912.3 44.0 %collective-permute-start.59 = (bf16[256,2048]{1,0:T(8,128)(2,1)}, bf16[256,2048]{1,0:T(8,128)(2,1)}, u32[]{:S(2)}, u32[]{:S(2)}) collective-permute-start(bf16[256,2048]{1,0:T(8,128)(2,1)} %get-tuple-element.269), channel_id=1, source_target_pairs={{0,1},{1,0},{2,3},{3,2},{4,5},{5,4},{6,7},{7,6},{8,9},{9,8},{10,11... | collective-permute-start | bytes 3145736 | tf_op jit(solution)/shard_map/ppermute | solution.py:933
  915.4 65.7 %collective-permute-start.61 = (bf16[256,2048]{1,0:T(8,128)(2,1)}, bf16[256,2048]{1,0:T(8,128)(2,1)}, u32[]{:S(2)}, u32[]{:S(2)}) collective-permute-start(bf16[256,2048]{1,0:T(8,128)(2,1)} %add_convert_fusion), channel_id=1, source_target_pairs={{0,2},{1,3},{2,0},{3,1},{4,6},{5,7},{6,4},{7,5},{8,10},{9,11},{10,... | collective-permute-start | bytes 3145736 | tf_op jit(solution)/shard_map/ppermute | solution.py:933
  919.4 93.1 %collective-permute-start.68 = (bf16[1536,512]{1,0:T(8,128)(2,1)}, bf16[1536,512]{1,0:T(8,128)(2,1)}, u32[]{:S(2)}, u32[]{:S(2)}) collective-permute-start(bf16[1536,512]{1,0:T(8,128)(2,1)} %outer.32), channel_id=1, source_target_pairs={{0,8},{4,12},{8,0},{12,4},{1,9},{5,13},{9,1},{13,5},{2,10},{6,14},... | collective-permute-start | bytes 4718600 | tf_op jit(solution)/shard_map/ppermute | solution.py:933
  929.6 60.0 %collective-permute-start.80 = (bf16[704,512]{1,0:T(8,128)(2,1)}, bf16[704,512]{1,0:T(8,128)(2,1)}, u32[]{:S(2)}, u32[]{:S(2)}) collective-permute-start(bf16[704,512]{1,0:T(8,128)(2,1)} %get-tuple-element.295), channel_id=1, source_target_pairs={{0,16},{16,0},{1,17},{17,1},{2,18},{18,2},{3,19},{19,3},{4,20},{20... | collective-permute-start | bytes 2162696 | tf_op jit(solution)/shard_map/ppermute | solution.py:933
  931.4 63.9 %collective-permute-start.82 = (bf16[704,512]{1,0:T(8,128)(2,1)}, bf16[704,512]{1,0:T(8,128)(2,1)}, u32[]{:S(2)}, u32[]{:S(2)}) collective-permute-start(bf16[704,512]{1,0:T(8,128)(2,1)} %add_convert_fusion.7), channel_id=1, source_target_pairs={{0,2},{1,3},{2,0},{3,1},{4,6},{5,7},{6,4},{7,5},{8,10},{9,11},{10,... | collective-permute-start | bytes 2162696 | tf_op jit(solution)/shard_map/ppermute | solution.py:933
  962.3 38.5 %collective-permute-start.70 = (bf16[768,512]{1,0:T(8,128)(2,1)}, bf16[768,512]{1,0:T(8,128)(2,1)}, u32[]{:S(2)}, u32[]{:S(2)}) collective-permute-start(bf16[768,512]{1,0:T(8,128)(2,1)} %get-tuple-element.286), channel_id=1, source_target_pairs={{0,16},{16,0},{1,17},{17,1},{2,18},{18,2},{3,19},{19,3},{4,20},{20... | collective-permute-start | bytes 2359304 | tf_op jit(solution)/shard_map/ppermute | solution.py:933
  1003.1 46.1 %collective-permute-start.71 = (bf16[768,512]{1,0:T(8,128)(2,1)}, bf16[768,512]{1,0:T(8,128)(2,1)}, u32[]{:S(2)}, u32[]{:S(2)}) collective-permute-start(bf16[768,512]{1,0:T(8,128)(2,1)} %add_convert_fusion.5), channel_id=1, source_target_pairs={{0,2},{1,3},{2,0},{3,1},{4,6},{5,7},{6,4},{7,5},{8,10},{9,11},{10,... | collective-permute-start | bytes 2359304 | tf_op jit(solution)/shard_map/ppermute | solution.py:933
  1018.6 30.6 %collective-permute-start.69 = (bf16[768,512]{1,0:T(8,128)(2,1)}, bf16[768,512]{1,0:T(8,128)(2,1)}, u32[]{:S(2)}, u32[]{:S(2)}) collective-permute-start(bf16[768,512]{1,0:T(8,128)(2,1)} %get-tuple-element.285), channel_id=1, source_target_pairs={{0,16},{16,0},{1,17},{17,1},{2,18},{18,2},{3,19},{19,3},{4,20},{20... | collective-permute-start | bytes 2359304 | tf_op jit(solution)/shard_map/ppermute | solution.py:933
  (111 other events, 1734.5 us)
Sparse Core Ops, SparseCore 0:
  858.6 196.1 all-reduce.2
